TPU v7x, 32 devices: a whole 2x2x4 slice. The times are simulated.
32 devices in a mesh: row: 16 (over z, y, core), col: 2 (over x).
Axes of the slice: x: 2, y: 2, z: 4, core: 2. Of those that a mesh axis runs over, the one named last changes fastest.
Arguments:
- image_tokens: bfloat16 [8192, 2, 1536], P('row', 'col'), may hold values from -6 to 6
- text_tokens: bfloat16 [1232, 2, 1536], P('row', 'col'), may hold values from -6 to 6
- conditioning: float32 [16, 1536], P('row', 'col'), may hold values from -6 to 6
- ada_weight: float32 [1536, 2, 9216], P('row', 'col'), may hold values from -0.15625 to 0.15625
- qkv_weight: float32 [1536, 2, 4608], P('row', 'col'), may hold values from -0.15625 to 0.15625
- proj_weight: float32 [1536, 2, 1536], P('row', 'col'), may hold values from -0.625 to 0.625
- fc1_weight: float32 [1536, 2, 6144], P('row', None, 'col'), may hold values from -0.15625 to 0.15625
- fc2_weight: float32 [6144, 2, 1536], P('row', 'col'), may hold values from -0.078125 to 0.078125
- image_cotangent: bfloat16 [8192, 2, 1536], P('row', 'col'), may hold values from -6 to 6
- text_cotangent: bfloat16 [1232, 2, 1536], P('row', 'col'), may hold values from -6 to 6
Outputs:
- image_out: bfloat16 [8192, 2, 1536], P('row', 'col')
- text_out: bfloat16 [1232, 2, 1536], P('row', 'col')
- grad_image: float32 [8192, 2, 1536], P('row', 'col')
- grad_text: float32 [1232, 2, 1536], P('row', 'col')
- grad_cond: float32 [16, 1536], P('row', 'col')
- grad_ada: float32 [1536, 2, 9216], P('row', 'col')
- grad_qkv: float32 [1536, 2, 4608], P('row', 'col')
- grad_proj: float32 [1536, 2, 1536], P('row', 'col')
- grad_fc1: float32 [1536, 2, 6144], P('row', None, 'col')
- grad_fc2: float32 [6144, 2, 1536], P('row', 'col')
All inputs are finite; a program needn't handle non-finite values.
Results may differ from a plain program's by a relative error of at most 0.015.
The roundings to bfloat16 on the way count: a program that leaves them out, or rounds other values in their place, can miss the bound.
Values may be sent and summed in bfloat16 or wider, within the bound.
No kernel may reach another device: no remote copies, remote signals or barrier semaphores. Data moves between devices by JAX's collectives and lax.ppermute only.
A program may use at most 448 MiB of HBM per device.

v0:
```python
from functools import partial

import jax
import jax.numpy as jnp
from jax import lax
from jax.sharding import PartitionSpec as P

MODEL_WIDTH = 1536
HEAD_DIM = 64
FEEDFORWARD_UNITS = 6144


EPSILON = 1e-06


def for_sending(array):
    return jax.tree.map(lambda a: a.astype(jnp.bfloat16) if a.dtype == jnp.float32 else a, array)


def tensor_contraction(spec, first, second):
    return jnp.einsum(spec, first, second, preferred_element_type=jnp.float32)


def collect_pair(first, second):
    return (
        lax.all_gather(first, "col", axis=2, tiled=True),
        lax.all_gather(second, "col", axis=2, tiled=True),
    )


def spread_pair(first, second):
    return (
        lax.psum_scatter(first, "col", scatter_dimension=1, tiled=True),
        lax.psum_scatter(second, "col", scatter_dimension=1, tiled=True),
    )


def weight_blocks(ada_weight, qkv_weight, proj_weight, fc1_weight, fc2_weight, local_width):
    return (
        ada_weight.reshape(ada_weight.shape[0], 2, 6, local_width).astype(jnp.bfloat16),
        qkv_weight.reshape(qkv_weight.shape[0], 2, 3, local_width).astype(jnp.bfloat16),
        proj_weight.reshape(proj_weight.shape[0], 2, local_width).astype(jnp.bfloat16),
        fc1_weight.astype(jnp.bfloat16),
        fc2_weight.reshape(fc2_weight.shape[0], 2, local_width).astype(jnp.bfloat16),
    )


def stored_weight(gradient):
    return gradient.reshape(gradient.shape[0], 1, -1)


def stored_rows(values, local_width):
    return values.reshape(-1, 1, 2 * local_width)


def normalize_pair(first, second):
    totals = lax.psum(
        (
            jnp.sum(first, axis=-1, keepdims=True),
            jnp.sum(first * first, axis=-1, keepdims=True),
            jnp.sum(second, axis=-1, keepdims=True),
            jnp.sum(second * second, axis=-1, keepdims=True),
        ),
        "col",
    )
    result = []
    for position, member in enumerate((first, second)):
        average = totals[2 * position] / MODEL_WIDTH
        reciprocal = lax.rsqrt(totals[2 * position + 1] / MODEL_WIDTH - average * average + EPSILON)
        result.append(((member - average) * reciprocal, reciprocal))
    return result


def normalize_back(first, first_normed, second, second_normed):
    totals = lax.psum(
        (
            jnp.sum(first, axis=-1, keepdims=True),
            jnp.sum(first * first_normed, axis=-1, keepdims=True),
            jnp.sum(second, axis=-1, keepdims=True),
            jnp.sum(second * second_normed, axis=-1, keepdims=True),
        ),
        "col",
    )
    return (
        first - totals[0] / MODEL_WIDTH - first_normed * totals[1] / MODEL_WIDTH,
        second - totals[2] / MODEL_WIDTH - second_normed * totals[3] / MODEL_WIDTH,
    )


def attend_forward(attention_heads_number, members):
    queries, key_rows, values = members
    length = queries.shape[0]
    queries = queries.reshape(length, attention_heads_number, HEAD_DIM)
    key_rows = key_rows.reshape(length, attention_heads_number, HEAD_DIM)
    values = values.reshape(length, attention_heads_number, HEAD_DIM)
    scores = tensor_contraction("qhd,khd->hqk", queries, key_rows) * HEAD_DIM ** (-0.5)
    highest = jnp.max(scores, axis=-1, keepdims=True)
    expo = jnp.exp(scores - highest)
    totals = jnp.sum(expo, axis=-1, keepdims=True)
    probabilities = expo / totals
    output = tensor_contraction("hqk,khd->qhd", probabilities.astype(jnp.bfloat16), values)
    return (output.reshape(length, attention_heads_number * HEAD_DIM), highest + jnp.log(totals))


def attend_back(attention_heads_number, members):
    queries, key_rows, values, result_cotangent_map, log_totals = members
    length = queries.shape[0]
    factor = HEAD_DIM ** (-0.5)
    queries = queries.reshape(length, attention_heads_number, HEAD_DIM)
    key_rows = key_rows.reshape(length, attention_heads_number, HEAD_DIM)
    values = values.reshape(length, attention_heads_number, HEAD_DIM)
    result_cotangent_map = result_cotangent_map.reshape(length, attention_heads_number, HEAD_DIM)
    scores = tensor_contraction("qhd,khd->hqk", queries, key_rows) * factor
    probabilities = jnp.exp(scores - log_totals)
    d_values = tensor_contraction(
        "hqk,qhd->khd", probabilities.astype(jnp.bfloat16), result_cotangent_map
    )
    d_probs = tensor_contraction("qhd,khd->hqk", result_cotangent_map, values)
    d_scores = (
        probabilities * (d_probs - jnp.sum(d_probs * probabilities, axis=-1, keepdims=True))
    ).astype(jnp.bfloat16)
    d_queries = tensor_contraction("hqk,khd->qhd", d_scores, key_rows) * factor
    d_keys = tensor_contraction("hqk,qhd->khd", d_scores, queries) * factor
    return (
        jnp.stack([d_queries, d_keys, d_values])
        .reshape(3, length, attention_heads_number * HEAD_DIM)
        .astype(jnp.bfloat16)
    )


def per_device(
    image_tokens,
    text_tokens,
    conditioning,
    ada_weight,
    qkv_weight,
    proj_weight,
    fc1_weight,
    fc2_weight,
    image_cotangent,
    text_cotangent,
):
    seq_count = conditioning.shape[0]
    local_width = image_tokens.shape[2] // 2
    attention_heads_number = local_width // HEAD_DIM
    image_flat = image_tokens.reshape(-1, local_width)
    text_flat = text_tokens.reshape(-1, local_width)
    image_length = image_flat.shape[0] // seq_count
    text_length = text_flat.shape[0] // seq_count
    ada_full, qkv_full, complete_linear_map, fc1_full, whole_down_weight = lax.all_gather(
        for_sending(
            weight_blocks(ada_weight, qkv_weight, proj_weight, fc1_weight, fc2_weight, local_width)
        ),
        "row",
        axis=0,
        tiled=True,
    )
    silu_cond = lax.all_gather(
        jax.nn.silu(conditioning).astype(jnp.bfloat16), "col", axis=1, tiled=True
    )
    modulation = tensor_contraction("sd,dtje->stje", silu_cond, ada_full)

    def mod_row(modality_label, column):
        return modulation[:, modality_label, column][:, None, :]

    inputs = (
        image_flat.reshape(seq_count, image_length, local_width).astype(jnp.float32),
        text_flat.reshape(seq_count, text_length, local_width).astype(jnp.float32),
    )
    cotangents = (
        image_cotangent.reshape(seq_count, image_length, local_width).astype(jnp.float32),
        text_cotangent.reshape(seq_count, text_length, local_width).astype(jnp.float32),
    )
    first_norm = normalize_pair(inputs[0], inputs[1])
    hidden_one = [
        (
            first_norm[modality_label][0] * (1.0 + mod_row(modality_label, 1))
            + mod_row(modality_label, 0)
        ).astype(jnp.bfloat16)
        for modality_label in range(2)
    ]
    hidden_full = collect_pair(hidden_one[0], hidden_one[1])
    projected = [
        tensor_contraction(
            "snd,djf->jsnf", hidden_full[modality_label], qkv_full[:, modality_label]
        ).astype(jnp.bfloat16)
        for modality_label in range(2)
    ]
    joined = jnp.concatenate([projected[1], projected[0]], axis=2)
    attended, log_totals = lax.map(
        partial(attend_forward, attention_heads_number), (joined[0], joined[1], joined[2])
    )
    attended = attended.astype(jnp.bfloat16)
    complete_segments = collect_pair(attended[:, text_length:], attended[:, :text_length])
    branch_one = [
        tensor_contraction(
            "twe,eb->twb", complete_segments[modality_label], complete_linear_map[:, modality_label]
        )
        for modality_label in range(2)
    ]
    middle = [
        inputs[modality_label] + mod_row(modality_label, 2) * branch_one[modality_label]
        for modality_label in range(2)
    ]
    second_norm = normalize_pair(middle[0], middle[1])
    hidden_two = [
        (
            second_norm[modality_label][0] * (1.0 + mod_row(modality_label, 4))
            + mod_row(modality_label, 3)
        ).astype(jnp.bfloat16)
        for modality_label in range(2)
    ]
    hidden_two_full = collect_pair(hidden_two[0], hidden_two[1])
    preact = [
        tensor_contraction(
            "snd,df->snf", hidden_two_full[modality_label], fc1_full[:, modality_label]
        )
        for modality_label in range(2)
    ]
    activated = [
        jax.nn.gelu(preact[modality_label], approximate=True).astype(jnp.bfloat16)
        for modality_label in range(2)
    ]
    whole_activated = collect_pair(activated[0], activated[1])
    latter_path = [
        tensor_contraction(
            "tok,kq->toq", whole_activated[modality_label], whole_down_weight[:, modality_label]
        )
        for modality_label in range(2)
    ]
    results = [
        middle[modality_label] + mod_row(modality_label, 5) * latter_path[modality_label]
        for modality_label in range(2)
    ]
    ada_full, qkv_full, complete_linear_map, fc1_full, whole_down_weight = lax.all_gather(
        for_sending(
            weight_blocks(ada_weight, qkv_weight, proj_weight, fc1_weight, fc2_weight, local_width)
        ),
        "row",
        axis=0,
        tiled=True,
    )
    grad_second_branch = [
        (mod_row(modality_label, 5) * cotangents[modality_label]).astype(jnp.bfloat16)
        for modality_label in range(2)
    ]
    d_gate_two = [
        jnp.sum(cotangents[modality_label] * latter_path[modality_label], axis=1)
        for modality_label in range(2)
    ]
    grad_fc2 = jnp.stack(
        [
            tensor_contraction(
                "pow,pob->wb", whole_activated[modality_label], grad_second_branch[modality_label]
            )
            for modality_label in range(2)
        ],
        axis=1,
    )
    d_activated = (
        lax.psum_scatter(
            tensor_contraction(
                "wrh,oh->wro", grad_second_branch[0], whole_down_weight[:, 0]
            ).reshape(-1, FEEDFORWARD_UNITS),
            "col",
            scatter_dimension=1,
            tiled=True,
        ),
        lax.psum_scatter(
            tensor_contraction(
                "wrh,oh->wro", grad_second_branch[1], whole_down_weight[:, 1]
            ).reshape(-1, FEEDFORWARD_UNITS),
            "col",
            scatter_dimension=1,
            tiled=True,
        ),
    )
    d_preact = []
    for modality_label in range(2):
        unused, pullback = jax.vjp(partial(jax.nn.gelu, approximate=True), preact[modality_label])
        d_preact.append(
            pullback(d_activated[modality_label].reshape(preact[modality_label].shape))[0].astype(
                jnp.bfloat16
            )
        )
    grad_fc1 = jnp.stack(
        [
            tensor_contraction(
                "snd,snf->df", hidden_two_full[modality_label], d_preact[modality_label]
            )
            for modality_label in range(2)
        ],
        axis=1,
    )
    d_hidden_two = spread_pair(
        tensor_contraction("snf,df->snd", d_preact[0], fc1_full[:, 0]).reshape(-1, MODEL_WIDTH),
        tensor_contraction("snf,df->snd", d_preact[1], fc1_full[:, 1]).reshape(-1, MODEL_WIDTH),
    )
    d_hidden_two = [
        d_hidden_two[modality_label]
        .reshape(middle[modality_label].shape)
        .astype(jnp.bfloat16)
        .astype(jnp.float32)
        for modality_label in range(2)
    ]
    d_offset_two = [jnp.sum(d_hidden_two[modality_label], axis=1) for modality_label in range(2)]
    d_scale_two = [
        jnp.sum(d_hidden_two[modality_label] * second_norm[modality_label][0], axis=1)
        for modality_label in range(2)
    ]
    d_normed_two = [
        d_hidden_two[modality_label] * (1.0 + mod_row(modality_label, 4))
        for modality_label in range(2)
    ]
    back_two = normalize_back(
        d_normed_two[0], second_norm[0][0], d_normed_two[1], second_norm[1][0]
    )
    d_middle = [
        cotangents[modality_label] + second_norm[modality_label][1] * back_two[modality_label]
        for modality_label in range(2)
    ]
    grad_first_branch = [
        (mod_row(modality_label, 2) * d_middle[modality_label]).astype(jnp.bfloat16)
        for modality_label in range(2)
    ]
    d_gate_one = [
        jnp.sum(d_middle[modality_label] * branch_one[modality_label], axis=1)
        for modality_label in range(2)
    ]
    grad_proj = jnp.stack(
        [
            tensor_contraction(
                "fqp,fqt->pt", complete_segments[modality_label], grad_first_branch[modality_label]
            )
            for modality_label in range(2)
        ],
        axis=1,
    )
    d_pieces = spread_pair(
        tensor_contraction("twv,yv->twy", grad_first_branch[0], complete_linear_map[:, 0]).reshape(
            -1, MODEL_WIDTH
        ),
        tensor_contraction("twv,yv->twy", grad_first_branch[1], complete_linear_map[:, 1]).reshape(
            -1, MODEL_WIDTH
        ),
    )
    d_attended = jnp.concatenate(
        [
            d_pieces[1].reshape(seq_count, text_length, local_width),
            d_pieces[0].reshape(seq_count, image_length, local_width),
        ],
        axis=1,
    ).astype(jnp.bfloat16)
    d_joined = lax.map(
        partial(attend_back, attention_heads_number),
        (joined[0], joined[1], joined[2], d_attended, log_totals),
    )
    d_projected = [d_joined[:, :, text_length:], d_joined[:, :, :text_length]]
    grad_qkv = jnp.stack(
        [
            tensor_contraction(
                "snd,sjne->dje", hidden_full[modality_label], d_projected[modality_label]
            )
            for modality_label in range(2)
        ],
        axis=1,
    )
    d_hidden_one = spread_pair(
        tensor_contraction("sjne,dje->snd", d_projected[0], qkv_full[:, 0]).reshape(
            -1, MODEL_WIDTH
        ),
        tensor_contraction("sjne,dje->snd", d_projected[1], qkv_full[:, 1]).reshape(
            -1, MODEL_WIDTH
        ),
    )
    d_hidden_one = [
        d_hidden_one[modality_label]
        .reshape(inputs[modality_label].shape)
        .astype(jnp.bfloat16)
        .astype(jnp.float32)
        for modality_label in range(2)
    ]
    d_offset_one = [jnp.sum(d_hidden_one[modality_label], axis=1) for modality_label in range(2)]
    d_scale_one = [
        jnp.sum(d_hidden_one[modality_label] * first_norm[modality_label][0], axis=1)
        for modality_label in range(2)
    ]
    d_normed_one = [
        d_hidden_one[modality_label] * (1.0 + mod_row(modality_label, 1))
        for modality_label in range(2)
    ]
    back_one = normalize_back(d_normed_one[0], first_norm[0][0], d_normed_one[1], first_norm[1][0])
    grad_inputs = [
        d_middle[modality_label] + first_norm[modality_label][1] * back_one[modality_label]
        for modality_label in range(2)
    ]
    d_modulation = jnp.stack(
        [
            jnp.stack(
                [
                    d_offset_one[modality_label],
                    d_scale_one[modality_label],
                    d_gate_one[modality_label],
                    d_offset_two[modality_label],
                    d_scale_two[modality_label],
                    d_gate_two[modality_label],
                ],
                axis=1,
            )
            for modality_label in range(2)
        ],
        axis=1,
    ).astype(jnp.bfloat16)
    grad_ada = tensor_contraction("sd,stje->dtje", silu_cond, d_modulation)
    d_silu = lax.psum_scatter(
        tensor_contraction("stje,dtje->sd", d_modulation, ada_full),
        "col",
        scatter_dimension=1,
        tiled=True,
    )
    unused, pullback = jax.vjp(jax.nn.silu, conditioning)
    grad_cond = pullback(d_silu)[0]
    grad_ada, grad_qkv, grad_proj, grad_fc1, grad_fc2 = (
        lax.psum_scatter(grad_ada, "row", scatter_dimension=0, tiled=True),
        lax.psum_scatter(grad_qkv, "row", scatter_dimension=0, tiled=True),
        lax.psum_scatter(grad_proj, "row", scatter_dimension=0, tiled=True),
        lax.psum_scatter(grad_fc1, "row", scatter_dimension=0, tiled=True),
        lax.psum_scatter(grad_fc2, "row", scatter_dimension=0, tiled=True),
    )
    return (
        stored_rows(results[0], local_width).astype(jnp.bfloat16),
        stored_rows(results[1], local_width).astype(jnp.bfloat16),
        stored_rows(grad_inputs[0], local_width),
        stored_rows(grad_inputs[1], local_width),
        grad_cond,
        stored_weight(grad_ada),
        stored_weight(grad_qkv),
        stored_weight(grad_proj),
        grad_fc1,
        stored_weight(grad_fc2),
    )


def solution(mesh):
    placed = (
        P("row", "col", None),
        P("row", "col", None),
        P("row", "col"),
        P("row", "col", None),
        P("row", "col", None),
        P("row", "col", None),
        P("row", None, "col"),
        P("row", "col", None),
        P("row", "col", None),
        P("row", "col", None),
    )
    return jax.shard_map(
        per_device,
        mesh=mesh,
        in_specs=placed,
        out_specs=(
            P("row", "col", None),
            P("row", "col", None),
            P("row", "col", None),
            P("row", "col", None),
            P("row", "col"),
            P("row", "col", None),
            P("row", "col", None),
            P("row", "col", None),
            P("row", None, "col"),
            P("row", "col", None),
        ),
        check_vma=False,
    )
```

profile of v0, /device:TPU:0, one launch (start us, length us, event | category | flops | bytes accessed | tf_op | source)
XLA Modules:
  0.0 3612.4 jit_solution(5383847595233145751)
XLA Ops:
  53.5 118.6 %all-gather.15.cloned.1.call-done = bf16[1536,2,6,768]{3,1,2,0:T(2,128)(2,1)} async-done(((bf16[96,2,6,768]{3,1,2,0:T(2,128)(2,1)}), bf16[1536,2,6,768]{3,1,2,0:T(2,128)(2,1)}) %all-gather.15.cloned.1.call-update) | async-done | bytes 28311568 | tf_op jit(solution)/shard_map/all_gather | solution.py:150
  209.2 76.4 %all-gather.17.cloned.1.call-done = bf16[1536,2,3,768]{3,0,2,1:T(8,128)(2,1)} async-done(((bf16[96,2,3,768]{3,0,2,1:T(8,128)(2,1)}), bf16[1536,2,3,768]{3,0,2,1:T(8,128)(2,1)}) %all-gather.17.cloned.1.call-update) | async-done | bytes 14155792 | tf_op jit(solution)/shard_map/all_gather | solution.py:150
  289.9 40.9 %all-gather.19.cloned.1.call-done = bf16[1,1024,1536]{2,1,0:T(8,128)(2,1)} async-done(((bf16[1,1024,768]{2,1,0:T(8,128)(2,1)}), bf16[1,1024,1536]{2,1,0:T(8,128)(2,1)}) %all-gather.19.cloned.1.call-update) | async-done | bytes 3145744 | tf_op jit(solution)/shard_map/all_gather | solution.py:26
  356.1 28.8 fusion.133
  384.9 24.4 fusion
  410.0 26.3 fusion.36
  455.7 32.1 all-gather.23.cloned.1.call-done
  588.7 53.6 %all-gather.25.cloned.1.call-done = bf16[1536,2,3072]{2,0,1:T(8,128)(2,1)} async-done(((bf16[96,2,3072]{2,0,1:T(8,128)(2,1)}), bf16[1536,2,3072]{2,0,1:T(8,128)(2,1)}) %all-gather.25.cloned.1.call-update) | async-done | bytes 18874384 | tf_op jit(solution)/shard_map/all_gather | solution.py:150
  642.3 54.3 %reduce-scatter.21.cloned.1.call-done = f32[154,3072]{1,0:T(8,128)} async-done(((f32[154,6144]{1,0:T(8,128)}), f32[154,3072]{1,0:T(8,128)}) %reduce-scatter.21.cloned.1.call-update) | async-done | bytes 1892368 | tf_op jit(solution)/shard_map/reduce_scatter | solution.py:269
  711.8 31.9 all-gather.29.cloned.1.call-done
  743.7 281.6 %reduce-scatter.17.cloned.1.call-done = f32[1024,3072]{1,0:T(8,128)} async-done(((f32[1024,6144]{1,0:T(8,128)}), f32[1024,3072]{1,0:T(8,128)}) %reduce-scatter.17.cloned.1.call-update) | async-done | bytes 12582928 | tf_op jit(solution)/shard_map/reduce_scatter | solution.py:261
  1025.3 25.8 fusion.16
  1079.8 64.9 %reduce-scatter.19.cloned.1.call-done = f32[1024,768]{0,1:T(8,128)} async-done(((f32[1024,1536]{0,1:T(8,128)}), f32[1024,768]{0,1:T(8,128)}) %reduce-scatter.19.cloned.1.call-update) | async-done | bytes 3145744 | tf_op jit(solution)/shard_map/reduce_scatter | solution.py:33
  1194.3 138.4 %all-gather.31.cloned.1.call-done = bf16[1024,6144]{1,0:T(8,128)(2,1)} async-done(((bf16[1024,3072]{1,0:T(8,128)(2,1)}), bf16[1024,6144]{1,0:T(8,128)(2,1)}) %all-gather.31.cloned.1.call-update) | async-done | bytes 12582928 | tf_op jit(solution)/shard_map/all_gather | solution.py:26
  1373.4 73.7 %reduce-scatter.27.cloned.1.call-done = f32[1024,768]{1,0:T(8,128)} async-done(((f32[1024,1536]{1,0:T(8,128)}), f32[1024,768]{1,0:T(8,128)}) %reduce-scatter.27.cloned.1.call-update) | async-done | bytes 3145744 | tf_op jit(solution)/shard_map/reduce_scatter | solution.py:33
  1450.1 26.6 fusion.39
  1476.7 46.7 %multiply_reduce_fusion = (f32[12,1178]{1,0:T(8,128)}, f32[12,1178,1178]{1,2,0:T(8,128)}) fusion(f32[12,1178,1178]{1,2,0:T(8,128)} %get-tuple-element.178, f32[12,1178]{1,0:T(8,128)} %log_add_fusion, bf16[1178,12,64]{0,2,1:T(8,128)(2,1)S(1)} %bitcast.295, bf16[1024,12,64]{0,2,1:T(8,128)(2,1)S(1)} %bitcast.289, bf16[154,12,64]{0,2,1:T(8,128)(2,1)} %bitcast.298), kind=kOutput, calls=%fused_computation.2 | convolution fusion | flops 2185043968 | bytes 136949568 | tf_op jit(solution)/shard_map/while/body/eval_jaxpr/qhd,khd->hqk/dot_general | solution.py:21
  1523.4 58.0 %multiply_convert_fusion = bf16[12,1178,1178]{1,2,0:T(8,128)(2,1)} fusion(f32[12,1178,1178]{1,2,0:T(8,128)} %get-tuple-element.182, f32[12,1178,1178]{1,2,0:T(8,128)} %get-tuple-element.178, f32[12,1178]{1,0:T(8,128)} %get-tuple-element.181, f32[12,1178]{1,0:T(8,128)} %log_add_fusion), kind=kLoop, calls=%fused_computation.1 | loop fusion | flops 66608832 | bytes 166635168 | tf_op jit(solution)/shard_map/while/body/eval_jaxpr/convert_element_type | solution.py:121
  1692.6 44.6 %reduce-scatter.29.cloned.1.call-done = f32[1024,768]{0,1:T(8,128)} async-done(((f32[1024,1536]{0,1:T(8,128)}), f32[1024,768]{0,1:T(8,128)}) %reduce-scatter.29.cloned.1.call-update) | async-done | bytes 3145744 | tf_op jit(solution)/shard_map/reduce_scatter | solution.py:33
  1760.0 29.3 pad_maximum_fusion
  1918.2 327.6 %reduce-scatter.39.cloned.1.call-done = f32[96,2,3072]{2,0,1:T(8,128)} async-done(((f32[1536,2,3072]{2,0,1:T(8,128)}), f32[96,2,3072]{2,0,1:T(8,128)}) %reduce-scatter.39.cloned.1.call-update) | async-done | bytes 2359312 | tf_op jit(solution)/shard_map/reduce_scatter | solution.py:427
  2250.7 268.3 %reduce-scatter.35.cloned.1.call-done = f32[96,2,3,768]{3,0,2,1:T(8,128)} async-done(((f32[1536,2,3,768]{3,0,2,1:T(8,128)}), f32[96,2,3,768]{3,0,2,1:T(8,128)}) %reduce-scatter.35.cloned.1.call-update) | async-done | bytes 1769488 | tf_op jit(solution)/shard_map/reduce_scatter | solution.py:425
  2525.0 365.8 %reduce-scatter.41.cloned.1.call-done = f32[384,2,768]{2,0,1:T(8,128)} async-done(((f32[6144,2,768]{2,0,1:T(8,128)}), f32[384,2,768]{2,0,1:T(8,128)}) %reduce-scatter.41.cloned.1.call-update) | async-done | bytes 2359312 | tf_op jit(solution)/shard_map/reduce_scatter | solution.py:428
  2897.1 701.7 %reduce-scatter.33.cloned.1.call-done = f32[96,2,6,768]{3,2,1,0:T(8,128)} async-done(((f32[1536,2,6,768]{3,2,1,0:T(8,128)}), f32[96,2,6,768]{3,2,1,0:T(8,128)}) %reduce-scatter.33.cloned.1.call-update) | async-done | bytes 3538960 | tf_op jit(solution)/shard_map/reduce_scatter | solution.py:424
  (389 shorter events, 656.4 us)
Async XLA Ops:
  7.2 164.9 %all-gather.15.cloned.1.call-start = ((), (), s32[]{:S(2)}) async-start(), calls=%async_computation.14 | async-start | bytes 30081024 | tf_op jit(solution)/shard_map/all_gather | solution.py:150
  25.8 259.8 %all-gather.17.cloned.1.call-start = ((), (), s32[]{:S(2)}) async-start(), calls=%async_computation.15 | async-start | bytes 15040512 | tf_op jit(solution)/shard_map/all_gather | solution.py:150
  33.8 297.1 %all-gather.19.cloned.1.call-start = ((), (), s32[]{:S(2)}) async-start(), calls=%async_computation.16 | async-start | bytes 4718592 | tf_op jit(solution)/shard_map/all_gather | solution.py:26
  191.3 250.2 %all-gather.27.cloned.1.call-start = ((), (), s32[]{:S(2)}) async-start(), calls=%async_computation.20 | async-start | bytes 20054016 | tf_op jit(solution)/shard_map/all_gather | solution.py:150
  197.7 290.1 %all-gather.23.cloned.1.call-start = ((), (), s32[]{:S(2)}) async-start(), calls=%async_computation.18 | async-start | bytes 5013504 | tf_op jit(solution)/shard_map/all_gather | solution.py:150
  200.1 341.6 %all-gather.21.cloned.1.call-start = ((), (), s32[]{:S(2)}) async-start(), calls=%async_computation.17 | async-start | bytes 4718592 | tf_op jit(solution)/shard_map/all_gather | solution.py:26
  439.4 202.9 %all-gather.25.cloned.1.call-start = ((), (), s32[]{:S(2)}) async-start(), calls=%async_computation.19 | async-start | bytes 20054016 | tf_op jit(solution)/shard_map/all_gather | solution.py:150
  441.2 255.3 %reduce-scatter.21.cloned.1.call-start = ((), (), s32[]{:S(2)}) async-start(), calls=%async_computation.23 | async-start | bytes 5898240 | tf_op jit(solution)/shard_map/reduce_scatter | solution.py:269
  449.6 294.1 %all-gather.29.cloned.1.call-start = ((), (), s32[]{:S(2)}) async-start(), calls=%async_computation.34 | async-start | bytes 4718592 | tf_op jit(solution)/shard_map/all_gather | solution.py:26
  561.4 463.9 %reduce-scatter.17.cloned.1.call-start = ((), (), s32[]{:S(2)}) async-start(), calls=%async_computation.21 | async-start | bytes 37748736 | tf_op jit(solution)/shard_map/reduce_scatter | solution.py:261
  580.3 495.8 %reduce-scatter.23.cloned.1.call-start = ((), (), s32[]{:S(2)}) async-start(), calls=%async_computation.24 | async-start | bytes 1474560 | tf_op jit(solution)/shard_map/reduce_scatter | solution.py:34
  711.7 433.0 %reduce-scatter.19.cloned.1.call-start = ((), (), s32[]{:S(2)}) async-start(), calls=%async_computation.22 | async-start | bytes 9437184 | tf_op jit(solution)/shard_map/reduce_scatter | solution.py:33
  1067.4 111.2 %all-gather.33.cloned.1.call-start = ((), (), s32[]{:S(2)}) async-start(), calls=%async_computation.36 | async-start | bytes 2949120 | tf_op jit(solution)/shard_map/all_gather | solution.py:27
  1068.2 264.5 %all-gather.31.cloned.1.call-start = ((), (), s32[]{:S(2)}) async-start(), calls=%async_computation.35 | async-start | bytes 18874368 | tf_op jit(solution)/shard_map/all_gather | solution.py:26
  1068.8 302.6 %reduce-scatter.25.cloned.1.call-start = ((), (), s32[]{:S(2)}) async-start(), calls=%async_computation.25 | async-start | bytes 1474560 | tf_op jit(solution)/shard_map/reduce_scatter | solution.py:34
  1194.2 252.8 %reduce-scatter.27.cloned.1.call-start = ((), (), s32[]{:S(2)}) async-start(), calls=%async_computation.26 | async-start | bytes 9437184 | tf_op jit(solution)/shard_map/reduce_scatter | solution.py:33
  1369.9 318.8 %reduce-scatter.31.cloned.1.call-start = ((), (), s32[]{:S(2)}) async-start(), calls=%async_computation.28 | async-start | bytes 1474560 | tf_op jit(solution)/shard_map/reduce_scatter | solution.py:34
  1638.2 99.0 %reduce-scatter.29.cloned.1.call-start = ((), (), s32[]{:S(2)}) async-start(), calls=%async_computation.27 | async-start | bytes 9437184 | tf_op jit(solution)/shard_map/reduce_scatter | solution.py:33
  1651.2 234.2 %reduce-scatter.37.cloned.1.call-start = ((), (), s32[]{:S(2)}) async-start(), calls=%async_computation.31 | async-start | bytes 10027008 | tf_op jit(solution)/shard_map/reduce_scatter | solution.py:426
  1663.2 253.2 %reduce-scatter.43.cloned.1.call-start = ((), (), s32[]{:S(2)}) async-start(), calls=%async_computation.37 | async-start | bytes 1179648
  1759.9 485.8 %reduce-scatter.39.cloned.1.call-start = ((), (), s32[]{:S(2)}) async-start(), calls=%async_computation.32 | async-start | bytes 40108032 | tf_op jit(solution)/shard_map/reduce_scatter | solution.py:427
  1789.3 729.7 %reduce-scatter.35.cloned.1.call-start = ((), (), s32[]{:S(2)}) async-start(), calls=%async_computation.30 | async-start | bytes 30081024 | tf_op jit(solution)/shard_map/reduce_scatter | solution.py:425
  1813.7 1077.1 %reduce-scatter.41.cloned.1.call-start = ((), (), s32[]{:S(2)}) async-start(), calls=%async_computation.33 | async-start | bytes 40108032 | tf_op jit(solution)/shard_map/reduce_scatter | solution.py:428
  1856.8 1742.1 %reduce-scatter.33.cloned.1.call-start = ((), (), s32[]{:S(2)}) async-start(), calls=%async_computation.29 | async-start | bytes 80216064 | tf_op jit(solution)/shard_map/reduce_scatter | solution.py:424
  (95 other events, 1722.8 us)
Sparse Core Ops, SparseCore 0:
  25.9 146.0 all-gather.14
  174.9 110.6 all-gather.16
  287.7 43.0 all-gather.18
  332.8 98.8 all-gather.26
  434.4 53.3 all-gather.22
  489.8 51.8 all-gather.20
  543.3 98.9 all-gather.24
  644.5 51.9 reduce-scatter.20
  698.7 44.9 all-gather.28
  745.9 279.2 reduce-scatter.16
  1027.6 19.5 reduce-scatter.22
  1067.6 77.0 reduce-scatter.18
  1146.9 31.6 all-gather.32
  1180.1 152.4 all-gather.30
  1335.4 19.5 reduce-scatter.24
  1370.0 77.0 reduce-scatter.26
  1638.3 19.5 reduce-scatter.30
  1660.1 77.0 reduce-scatter.28
  1741.8 111.3 reduce-scatter.36
  1855.9 17.1 reduce-scatter.42
  1877.9 367.8 reduce-scatter.38
  2250.5 268.4 reduce-scatter.34
  2523.8 366.9 reduce-scatter.40
  2895.5 703.3 reduce-scatter.32
where the time goes:
time: 3620 us; the launch traced here: 3610 us
  waiting for transfers between devices  2710 us (75%)
  matrix products  427 us (12%)
  other arithmetic  242 us (7%)
  local copies, waits for them, and re-layouts  141 us (4%)
  blocking collectives  71.5 us (2%)
    reduce_scatter x1, waiting for transfers between devices, per_device(): lax.psum_scatter(grad_ada, 'row', scatter_dimension=0, tiled=True)  702 us
    dot_general x32, matrix products, tensor_contraction(): return jnp.einsum(spec, first, second, preferred_element_type=jnp.float32)  427 us
    reduce_scatter x1, waiting for transfers between devices, per_device(): lax.psum_scatter(grad_fc2, 'row', scatter_dimension=0, tiled=True)  366 us
    reduce_scatter x1, waiting for transfers between devices, per_device(): lax.psum_scatter(grad_fc1, 'row', scatter_dimension=0, tiled=True)  328 us
    reduce_scatter x1, waiting for transfers between devices, per_device(): lax.psum_scatter(tensor_contraction('wrh,oh->wro', grad_second_branch[0],...  282 us
    all_gather x5, waiting for transfers between devices, per_device(): lax.all_gather(for_sending(weight_blocks(ada_weight, qkv_weight, proj_wei...  281 us
    reduce_scatter x1, waiting for transfers between devices, per_device(): lax.psum_scatter(grad_qkv, 'row', scatter_dimension=0, tiled=True)  268 us
    all_gather x4, waiting for transfers between devices, collect_pair(): lax.all_gather(first, 'col', axis=2, tiled=True)  228 us
  transfers between devices with their start and end apart: 24, of which 18 were waited for; matrix products, arithmetic and copies ran while one was open for 16% of the time, Pallas kernels for 0%

commit v1 on v0

v1 whole, which is shorter than its diff:
```python
from functools import partial

import jax
import jax.numpy as jnp
from jax import lax
from jax.sharding import PartitionSpec as P

MODEL_WIDTH = 1536
HEAD_DIM = 64
FEEDFORWARD_UNITS = 6144
EPSILON = 1e-06

bf16 = jnp.bfloat16
f32 = jnp.float32


def dot(spec, a, b):
    return jnp.einsum(spec, a, b, preferred_element_type=f32)


def attend_forward(q, k, v):
    length, width = q.shape
    heads = width // HEAD_DIM
    q = q.reshape(length, heads, HEAD_DIM)
    k = k.reshape(length, heads, HEAD_DIM)
    v = v.reshape(length, heads, HEAD_DIM)
    scores = dot("qhd,khd->hqk", q, k) * HEAD_DIM ** (-0.5)
    highest = jnp.max(scores, axis=-1, keepdims=True)
    expo = jnp.exp(scores - highest)
    totals = jnp.sum(expo, axis=-1, keepdims=True)
    probs = expo / totals
    out = dot("hqk,khd->qhd", probs.astype(bf16), v)
    return out.reshape(length, width).astype(bf16), highest + jnp.log(totals)


def attend_back(q, k, v, d_out, log_totals):
    length, width = q.shape
    heads = width // HEAD_DIM
    factor = HEAD_DIM ** (-0.5)
    q = q.reshape(length, heads, HEAD_DIM)
    k = k.reshape(length, heads, HEAD_DIM)
    v = v.reshape(length, heads, HEAD_DIM)
    d_out = d_out.reshape(length, heads, HEAD_DIM)
    scores = dot("qhd,khd->hqk", q, k) * factor
    probs = jnp.exp(scores - log_totals)
    d_v = dot("hqk,qhd->khd", probs.astype(bf16), d_out)
    d_probs = dot("qhd,khd->hqk", d_out, v)
    d_scores = (
        probs * (d_probs - jnp.sum(d_probs * probs, axis=-1, keepdims=True))
    ).astype(bf16)
    d_q = dot("hqk,khd->qhd", d_scores, k) * factor
    d_k = dot("hqk,qhd->khd", d_scores, q) * factor
    return [g.reshape(length, width).astype(bf16) for g in (d_q, d_k, d_v)]


def row_factors(rows):
    if rows % 4 == 0:
        z = 4 if rows >= 16 else 2
        return z, rows // 2 // z
    return 1, rows // 2


def per_device(
    R,
    C,
    image_tokens,
    text_tokens,
    conditioning,
    ada_weight,
    qkv_weight,
    proj_weight,
    fc1_weight,
    fc2_weight,
    image_cotangent,
    text_cotangent,
):
    w = image_tokens.shape[2] // 2
    me_r = lax.axis_index("row")
    me_c = lax.axis_index("col")
    Z, Y = row_factors(R)
    ZY = Z * Y
    my_core = me_r % 2
    my_y = (me_r // 2) % Y
    pair = C == 2
    parity = pair and (R // C) % C == 0
    CORE = [(r, r ^ 1) for r in range(R)]
    YSWAP = [(r, r ^ 2) for r in range(R)]
    YGROUPS = [[(z * Y + y) * 2 + c for y in range(Y)] for z in range(Z) for c in range(2)]
    ZGROUPS = [[(z * Y + y) * 2 + c for z in range(Z)] for y in range(Y) for c in range(2)]
    XSWAP = [(0, 1), (1, 0)]

    def swap(a):
        return lax.ppermute(a, "col", XSWAP)

    def natural(own, other, axis=-1):
        first = jnp.where(me_c == 0, own, other)
        second = jnp.where(me_c == 0, other, own)
        return jnp.concatenate([first, second], axis=axis)

    def gather_features(own):
        if pair:
            return natural(own, swap(own))
        return lax.all_gather(own, "col", axis=own.ndim - 1, tiled=True)

    def scatter_features(make):
        if pair:
            arrived = swap(make(1 - me_c).astype(bf16))
            return make(me_c) + arrived.astype(f32)
        whole = jnp.concatenate([make(c) for c in range(C)], axis=-1)
        return lax.psum_scatter(whole, "col", scatter_dimension=1, tiled=True)

    def sum_col(a):
        if pair:
            return a + swap(a)
        return lax.psum(a, "col")

    def unpack(packed):
        rows = packed.reshape(packed.shape[0], 2 * w)
        return jnp.concatenate([rows[:, :w], rows[:, w:]], axis=0)

    def pack(plain):
        half = plain.shape[0] // 2
        return jnp.concatenate([plain[:half], plain[half:]], axis=1).reshape(half, 1, 2 * w)

    def gather_rows(a):
        return lax.all_gather(a, "row", axis=0, tiled=True)

    def reduce_rows(part):
        arrived = lax.ppermute(part(1 - my_core).astype(bf16), "row", CORE)
        own = part(my_core) + arrived.astype(f32)
        blk, n = own.shape[0] // ZY, own.shape[1]
        own = own.reshape(Z, Y, blk, n)
        if Y == 2:
            sent = lax.dynamic_index_in_dim(own, 1 - my_y, 1, keepdims=False).astype(bf16)
            kept = lax.dynamic_index_in_dim(own, my_y, 1, keepdims=False)
            kept = kept + lax.ppermute(sent, "row", YSWAP).astype(f32)
        elif Y > 1:
            kept = lax.psum_scatter(
                own.astype(bf16), "row", scatter_dimension=1, axis_index_groups=YGROUPS
            )
        else:
            kept = own[:, 0]
        if Z > 1:
            kept = lax.psum_scatter(
                kept.astype(bf16), "row", scatter_dimension=0, axis_index_groups=ZGROUPS
            )
        else:
            kept = kept[0]
        return kept.astype(f32)

    def rows_of(a, core):
        t, width = a.shape
        blk = width // R
        parts = a.reshape(t, ZY, 2, blk)
        return lax.dynamic_index_in_dim(parts, core, 2, keepdims=False).reshape(t, ZY * blk)

    qkv_shard = qkv_weight.reshape(qkv_weight.shape[0], 6 * w).astype(bf16)
    proj_shard = proj_weight.reshape(proj_weight.shape[0], 2 * w).astype(bf16)
    fc1_shard = fc1_weight.astype(bf16)
    fc2_shard = fc2_weight.reshape(fc2_weight.shape[0], 2 * w).astype(bf16)
    units = fc1_shard.shape[2]
    blk2 = fc2_shard.shape[0]
    blocks = units // blk2
    ada_shard = ada_weight.reshape(ada_weight.shape[0], 12 * w).astype(bf16)

    if parity:
        TO = [(r * C + c, ((r // C) * C + c) * C + r % C) for r in range(R) for c in range(C)]
        half = blocks // 2
        group = fc1_shard.reshape(fc1_shard.shape[0], 2, half, 2, blk2)

        def fc1_swap(g):
            mine = lax.dynamic_index_in_dim(g, me_c, 3, keepdims=False)
            theirs = swap(lax.dynamic_index_in_dim(g, 1 - me_c, 3, keepdims=False))
            return natural(mine, theirs, axis=2)

        def fc1_unswap(g):
            first, second = g[:, :, :half], g[:, :, half:]
            mine = jnp.where(me_c == 0, first, second)
            theirs = swap(jnp.where(me_c == 0, second, first))
            even = jnp.where(me_c == 0, mine, theirs)
            odd = jnp.where(me_c == 0, theirs, mine)
            return jnp.stack([even, odd], axis=3)

        fc1_shard = fc1_swap(group).reshape(fc1_shard.shape)
    else:
        TO = [
            (r * C + c, (c * (R // C) + r % (R // C)) * C + r // (R // C))
            for r in range(R)
            for c in range(C)
        ]
    FROM = [(b, a) for a, b in TO]
    fc2_shard = lax.ppermute(fc2_shard, ("row", "col"), TO)

    qkv_full = [gather_rows(qkv_shard[:, m * 3 * w : (m + 1) * 3 * w]) for m in range(2)]
    proj_full = gather_rows(proj_shard)
    proj_full = [proj_full[:, m * w : (m + 1) * w] for m in range(2)]
    fc1_full = [gather_rows(fc1_shard[:, m]) for m in range(2)]
    fc2_parts = []
    for m in range(2):
        got = gather_rows(fc2_shard[:, m * w : (m + 1) * w])
        if parity:
            got = got.reshape(R // C, C, blk2, w).transpose(1, 0, 2, 3)
        fc2_parts.append(got.reshape(C, units, w))

    silu_all = lax.all_gather(jax.nn.silu(conditioning).astype(bf16), ("row", "col"), axis=0, tiled=True)
    silu_all = silu_all.reshape(-1, MODEL_WIDTH)
    ada_rows = ada_shard.shape[0]
    silu_rows = lax.dynamic_slice_in_dim(silu_all, me_r * ada_rows, ada_rows, 1)
    mod = lax.psum_scatter(
        dot("sd,de->se", silu_rows, ada_shard), "row", scatter_dimension=0, tiled=True
    ).reshape(2, 6, w)

    packed = (image_tokens, text_tokens)
    inputs = [unpack(p).astype(f32) for p in packed]
    cotangents = [unpack(p).astype(f32) for p in (image_cotangent, text_cotangent)]
    counts = [a.shape[0] for a in inputs]

    if pair:
        inputs_full = [natural(unpack(p), unpack(swap(p))).astype(f32) for p in packed]
    else:
        inputs_full = [gather_features(unpack(p)).astype(f32) for p in packed]
    first_mod = gather_features(mod[:, 0:2].reshape(4, w)).reshape(2, 2, MODEL_WIDTH)

    mean1, rstd1, hidden1 = [], [], []
    for m in range(2):
        x = inputs_full[m]
        mean = jnp.sum(x, axis=-1, keepdims=True) / MODEL_WIDTH
        meansq = jnp.sum(x * x, axis=-1, keepdims=True) / MODEL_WIDTH
        rstd = lax.rsqrt(meansq - mean * mean + EPSILON)
        mean1.append(mean)
        rstd1.append(rstd)
        hidden1.append(
            ((x - mean) * rstd * (1.0 + first_mod[m, 1]) + first_mod[m, 0]).astype(bf16)
        )
    norm1 = [(inputs[m] - mean1[m]) * rstd1[m] for m in range(2)]

    d_branch2 = [(mod[m, 5] * cotangents[m]).astype(bf16) for m in range(2)]
    d_branch2_full = [gather_features(d_branch2[m]) for m in range(2)]

    projected = [dot("td,de->te", hidden1[m], qkv_full[m]).astype(bf16) for m in range(2)]
    joined = jnp.concatenate(projected, axis=0)
    q, k, v = (joined[:, j * w : (j + 1) * w] for j in range(3))
    attended, log_totals = attend_forward(q, k, v)
    attended = [attended[: counts[0]], attended[counts[0] :]]
    attended_full = [gather_features(a) for a in attended]
    branch1 = [dot("te,eb->tb", attended_full[m], proj_full[m]) for m in range(2)]
    middle = [inputs[m] + mod[m, 2] * branch1[m] for m in range(2)]

    def token_sums(firsts, seconds):
        own = jnp.concatenate(
            [
                jnp.stack([jnp.sum(firsts[m], axis=-1), jnp.sum(seconds[m], axis=-1)])
                for m in range(2)
            ],
            axis=1,
        )
        both = sum_col(own) / MODEL_WIDTH
        parts = (both[:, : counts[0]], both[:, counts[0] :])
        return [(p[0][:, None], p[1][:, None]) for p in parts]

    stats = token_sums(middle, [a * a for a in middle])
    rstd2 = [lax.rsqrt(sq - mean * mean + EPSILON) for mean, sq in stats]
    norm2 = [(middle[m] - stats[m][0]) * rstd2[m] for m in range(2)]
    hidden2 = [(norm2[m] * (1.0 + mod[m, 4]) + mod[m, 3]).astype(bf16) for m in range(2)]
    hidden2_full = [gather_features(a) for a in hidden2]
    preact = [dot("td,df->tf", hidden2_full[m], fc1_full[m]) for m in range(2)]
    activated = [jax.nn.gelu(a, approximate=True).astype(bf16) for a in preact]

    def fc2_block(m, c):
        return lax.dynamic_index_in_dim(fc2_parts[m], c, 0, keepdims=False)

    branch2 = [
        scatter_features(lambda c, m=m: dot("tf,fe->te", activated[m], fc2_block(m, c)))
        for m in range(2)
    ]
    results = [middle[m] + mod[m, 5] * branch2[m] for m in range(2)]
    d_gate2 = [jnp.sum(cotangents[m] * branch2[m], axis=0) for m in range(2)]

    d_activated = [
        dot("tce,cfe->tf", d_branch2_full[m].reshape(-1, C, w), fc2_parts[m]) for m in range(2)
    ]
    d_preact = []
    for m in range(2):
        _, pullback = jax.vjp(partial(jax.nn.gelu, approximate=True), preact[m])
        d_preact.append(pullback(d_activated[m])[0].astype(bf16))
    d_hidden2 = [
        scatter_features(
            lambda c, m=m: dot(
                "tf,df->td", d_preact[m], lax.dynamic_slice_in_dim(fc1_full[m], c * w, w, 0)
            )
        )
        .astype(bf16)
        .astype(f32)
        for m in range(2)
    ]

    def fc2_part(m):
        def part(core):
            if parity:
                grad = lax.dynamic_slice_in_dim(d_branch2_full[m], core * w, w, 1)
                return dot("tf,te->fe", activated[m], grad)
            whole = jnp.concatenate(
                [
                    dot("tf,te->fe", activated[m], d_branch2_full[m][:, c * w : (c + 1) * w])
                    for c in range(C)
                ],
                axis=0,
            )
            return lax.dynamic_index_in_dim(
                whole.reshape(ZY, 2, blk2, w), core, 1, keepdims=False
            ).reshape(ZY * blk2, w)

        return part

    grad_fc2 = jnp.concatenate([reduce_rows(fc2_part(m)) for m in range(2)], axis=1)
    grad_fc2 = lax.ppermute(grad_fc2, ("row", "col"), FROM)

    def product_part(a, b):
        return lambda core: dot("tp,tn->pn", rows_of(a, core), b)

    grad_fc1 = jnp.stack(
        [reduce_rows(product_part(hidden2_full[m], d_preact[m])) for m in range(2)], axis=1
    )
    if parity:
        grad_fc1 = fc1_unswap(grad_fc1.reshape(-1, 2, blocks, blk2)).reshape(grad_fc1.shape)

    d_shift2 = [jnp.sum(d_hidden2[m], axis=0) for m in range(2)]
    d_scale2 = [jnp.sum(d_hidden2[m] * norm2[m], axis=0) for m in range(2)]

    def norm_back(d_hidden, norm, rstd, scale):
        d_norm = [d_hidden[m] * (1.0 + scale[m]) for m in range(2)]
        sums = token_sums(d_norm, [d_norm[m] * norm[m] for m in range(2)])
        return [rstd[m] * (d_norm[m] - sums[m][0] - norm[m] * sums[m][1]) for m in range(2)]

    back2 = norm_back(d_hidden2, norm2, rstd2, [mod[m, 4] for m in range(2)])
    d_middle = [cotangents[m] + back2[m] for m in range(2)]
    d_branch1 = [(mod[m, 2] * d_middle[m]).astype(bf16) for m in range(2)]
    d_gate1 = [jnp.sum(d_middle[m] * branch1[m], axis=0) for m in range(2)]

    d_attended = [
        scatter_features(
            lambda c, m=m: dot(
                "tv,yv->ty", d_branch1[m], lax.dynamic_slice_in_dim(proj_full[m], c * w, w, 0)
            )
        ).astype(bf16)
        for m in range(2)
    ]
    grad_proj = jnp.concatenate(
        [reduce_rows(product_part(attended_full[m], d_branch1[m])) for m in range(2)], axis=1
    )
    d_joined = jnp.concatenate(
        attend_back(q, k, v, jnp.concatenate(d_attended, axis=0), log_totals), axis=1
    )
    d_projected = [d_joined[: counts[0]], d_joined[counts[0] :]]
    d_hidden1 = [
        scatter_features(
            lambda c, m=m: dot(
                "te,de->td", d_projected[m], lax.dynamic_slice_in_dim(qkv_full[m], c * w, w, 0)
            )
        )
        .astype(bf16)
        .astype(f32)
        for m in range(2)
    ]
    grad_qkv = jnp.concatenate(
        [reduce_rows(product_part(hidden1[m], d_projected[m])) for m in range(2)], axis=1
    )
    d_shift1 = [jnp.sum(d_hidden1[m], axis=0) for m in range(2)]
    d_scale1 = [jnp.sum(d_hidden1[m] * norm1[m], axis=0) for m in range(2)]
    back1 = norm_back(d_hidden1, norm1, rstd1, [mod[m, 1] for m in range(2)])
    grad_inputs = [d_middle[m] + back1[m] for m in range(2)]

    d_mod = jnp.concatenate(
        [
            part[m].reshape(1, w)
            for m in range(2)
            for part in (d_shift1, d_scale1, d_gate1, d_shift2, d_scale2, d_gate2)
        ],
        axis=1,
    ).astype(bf16)
    d_mod_all = gather_rows(d_mod)
    grad_ada = dot("sd,se->de", silu_rows, d_mod_all)
    d_silu_part = dot("se,de->sd", d_mod_all, ada_shard)
    d_silu = lax.all_to_all(d_silu_part, "row", 0, 0, tiled=True).reshape(1, MODEL_WIDTH)
    d_silu = lax.psum_scatter(d_silu, "col", scatter_dimension=1, tiled=True)
    _, pullback = jax.vjp(jax.nn.silu, conditioning)
    grad_cond = pullback(d_silu)[0]

    def stored(gradient):
        return gradient.reshape(gradient.shape[0], 1, -1)

    return (
        pack(results[0]).astype(bf16),
        pack(results[1]).astype(bf16),
        pack(grad_inputs[0]),
        pack(grad_inputs[1]),
        grad_cond,
        stored(grad_ada),
        stored(grad_qkv),
        stored(grad_proj),
        grad_fc1,
        stored(grad_fc2),
    )


def solution(mesh):
    tokens = P("row", "col", None)
    units = P("row", None, "col")
    cond = P("row", "col")
    return jax.shard_map(
        partial(per_device, mesh.shape["row"], mesh.shape["col"]),
        mesh=mesh,
        in_specs=(tokens, tokens, cond, tokens, tokens, tokens, units, tokens, tokens, tokens),
        out_specs=(tokens, tokens, tokens, tokens, cond, tokens, tokens, tokens, units, tokens),
        check_vma=False,
    )
```

time: 3620 us -> 1500 us (0.41)
  waiting for transfers between devices: 2710 us -> 470 us
  starting transfers between devices: 1.57 us -> 64.7 us
  blocking collectives: 71.5 us -> 134 us
  local copies, waits for them, and re-layouts: 141 us -> 186 us
  other arithmetic: 242 us -> 199 us
    reduce_scatter x13 -> x8, waiting for transfers between devices: 2180 us -> 0.05 us  [reduce_rows(): lax.psum_scatter(kept.astype(bf16), 'row', scatter_dimension=0, axis_inde...]
    all_gather x10 -> x7, waiting for transfers between devices: 530 us -> 173 us  [gather_rows(): return lax.all_gather(a, 'row', axis=0, tiled=True)]
    ppermute x0 -> x40, waiting for transfers between devices: none -> 276 us  [the longest x22 172 us: swap(): return lax.ppermute(a, 'col', XSWAP)]
    all_gather x4 -> x2, blocking collectives: 41.9 us -> 125 us  [the longest x1 70.2 us: per_device(): lax.all_gather(jax.nn.silu(conditioning).astype(bf16), ('row', 'col'), ax...]
    another operation x10 -> x3, other arithmetic: 72.4 us -> 0.53 us  [the longest x2 0.37 us: fc1_unswap(): return jnp.stack([even, odd], axis=3)]
    ppermute x0 -> x40, starting transfers between devices: none -> 63.3 us  [the longest x22 36.9 us: swap(): return lax.ppermute(a, 'col', XSWAP)]
    convert_element_type x11 -> x21, other arithmetic: 84.1 us -> 112 us  [the longest x1 57.7 us: attend_back(): d_scores = (probs * (d_probs - jnp.sum(d_probs * probs, axis=-1, keepdims...]
    dot_general x32 -> x49, matrix products: 427 us -> 423 us  [dot(): return jnp.einsum(spec, a, b, preferred_element_type=f32)]
  transfers between devices with their start and end apart: 24 -> 57, of which waited for: 18 -> 19; matrix products, arithmetic and copies ran while one was open for 16% -> 51% of each run, Pallas kernels for 0% -> 0%
where the time goes in v1:
time: 1500 us; the launch traced here: 1490 us
  waiting for transfers between devices  470 us (31%)
  matrix products  423 us (28%)
  other arithmetic  199 us (13%)
  local copies, waits for them, and re-layouts  186 us (12%)
  blocking collectives  134 us (9%)
  starting transfers between devices  64.7 us (4%)
  between operations  16.4 us (1%)
    dot_general x49, matrix products, dot(): return jnp.einsum(spec, a, b, preferred_element_type=f32)  423 us
    all_gather x7, waiting for transfers between devices, gather_rows(): return lax.all_gather(a, 'row', axis=0, tiled=True)  173 us
    ppermute x22, waiting for transfers between devices, swap(): return lax.ppermute(a, 'col', XSWAP)  172 us
    ppermute x8, waiting for transfers between devices, reduce_rows(): kept = kept + lax.ppermute(sent, 'row', YSWAP).astype(f32)  105 us
    all_gather x1, blocking collectives, per_device(): lax.all_gather(jax.nn.silu(conditioning).astype(bf16), ('row', 'col'), ax...  70.2 us
    unnamed x303, local copies, waits for them, and re-layouts  69.9 us
    convert_element_type x1, other arithmetic, attend_back(): d_scores = (probs * (d_probs - jnp.sum(d_probs * probs, axis=-1, keepdims...  57.7 us
    all_gather x1, blocking collectives, gather_rows(): return lax.all_gather(a, 'row', axis=0, tiled=True)  54.8 us
  transfers between devices with their start and end apart: 57, of which 19 were waited for; matrix products, arithmetic and copies ran while one was open for 51% of the time, Pallas kernels for 0%

profile of v1, /device:TPU:0, one launch (start us, length us, event | category | flops | bytes accessed | tf_op | source)
XLA Modules:
  0.0 1492.9 jit_solution(8044367556751945637)
XLA Ops:
  8.5 70.2 %all-gather.3 = bf16[32,1,768]{2,1,0:T(2,128)(2,1)S(1)} all-gather(bf16[1,1,768]{2,1,0:T(2,128)(2,1)S(1)} %get-tuple-element.94), channel_id=1, replica_groups=mesh['row'=16,'col'=2] {'row','col'}, dimensions={0}, use_global_device_ids=true | all-gather | bytes 50688 | tf_op jit(solution)/shard_map/all_gather | solution.py:205
  154.7 19.0 %all-reduce.3.cloned.1.call-done = f32[16,9216]{1,0:T(8,128)} async-done(((f32[16,9216]{1,0:T(8,128)}), f32[16,9216]{1,0:T(8,128)}) %all-reduce.3.cloned.1.call-update) | async-done | bytes 589840
  247.7 62.5 %all-gather.13.cloned.1.call-done = bf16[1536,2304]{1,0:T(8,128)(2,1)} async-done(((bf16[96,2304]{1,0:T(8,128)(2,1)}), bf16[1536,2304]{1,0:T(8,128)(2,1)}) %all-gather.13.cloned.1.call-update) | async-done | bytes 7077904 | tf_op jit(solution)/shard_map/all_gather | solution.py:126
  337.6 28.3 %fusion.266 = (f32[12,1178]{1,0:T(8,128)S(1)}, f32[12,1178,1178]{1,2,0:T(8,128)}) fusion(bf16[1178,12,64]{0,2,1:T(8,128)(2,1)} %bitcast.381, bf16[1178,12,64]{0,2,1:T(8,128)(2,1)S(1)} %bitcast.379), kind=kOutput, calls=%fused_computation.469 | convolution fusion | flops 2164772864 | bytes 70284192 | tf_op jit(solution)/shard_map/qhd,khd->hqk/dot_general | solution.py:18
  365.9 23.8 %fusion = f32[12,1178]{1,0:T(8,128)S(1)} fusion(f32[12,1178,1178]{1,2,0:T(8,128)} %get-tuple-element.188, f32[12,1178]{1,0:T(8,128)S(1)} %get-tuple-element.187), kind=kLoop, calls=%fused_computation.6 | loop fusion | flops 33290280 | bytes 66721920 | tf_op jit(solution)/shard_map/reduce_sum | solution.py:30
  389.7 26.5 %fusion.100 = bf16[1178,12,64]{0,2,1:T(8,128)(2,1)S(1)} fusion(bf16[1178,12,64]{0,2,1:T(8,128)(2,1)S(1)} %bitcast.401, f32[12,1178,1178]{1,2,0:T(8,128)} %get-tuple-element.188, f32[12,1178]{1,0:T(8,128)S(1)} %fusion, f32[12,1178]{1,0:T(8,128)S(1)} %get-tuple-element.187), kind=kOutput, calls=%fused_computation.172 | convolution fusion | flops 2182343936 | bytes 70340736 | tf_op jit(solution)/shard_map/hqk,khd->qhd/dot_general | solution.py:18
  425.3 34.0 %collective-permute-done.4 = bf16[154,768]{1,0:T(8,128)(2,1)S(1)} collective-permute-done((bf16[154,768]{1,0:T(8,128)(2,1)S(1)}, bf16[154,768]{1,0:T(8,128)(2,1)S(1)}, u32[]{:S(2)}, u32[]{:S(2)}) %collective-permute-start.4) | collective-permute-done | bytes 236576 | tf_op jit(solution)/shard_map/ppermute | solution.py:93
  481.4 36.8 %collective-permute-done.10 = bf16[154,768]{1,0:T(8,128)(2,1)S(1)} collective-permute-done((bf16[154,768]{1,0:T(8,128)(2,1)S(1)}, bf16[154,768]{1,0:T(8,128)(2,1)S(1)}, u32[]{:S(2)}, u32[]{:S(2)}) %collective-permute-start.10) | collective-permute-done | bytes 236576 | tf_op jit(solution)/shard_map/ppermute | solution.py:93
  561.0 19.2 %multiply_convert_fusion.1 = (bf16[1024,3072]{1,0:T(8,128)(2,1)S(1)}, f32[1024,3072]{1,0:T(8,128)}) fusion(bf16[1536,1,3072]{2,0,1:T(8,128)(2,1)} %all-gather.23.cloned.1.call-done, bf16[1024,768]{0,1:T(8,128)(2,1)} %copy-done.40, bf16[1024,768]{0,1:T(8,128)(2,1)} %copy-done.39), kind=kOutput, calls=%fused_computation.25 | convolution fusion | flops 9698279424 | bytes 31457280 | tf_op jit(solution)/shard_map/td,df->tf/dot_general | solution.py:18
  590.5 20.2 %all-gather.19.cloned.1.call-done = bf16[6144,768]{1,0:T(8,128)(2,1)} async-done(((bf16[384,768]{1,0:T(8,128)(2,1)}), bf16[6144,768]{1,0:T(8,128)(2,1)}) %all-gather.19.cloned.1.call-update) | async-done | bytes 9437200 | tf_op jit(solution)/shard_map/all_gather | solution.py:126
  618.7 73.9 %all-gather.17.cloned.1.call-done = bf16[6144,768]{1,0:T(8,128)(2,1)} async-done(((bf16[384,768]{1,0:T(8,128)(2,1)}), bf16[6144,768]{1,0:T(8,128)(2,1)}) %all-gather.17.cloned.1.call-update) | async-done | bytes 9437200 | tf_op jit(solution)/shard_map/all_gather | solution.py:126
  714.2 24.7 %fusion.12 = bf16[1024,3072]{1,0:T(8,128)(2,1)} fusion(f32[1024,3072]{1,0:T(8,128)} %get-tuple-element.192, bf16[1024,2,768]{0,2,1:T(8,128)(2,1)} %bitcast.422, bf16[2,3072,768]{2,1,0:T(8,128)(2,1)} %bitcast.397), kind=kOutput, calls=%fused_computation.19 | convolution fusion | flops 9726590976 | bytes 31457280 | tf_op jit(solution)/shard_map/tce,cfe->tf/dot_general | solution.py:18
  765.0 20.0 %collective-permute-done.13 = bf16[1024,768]{0,1:T(8,128)(2,1)S(1)} collective-permute-done((bf16[1024,768]{0,1:T(8,128)(2,1)S(1)}, bf16[1024,768]{0,1:T(8,128)(2,1)S(1)}, u32[]{:S(2)}, u32[]{:S(2)}) %collective-permute-start.13) | collective-permute-done | bytes 1572896 | tf_op jit(solution)/shard_map/ppermute | solution.py:93
  806.1 17.1 %collective-permute-done.16 = f32[2,1178]{1,0:T(2,128)S(1)} collective-permute-done((f32[2,1178]{1,0:T(2,128)S(1)}, f32[2,1178]{1,0:T(2,128)S(1)}, u32[]{:S(2)}, u32[]{:S(2)}) %collective-permute-start.16) | collective-permute-done | bytes 9456 | tf_op jit(solution)/shard_map/ppermute | solution.py:93
  871.8 17.2 %collective-permute-done.17 = bf16[1024,768]{1,0:T(8,128)(2,1)} collective-permute-done((bf16[1024,768]{1,0:T(8,128)(2,1)}, bf16[1024,768]{1,0:T(8,128)(2,1)}, u32[]{:S(2)}, u32[]{:S(2)}) %collective-permute-start.17) | collective-permute-done | bytes 1572896 | tf_op jit(solution)/shard_map/ppermute | solution.py:93
  906.7 47.5 %multiply_reduce_fusion = (f32[12,1178]{1,0:T(8,128)}, f32[12,1178,1178]{1,2,0:T(8,128)}) fusion(f32[12,1178,1178]{1,2,0:T(8,128)} %get-tuple-element.188, f32[12,1178]{1,0:T(8,128)S(1)} %copy-done.26, bf16[1178,12,64]{0,2,1:T(8,128)(2,1)S(1)} %bitcast.389, bf16[1178,12,64]{0,2,1:T(8,128)(2,1)} %bitcast.400), kind=kOutput, calls=%fused_computation.2 | convolution fusion | flops 2181425152 | bytes 136949568 | tf_op jit(solution)/shard_map/qhd,khd->hqk/dot_general | solution.py:18
  967.2 57.7 %multiply_convert_fusion = bf16[12,1178,1178]{1,2,0:T(8,128)(2,1)} fusion(f32[12,1178,1178]{1,2,0:T(8,128)} %get-tuple-element.198, f32[12,1178,1178]{1,2,0:T(8,128)} %get-tuple-element.188, f32[12,1178]{1,0:T(8,128)S(1)} %copy-done.95, f32[12,1178]{1,0:T(8,128)S(1)} %copy-done.26), kind=kLoop, calls=%fused_computation.1 | loop fusion | flops 66608832 | bytes 166635168 | tf_op jit(solution)/shard_map/convert_element_type | solution.py:50
  1044.6 26.0 %fusion.72 = bf16[12,64,1178]{2,1,0:T(8,128)(2,1)} fusion(bf16[1178,12,64]{0,2,1:T(8,128)(2,1)S(1)} %bitcast.390, f32[12,1178,1178]{1,2,0:T(8,128)} %get-tuple-element.188, f32[12,1178]{1,0:T(8,128)S(1)} %copy-done.26), kind=kOutput, calls=%fused_computation.135 | convolution fusion | flops 2165691648 | bytes 70284192 | tf_op jit(solution)/shard_map/hqk,qhd->khd/dot_general | solution.py:18
  1070.6 24.6 %collective-permute-done.36 = bf16[4,384,768]{2,1,0:T(8,128)(2,1)} collective-permute-done((bf16[4,384,768]{2,1,0:T(8,128)(2,1)}, bf16[4,384,768]{2,1,0:T(8,128)(2,1)}, u32[]{:S(2)}, u32[]{:S(2)}) %collective-permute-start.36) | collective-permute-done | bytes 2359328 | tf_op jit(solution)/shard_map/ppermute | solution.py:136
  1101.7 18.1 %fusion.71 = bf16[12,64,1178]{2,1,0:T(8,128)(2,1)} fusion(bf16[1178,12,64]{0,2,1:T(8,128)(2,1)S(1)} %bitcast.382, bf16[12,1178,1178]{1,2,0:T(8,128)(2,1)} %multiply_convert_fusion), kind=kOutput, calls=%fused_computation.134 | convolution fusion | flops 2133292032 | bytes 36923232 | tf_op jit(solution)/shard_map/hqk,qhd->khd/dot_general | solution.py:18
  1147.3 31.6 %collective-permute-done.33 = bf16[4,96,3072]{2,1,0:T(8,128)(2,1)} collective-permute-done((bf16[4,96,3072]{2,1,0:T(8,128)(2,1)}, bf16[4,96,3072]{2,1,0:T(8,128)(2,1)}, u32[]{:S(2)}, u32[]{:S(2)}) %collective-permute-start.33) | collective-permute-done | bytes 2359328 | tf_op jit(solution)/shard_map/ppermute | solution.py:136
  1282.1 54.8 %all-gather.4 = bf16[16,1,9216]{2,1,0:T(2,128)(2,1)S(1)} all-gather(bf16[1,1,9216]{2,1,0:T(2,128)(2,1)S(1)} %bitcast.455), channel_id=1, replica_groups=mesh['row'=16,'col'=2] {'row'}, dimensions={0}, use_global_device_ids=true | all-gather | bytes 313344 | tf_op jit(solution)/shard_map/all_gather | solution.py:126
  1381.5 24.9 %collective-permute-done.23 = bf16[4,96,2304]{2,1,0:T(8,128)(2,1)} collective-permute-done((bf16[4,96,2304]{2,1,0:T(8,128)(2,1)}, bf16[4,96,2304]{2,1,0:T(8,128)(2,1)}, u32[]{:S(2)}, u32[]{:S(2)}) %collective-permute-start.23) | collective-permute-done | bytes 1769504 | tf_op jit(solution)/shard_map/ppermute | solution.py:136
  1420.1 19.3 %collective-permute-start.39 = (f32[384,1536]{1,0:T(8,128)}, f32[384,1536]{1,0:T(8,128)}, u32[]{:S(2)}, u32[]{:S(2)}) collective-permute-start(f32[384,1536]{1,0:T(8,128)} %maximum_convert_fusion.1), channel_id=1, source_target_pairs={{0,0},{2,1},{1,2},{3,3},{4,4},{6,5},{5,6},{7,7},{8,8},{10,9},{9,10... | collective-permute-start | bytes 7077896 | tf_op jit(solution)/shard_map/ppermute | solution.py:316
  (626 shorter events, 678.6 us)
Async XLA Ops:
  7.2 166.5 %all-reduce.3.cloned.1.call-start = ((), (), s32[]{:S(2)}) async-start(), calls=%async_computation.26 | async-start | bytes 1179648
  86.2 156.0 %all-gather.15.cloned.1.call-start = ((), (), s32[]{:S(2)}) async-start(), calls=%async_computation.11 | async-start | bytes 7520256 | tf_op jit(solution)/shard_map/all_gather | solution.py:126
  90.1 220.1 %all-gather.13.cloned.1.call-start = ((), (), s32[]{:S(2)}) async-start(), calls=%async_computation.10 | async-start | bytes 7520256 | tf_op jit(solution)/shard_map/all_gather | solution.py:126
  90.8 328.0 %all-gather.21.cloned.1.call-start = ((), (), s32[]{:S(2)}) async-start(), calls=%async_computation.22 | async-start | bytes 5013504 | tf_op jit(solution)/shard_map/all_gather | solution.py:126
  92.7 457.2 %all-gather.25.cloned.1.call-start = ((), (), s32[]{:S(2)}) async-start(), calls=%async_computation.24 | async-start | bytes 10027008 | tf_op jit(solution)/shard_map/all_gather | solution.py:126
  112.8 448.1 %all-gather.23.cloned.1.call-start = ((), (), s32[]{:S(2)}) async-start(), calls=%async_computation.23 | async-start | bytes 10027008 | tf_op jit(solution)/shard_map/all_gather | solution.py:126
  113.4 497.3 %all-gather.19.cloned.1.call-start = ((), (), s32[]{:S(2)}) async-start(), calls=%async_computation.13 | async-start | bytes 10027008 | tf_op jit(solution)/shard_map/all_gather | solution.py:126
  117.5 575.1 %all-gather.17.cloned.1.call-start = ((), (), s32[]{:S(2)}) async-start(), calls=%async_computation.12 | async-start | bytes 10027008 | tf_op jit(solution)/shard_map/all_gather | solution.py:126
  194.7 1176.3 %reduce-scatter.18.cloned.1.call-start = ((), (), s32[]{:S(2)}) async-start(), calls=%async_computation.17 | async-start | bytes 737280 | tf_op jit(solution)/shard_map/reduce_scatter | solution.py:144
  561.0 395.8 %collective-permute-start.37 = (bf16[3072,768]{1,0:T(8,128)(2,1)}, bf16[3072,768]{1,0:T(8,128)(2,1)}, u32[]{:S(2)}, u32[]{:S(2)}) collective-permute-start(bf16[3072,768]{1,0:T(8,128)(2,1)} %convolution_convert_fusion.5), channel_id=1, source_target_pairs={{0,2},{2,0},{4,6},{6,4},{8,10},{10,8},{12,14},{14,12},{16,18},{18,... | collective-permute-start | bytes 14155784 | tf_op jit(solution)/shard_map/ppermute | solution.py:129
  759.8 69.4 %collective-permute-start.9 = (bf16[1024,768]{0,1:T(8,128)(2,1)S(1)}, bf16[1024,768]{0,1:T(8,128)(2,1)S(1)}, u32[]{:S(2)}, u32[]{:S(2)}) collective-permute-start(bf16[1024,768]{0,1:T(8,128)(2,1)S(1)} %fusion.125), channel_id=1, source_target_pairs={{0,1},{1,0},{2,3},{3,2},{4,5},{5,4},{6,7},{7,6},{8,9},{9,8},{10,11... | collective-permute-start | bytes 4718600 | tf_op jit(solution)/shard_map/ppermute | solution.py:93
  861.2 168.9 %collective-permute-start.35 = (bf16[3072,768]{1,0:T(8,128)(2,1)}, bf16[3072,768]{1,0:T(8,128)(2,1)}, u32[]{:S(2)}, u32[]{:S(2)}) collective-permute-start(bf16[3072,768]{1,0:T(8,128)(2,1)} %convolution_convert_fusion.1), channel_id=1, source_target_pairs={{0,2},{2,0},{4,6},{6,4},{8,10},{10,8},{12,14},{14,12},{16,18},{18,... | collective-permute-start | bytes 14155784 | tf_op jit(solution)/shard_map/ppermute | solution.py:129
  863.0 256.8 %collective-permute-start.32 = (bf16[768,3072]{1,0:T(8,128)(2,1)}, bf16[768,3072]{1,0:T(8,128)(2,1)}, u32[]{:S(2)}, u32[]{:S(2)}) collective-permute-start(bf16[768,3072]{1,0:T(8,128)(2,1)} %convolution_convert_fusion.6), channel_id=1, source_target_pairs={{0,2},{2,0},{4,6},{6,4},{8,10},{10,8},{12,14},{14,12},{16,18},{18,... | collective-permute-start | bytes 14155784 | tf_op jit(solution)/shard_map/ppermute | solution.py:129
  867.9 316.3 %collective-permute-start.30 = (bf16[768,3072]{1,0:T(8,128)(2,1)}, bf16[768,3072]{1,0:T(8,128)(2,1)}, u32[]{:S(2)}, u32[]{:S(2)}) collective-permute-start(bf16[768,3072]{1,0:T(8,128)(2,1)} %convolution_convert_fusion.2), channel_id=1, source_target_pairs={{0,2},{2,0},{4,6},{6,4},{8,10},{10,8},{12,14},{14,12},{16,18},{18,... | collective-permute-start | bytes 14155784 | tf_op jit(solution)/shard_map/ppermute | solution.py:129
  906.7 464.3 %reduce-scatter.16.cloned.1.call-start = ((), (), s32[]{:S(2)}) async-start(), calls=%async_computation.16 | async-start | bytes 737280 | tf_op jit(solution)/shard_map/reduce_scatter | solution.py:144
  956.7 460.4 %reduce-scatter.26.cloned.1.call-start = ((), (), s32[]{:S(2)}) async-start(), calls=%async_computation.21 | async-start | bytes 2949120 | tf_op jit(solution)/shard_map/reduce_scatter | solution.py:144
  1030.0 387.1 %reduce-scatter.24.cloned.1.call-start = ((), (), s32[]{:S(2)}) async-start(), calls=%async_computation.20 | async-start | bytes 2949120 | tf_op jit(solution)/shard_map/reduce_scatter | solution.py:144
  1100.2 339.2 %reduce-scatter.22.cloned.1.call-start = ((), (), s32[]{:S(2)}) async-start(), calls=%async_computation.19 | async-start | bytes 2949120 | tf_op jit(solution)/shard_map/reduce_scatter | solution.py:144
  1184.1 256.6 %reduce-scatter.20.cloned.1.call-start = ((), (), s32[]{:S(2)}) async-start(), calls=%async_computation.18 | async-start | bytes 2949120 | tf_op jit(solution)/shard_map/reduce_scatter | solution.py:144
  1205.3 67.9 %collective-permute-start.24 = (bf16[768,2304]{1,0:T(8,128)(2,1)}, bf16[768,2304]{1,0:T(8,128)(2,1)}, u32[]{:S(2)}, u32[]{:S(2)}) collective-permute-start(bf16[768,2304]{1,0:T(8,128)(2,1)} %convolution_convert_fusion.3), channel_id=1, source_target_pairs={{0,2},{2,0},{4,6},{6,4},{8,10},{10,8},{12,14},{14,12},{16,18},{18,... | collective-permute-start | bytes 10616840 | tf_op jit(solution)/shard_map/ppermute | solution.py:129
  1247.3 207.8 %reduce-scatter.28.cloned.1.call-start = ((), (), s32[]{:S(2)}) async-start(), calls=%async_computation.25 | async-start | bytes 1179648
  1256.3 97.4 %collective-permute-start.22 = (bf16[768,2304]{1,0:T(8,128)(2,1)}, bf16[768,2304]{1,0:T(8,128)(2,1)}, u32[]{:S(2)}, u32[]{:S(2)}) collective-permute-start(bf16[768,2304]{1,0:T(8,128)(2,1)} %convolution_convert_fusion.4), channel_id=1, source_target_pairs={{0,2},{2,0},{4,6},{6,4},{8,10},{10,8},{12,14},{14,12},{16,18},{18,... | collective-permute-start | bytes 10616840 | tf_op jit(solution)/shard_map/ppermute | solution.py:129
  1349.3 107.5 %reduce-scatter.14.cloned.1.call-start = ((), (), s32[]{:S(2)}) async-start(), calls=%async_computation.15 | async-start | bytes 2211840 | tf_op jit(solution)/shard_map/reduce_scatter | solution.py:144
  1353.4 103.3 %reduce-scatter.12.cloned.1.call-start = ((), (), s32[]{:S(2)}) async-start(), calls=%async_computation.14 | async-start | bytes 2211840 | tf_op jit(solution)/shard_map/reduce_scatter | solution.py:144
  (171 other events, 3438.0 us)
Sparse Core Ops, SparseCore 0:
  86.3 87.3 all-reduce.2
  176.6 65.6 all-gather.14
  245.1 65.0 all-gather.12
  312.4 51.8 all-gather.20
  366.9 79.9 all-gather.24
  449.1 79.6 all-gather.22
  531.1 79.5 all-gather.18
  613.0 79.5 all-gather.16
  906.8 21.1 reduce-scatter.17
  956.8 21.0 reduce-scatter.15
  1030.1 46.1 reduce-scatter.25
  1100.3 46.1 reduce-scatter.23
  1184.2 46.6 reduce-scatter.21
  1247.4 48.4 reduce-scatter.19
  1349.4 14.4 reduce-scatter.27
  1366.8 38.3 reduce-scatter.13
  1410.6 35.7 reduce-scatter.11

commit v2 on v1

v2 whole, which is shorter than its diff:
```python
from functools import partial

import jax
import jax.numpy as jnp
from jax import lax
from jax.experimental import pallas as pl
from jax.experimental.pallas import tpu as pltpu
from jax.sharding import PartitionSpec as P

MODEL_WIDTH = 1536
HEAD_DIM = 64
FEEDFORWARD_UNITS = 6144
EPSILON = 1e-06
PAIR = 2 * HEAD_DIM
BLOCK = 256
MASKED = -1e30

bf16 = jnp.bfloat16
f32 = jnp.float32


def dot(spec, a, b):
    return jnp.einsum(spec, a, b, preferred_element_type=f32)


def mm_nn(a, b):
    return lax.dot_general(a, b, (((1,), (0,)), ((), ())), preferred_element_type=f32)


def mm_nt(a, b):
    return lax.dot_general(a, b, (((1,), (1,)), ((), ())), preferred_element_type=f32)


def attend_kernel(real, qi, qt, ki, kt, vi, vt, oi, ot, lse, q_s, k_s, v_s, s_0, s_1):
    ni, n = qi.shape[0], q_s.shape[0]
    scale = jnp.asarray(HEAD_DIM**-0.5, bf16)
    q_s[:ni, :] = qi[...] * scale
    q_s[ni:, :] = qt[...] * scale
    k_s[:ni, :] = ki[...]
    k_s[ni:, :] = kt[...]
    v_s[:, :ni] = vi[...].T
    v_s[:, ni:] = vt[...].T
    key = lax.broadcasted_iota(jnp.int32, (n - ni, BLOCK), 0)
    held = (s_0, s_1)

    def scores(i, h):
        head = slice(h * HEAD_DIM, (h + 1) * HEAD_DIM)
        held[h][...] = mm_nt(k_s[:, head], q_s[i * BLOCK : (i + 1) * BLOCK, head])

    def mix(i, h):
        head = slice(h * HEAD_DIM, (h + 1) * HEAD_DIM)
        s = held[h][...]
        s_i, s_t = s[:ni], jnp.where(key < real, s[ni:], MASKED)
        top = jnp.maximum(
            jnp.max(s_i, axis=0, keepdims=True), jnp.max(s_t, axis=0, keepdims=True)
        )
        e_i, e_t = jnp.exp(s_i - top), jnp.exp(s_t - top)
        total = jnp.sum(e_i, axis=0, keepdims=True) + jnp.sum(e_t, axis=0, keepdims=True)
        part = 1.0 / total
        lse[0, h : h + 1, i * BLOCK : (i + 1) * BLOCK] = top + jnp.log(total)
        return mm_nn(v_s[head, :ni], (e_i * part).astype(bf16)) + mm_nn(
            v_s[head, ni:], (e_t * part).astype(bf16)
        )

    blocks = n // BLOCK
    scores(0, 0)
    for i in range(blocks):
        scores(i, 1)
        first = mix(i, 0)
        if i + 1 < blocks:
            scores(i + 1, 0)
        out = jnp.concatenate([first, mix(i, 1)], axis=0).T.astype(bf16)
        if i * BLOCK < ni:
            oi[i * BLOCK : (i + 1) * BLOCK, :] = out
        else:
            ot[i * BLOCK - ni : (i + 1) * BLOCK - ni, :] = out


def attend_back_kernel(
    real, qi, qt, ki, kt, vi, vt, di, dt, lse, dqi, dqt, dki, dkt, dvi, dvt,
    q_s, k_s, kt_s, v_s, d_s, dq_s, dk_s, dv_s,
):
    ni, n = qi.shape[0], q_s.shape[0]
    scale = HEAD_DIM**-0.5
    q_s[:ni, :] = qi[...] * jnp.asarray(scale, bf16)
    q_s[ni:, :] = qt[...] * jnp.asarray(scale, bf16)
    k_s[:ni, :] = ki[...]
    k_s[ni:, :] = kt[...]
    kt_s[:, :ni] = ki[...].T
    kt_s[:, ni:] = kt[...].T
    v_s[:ni, :] = vi[...]
    v_s[ni:, :] = vt[...]
    d_s[:ni, :] = di[...]
    d_s[ni:, :] = dt[...]
    key = lax.broadcasted_iota(jnp.int32, (n - ni, BLOCK), 0)
    for i in range(n // BLOCK):
        rows = slice(i * BLOCK, (i + 1) * BLOCK)
        dq = []
        for h in range(2):
            head = slice(h * HEAD_DIM, (h + 1) * HEAD_DIM)
            q, d = q_s[rows, head], d_s[rows, head]
            s = mm_nt(k_s[:, head], q)
            s = jnp.concatenate([s[:ni], jnp.where(key < real, s[ni:], MASKED)], axis=0)
            p = jnp.exp(s - lse[0, h : h + 1, rows])
            t = p * mm_nt(v_s[:, head], d)
            d_scores = (t - p * jnp.sum(t, axis=0, keepdims=True)).astype(bf16)
            dv, dk = mm_nn(p.astype(bf16), d), mm_nn(d_scores, q)
            if i == 0:
                dv_s[:, head] = dv
                dk_s[:, head] = dk
            else:
                dv_s[:, head] += dv
                dk_s[:, head] += dk
            dq.append(mm_nn(kt_s[head, :], d_scores))
        dq_s[:, rows] = jnp.concatenate(dq, axis=0)
    d_q = (dq_s[...] * scale).T.astype(bf16)
    dqi[...] = d_q[:ni]
    dqt[...] = d_q[ni:]
    dki[...] = dk_s[:ni, :].astype(bf16)
    dkt[...] = dk_s[ni:, :].astype(bf16)
    dvi[...] = dv_s[:ni, :].astype(bf16)
    dvt[...] = dv_s[ni:, :].astype(bf16)


def projection_specs(ni, nt, total, first):
    specs = []
    for j in range(3):
        at = lambda p, j=j: (0, j * total + first + p)
        specs += [pl.BlockSpec((ni, PAIR), at), pl.BlockSpec((nt, PAIR), at)]
    return specs


def attend(image, text, real, first, pairs):
    ni, nt = image.shape[0], text.shape[0]
    n, total = ni + nt, image.shape[1] // 3 // PAIR
    at = lambda p: (0, p)
    return pl.pallas_call(
        partial(attend_kernel, real),
        grid=(pairs,),
        in_specs=projection_specs(ni, nt, total, first),
        out_specs=[
            pl.BlockSpec((ni, PAIR), at),
            pl.BlockSpec((nt, PAIR), at),
            pl.BlockSpec((1, 2, n), lambda p: (p, 0, 0)),
        ],
        out_shape=[
            jax.ShapeDtypeStruct((ni, pairs * PAIR), bf16),
            jax.ShapeDtypeStruct((nt, pairs * PAIR), bf16),
            jax.ShapeDtypeStruct((pairs, 2, n), f32),
        ],
        scratch_shapes=[
            pltpu.VMEM((n, PAIR), bf16),
            pltpu.VMEM((n, PAIR), bf16),
            pltpu.VMEM((PAIR, n), bf16),
            pltpu.VMEM((n, BLOCK), f32),
            pltpu.VMEM((n, BLOCK), f32),
        ],
        compiler_params=pltpu.CompilerParams(vmem_limit_bytes=40 * 2**20),
        cost_estimate=pl.CostEstimate(
            flops=pairs * 2 * n * n * 256 * 2 * 2,
            bytes_accessed=pairs * n * PAIR * 2 * 4,
            transcendentals=pairs * 2 * n * n,
        ),
    )(image, text, image, text, image, text)


def attend_back(image, text, real, first, pairs, d_image, d_text, lse):
    ni, nt = image.shape[0], text.shape[0]
    n, total = ni + nt, image.shape[1] // 3 // PAIR
    at = lambda p: (0, p)
    one_i, one_t = pl.BlockSpec((ni, PAIR), at), pl.BlockSpec((nt, PAIR), at)
    out_i = jax.ShapeDtypeStruct((ni, pairs * PAIR), bf16)
    out_t = jax.ShapeDtypeStruct((nt, pairs * PAIR), bf16)
    return pl.pallas_call(
        partial(attend_back_kernel, real),
        grid=(pairs,),
        in_specs=projection_specs(ni, nt, total, first)
        + [one_i, one_t, pl.BlockSpec((1, 2, n), lambda p: (p, 0, 0))],
        out_specs=[one_i, one_t] * 3,
        out_shape=[out_i, out_t] * 3,
        scratch_shapes=[
            pltpu.VMEM((n, PAIR), bf16),
            pltpu.VMEM((n, PAIR), bf16),
            pltpu.VMEM((PAIR, n), bf16),
            pltpu.VMEM((n, PAIR), bf16),
            pltpu.VMEM((n, PAIR), bf16),
            pltpu.VMEM((PAIR, n), f32),
            pltpu.VMEM((n, PAIR), f32),
            pltpu.VMEM((n, PAIR), f32),
        ],
        compiler_params=pltpu.CompilerParams(vmem_limit_bytes=40 * 2**20),
        cost_estimate=pl.CostEstimate(
            flops=pairs * 2 * n * n * 256 * 2 * 5,
            bytes_accessed=pairs * n * PAIR * 2 * 8,
            transcendentals=pairs * 2 * n * n,
        ),
    )(image, text, image, text, image, text, d_image, d_text, lse)


def split_heads(a):
    return a.reshape(a.shape[0], -1, HEAD_DIM)


def plain_attend(image, text, real):
    joined = jnp.concatenate([image, text[:real]], axis=0)
    q, k, v = (split_heads(a) for a in jnp.split(joined, 3, axis=1))
    scores = dot("qhd,khd->hqk", q, k) * HEAD_DIM ** (-0.5)
    top = jnp.max(scores, axis=-1, keepdims=True)
    expo = jnp.exp(scores - top)
    total = jnp.sum(expo, axis=-1, keepdims=True)
    out = dot("hqk,khd->qhd", (expo / total).astype(bf16), v).astype(bf16)
    out = out.reshape(joined.shape[0], -1)
    pad = ((0, text.shape[0] - real), (0, 0))
    ni = image.shape[0]
    return out[:ni], jnp.pad(out[ni:], pad), top + jnp.log(total)


def plain_attend_back(image, text, real, d_image, d_text, lse):
    ni, width = image.shape[0], d_image.shape[1]
    joined = jnp.concatenate([image, text[:real]], axis=0)
    q, k, v = (split_heads(a) for a in jnp.split(joined, 3, axis=1))
    d = split_heads(jnp.concatenate([d_image, d_text[:real]], axis=0))
    factor = HEAD_DIM ** (-0.5)
    probs = jnp.exp(dot("qhd,khd->hqk", q, k) * factor - lse)
    d_v = dot("hqk,qhd->khd", probs.astype(bf16), d)
    d_probs = dot("qhd,khd->hqk", d, v)
    d_scores = probs * (d_probs - jnp.sum(d_probs * probs, axis=-1, keepdims=True))
    d_scores = d_scores.astype(bf16)
    d_q = dot("hqk,khd->qhd", d_scores, k) * factor
    d_k = dot("hqk,qhd->khd", d_scores, q) * factor
    outs = []
    for g in (d_q, d_k, d_v):
        g = g.reshape(-1, width).astype(bf16)
        outs += [g[:ni], jnp.pad(g[ni:], ((0, text.shape[0] - real), (0, 0)))]
    return outs


def gelu_both(v):
    root = (2.0 / jnp.pi) ** 0.5
    t = jnp.tanh(root * (v + 0.044715 * (v * v * v)))
    half = 0.5 * (1.0 + t)
    slope = half + 0.5 * v * (1.0 - t * t) * (root * (1.0 + 3.0 * 0.044715 * (v * v)))
    return v * half, slope


def row_factors(rows):
    if rows % 4 == 0:
        z = 4 if rows >= 16 else 2
        return z, rows // 2 // z
    return 1, rows // 2


def after(value, *earlier):
    return lax.optimization_barrier((value, *earlier))[0]


def per_device(
    R,
    C,
    image_tokens,
    text_tokens,
    conditioning,
    ada_weight,
    qkv_weight,
    proj_weight,
    fc1_weight,
    fc2_weight,
    image_cotangent,
    text_cotangent,
):
    w = image_tokens.shape[2] // 2
    me_r = lax.axis_index("row")
    me_c = lax.axis_index("col")
    Z, Y = row_factors(R)
    ZY = Z * Y
    my_core = me_r % 2
    my_y = (me_r // 2) % Y
    pair = C == 2
    parity = pair and (R // C) % C == 0
    kernels = w % PAIR == 0
    both = range(2)
    CORE = [(r, r ^ 1) for r in range(R)]
    YSWAP = [(r, r ^ 2) for r in range(R)]
    YGROUPS = [[(z * Y + y) * 2 + c for y in range(Y)] for z in range(Z) for c in range(2)]
    ZGROUPS = [[(z * Y + y) * 2 + c for z in range(Z)] for y in range(Y) for c in range(2)]
    XSWAP = [(0, 1), (1, 0)]

    def swap(a):
        return lax.ppermute(a, "col", XSWAP)

    def natural(own, other, axis=-1):
        first = jnp.where(me_c == 0, own, other)
        second = jnp.where(me_c == 0, other, own)
        return jnp.concatenate([first, second], axis=axis)

    def send(own):
        if pair:
            return swap(own)
        return lax.all_gather(own, "col", axis=own.ndim - 1, tiled=True)

    def whole(own, got):
        return natural(own, got) if pair else got

    def gather_features(own):
        return whole(own, send(own))

    def col_start(makes):
        if pair:
            sent = jnp.concatenate([make(1 - me_c).astype(bf16) for make in makes], axis=0)
            return sent, swap(sent)
        sent = jnp.concatenate(
            [jnp.concatenate([make(c) for c in range(C)], axis=-1) for make in makes], axis=0
        )
        return sent, lax.psum_scatter(sent, "col", scatter_dimension=1, tiled=True)

    def col_end(makes, state, *earlier):
        got = after(state[1], *earlier)
        parts = (got[: counts[0]].astype(f32), got[counts[0] :].astype(f32))
        return [make(me_c) + part if pair else part for make, part in zip(makes, parts)]

    def sum_col(a):
        return lax.psum(a, "col")

    def core_start(part):
        sent = part(1 - my_core).astype(bf16)
        return sent, lax.ppermute(sent, "row", CORE)

    def y_start(parts, gots):
        owns = []
        for part, got in zip(parts, gots):
            own = part(my_core) + got.astype(f32)
            owns.append(own.reshape(Z, Y, own.shape[0] // ZY, own.shape[1]))
        if Y == 2:
            sent = jnp.concatenate(
                [
                    lax.dynamic_index_in_dim(own, 1 - my_y, 1, keepdims=False).astype(bf16)
                    for own in owns
                ],
                axis=2,
            )
            kept = [lax.dynamic_index_in_dim(own, my_y, 1, keepdims=False) for own in owns]
            sent, *kept = lax.optimization_barrier((sent, *kept))
            return sent, kept, lax.ppermute(sent, "row", YSWAP)
        own = jnp.concatenate([own.astype(bf16) for own in owns], axis=3)
        if Y > 1:
            own = lax.psum_scatter(own, "row", scatter_dimension=1, axis_index_groups=YGROUPS)
            return own, own, None
        return own[:, 0], own[:, 0], None

    def z_start(states, previous, *earlier):
        pieces = []
        for _, kept, got in states:
            if got is None:
                pieces.append(kept.astype(bf16))
                continue
            got, at = after(got, *earlier), 0
            for k in kept:
                pieces.append((k + got[:, :, at : at + k.shape[2]].astype(f32)).astype(bf16))
                at += k.shape[2]
        kept = jnp.concatenate(pieces, axis=2)
        if Z == 1:
            return [kept, kept[0]]
        if previous is not None:
            kept, previous[1] = lax.optimization_barrier((kept, previous[1]))
        summed = lax.psum_scatter(kept, "row", scatter_dimension=0, axis_index_groups=ZGROUPS)
        return [kept, summed]

    def rows_of(a):
        t, width = a.shape
        parts = a.reshape(t, ZY, 2, width // R)
        return [
            lax.dynamic_index_in_dim(parts, core, 2, keepdims=False).reshape(t, width // 2)
            for core in (1 - my_core, my_core)
        ]

    def product_part(rows, b):
        return lambda core: dot("tp,tn->pn", rows[0] if core is not my_core else rows[1], b)

    def unpack(packed):
        rows = packed.reshape(packed.shape[0], 2 * w)
        return jnp.concatenate([rows[:, :w], rows[:, w:]], axis=0)

    def pack(plain):
        half = plain.shape[0] // 2
        return jnp.concatenate([plain[:half], plain[half:]], axis=1).reshape(half, 1, 2 * w)

    def gather_rows(a, order=None):
        return lax.all_gather(a, "row", axis=1, tiled=True, axis_index_groups=order)

    fan = MODEL_WIDTH // R
    qkv_shard = qkv_weight.reshape(fan, 6 * w)
    proj_shard = proj_weight.reshape(fan, 2 * w)
    first_shard = jnp.stack(
        [
            jnp.concatenate(
                [
                    qkv_shard[:, m * 3 * w : (m + 1) * 3 * w].astype(bf16),
                    proj_shard[:, m * w : (m + 1) * w].astype(bf16),
                ],
                axis=1,
            )
            for m in both
        ]
    )
    first_full = gather_rows(first_shard)
    qkv_full = [first_full[m, :, : 3 * w] for m in both]
    proj_full = [first_full[m, :, 3 * w :] for m in both]

    silu_own = jax.nn.silu(conditioning).astype(bf16).reshape(R // C, 1, fan)
    silu_sent = jnp.broadcast_to(silu_own[None], (C, R // C, C, fan)).reshape(R * C, fan)
    silu_got = lax.all_to_all(silu_sent, ("row", "col"), 0, 0, tiled=True).reshape(R, C, fan)
    silu_rows = lax.dynamic_index_in_dim(silu_got, me_r // (R // C), 1, keepdims=False)
    ada_shard = ada_weight.reshape(fan, 12 * w).astype(bf16)
    mod = lax.all_to_all(dot("sd,de->se", silu_rows, ada_shard), "row", 0, 0, tiled=True)
    mod = jnp.sum(mod, axis=0).reshape(2, 6, w)

    packed = (image_tokens, text_tokens)
    packed_got = [send(after(p, silu_got)) if pair else None for p in packed]
    first_mod = gather_features(mod[:, 0:2].reshape(4, w)).reshape(2, 2, MODEL_WIDTH)
    inputs = [unpack(p).astype(f32) for p in packed]
    cotangents = [unpack(p).astype(f32) for p in (image_cotangent, text_cotangent)]
    counts = [a.shape[0] for a in inputs]
    real = counts[1]
    padding = -(counts[0] + real) % BLOCK
    d_branch2 = [(mod[m, 5] * cotangents[m]).astype(bf16) for m in both]

    early = [p for p in packed_got if p is not None] + [first_mod]
    fc1_weight, fc2_weight = lax.optimization_barrier((fc1_weight, fc2_weight, *early))[:2]
    fc1_shard = jnp.stack([fc1_weight[:, m] for m in both]).astype(bf16)
    blk2 = fc2_weight.shape[0]
    fc2_shard = fc2_weight.reshape(blk2, 2 * w)
    fc2_shard = jnp.stack([fc2_shard[:, m * w : (m + 1) * w] for m in both]).astype(bf16)
    units = fc1_shard.shape[2]
    blocks = units // blk2

    if parity:
        half = blocks // 2
        MOVES = [(r * C + c, ((r // C) * C + c) * C + r % C) for r in range(R) for c in range(C)]
        MOVES = [(a, b) for a, b in MOVES if a != b]
        stays = me_r % C == me_c
        ORDER = [[k * C + c for c in range(C) for k in range(R // C)]]

        def move_units(a):
            return jnp.where(stays, a, lax.ppermute(a, ("row", "col"), MOVES))

        unmove_units = move_units
        group = fc1_shard.reshape(2, fan, half, 2, blk2)
        mine = lax.dynamic_index_in_dim(group, me_c, 3, keepdims=False)
        theirs = swap(lax.dynamic_index_in_dim(group, 1 - me_c, 3, keepdims=False))
        fc1_shard = natural(mine, theirs, axis=2).reshape(fc1_shard.shape)

        def unmove_columns(g):
            g = g.reshape(fan, 2, blocks, blk2)
            first, second = g[:, :, :half], g[:, :, half:]
            mine = jnp.where(me_c == 0, first, second)
            theirs = swap(jnp.where(me_c == 0, second, first))
            even = jnp.where(me_c == 0, mine, theirs)
            odd = jnp.where(me_c == 0, theirs, mine)
            return jnp.stack([even, odd], axis=3).reshape(fan, 2, units)

    else:
        MOVES = [
            (r * C + c, (c * (R // C) + r % (R // C)) * C + r // (R // C))
            for r in range(R)
            for c in range(C)
        ]
        ORDER = None

        def move_units(a):
            return lax.ppermute(a, ("row", "col"), MOVES)

        def unmove_units(a):
            return lax.ppermute(a, ("row", "col"), [(b, a) for a, b in MOVES])

        def unmove_columns(g):
            return g

    fc2_shard = move_units(fc2_shard)
    d_branch2_got = [send(after(d_branch2[m], fc1_shard, fc2_shard)) for m in both]
    fc1_full = gather_rows(fc1_shard)
    fc2_full = gather_rows(fc2_shard, ORDER).reshape(2, C, units, w)

    def padded(a):
        return jnp.pad(a, ((0, padding), (0, 0)))

    if pair:
        inputs_full = [natural(unpack(packed[m]), unpack(packed_got[m])) for m in both]
    else:
        inputs_full = [gather_features(unpack(p)) for p in packed]

    mean1, rstd1, hidden1 = [], [], []
    for m in both:
        x = inputs_full[m].astype(f32)
        mean = jnp.sum(x, axis=-1, keepdims=True) / MODEL_WIDTH
        meansq = jnp.sum(x * x, axis=-1, keepdims=True) / MODEL_WIDTH
        rstd = lax.rsqrt(meansq - mean * mean + EPSILON)
        mean1.append(mean)
        rstd1.append(rstd)
        hidden1.append(
            ((x - mean) * rstd * (1.0 + first_mod[m, 1]) + first_mod[m, 0]).astype(bf16)
        )
    hidden1[1] = padded(hidden1[1])
    norm1 = [(inputs[m] - mean1[m]) * rstd1[m] for m in both]
    projected = [dot("td,de->te", hidden1[m], qkv_full[m]).astype(bf16) for m in both]

    total = w // PAIR
    groups = (3 if total % 3 == 0 else 1) if kernels else 1
    pairs = total // groups
    wide = w // groups
    attended, attended_got, lse = [], [], []
    for g in range(groups):
        text = projected[1]
        if g > 1:
            text = after(text, attended_got[g - 2])
        if kernels:
            out_i, out_t, saved = attend(projected[0], text, real, g * pairs, pairs)
        else:
            out_i, out_t, saved = plain_attend(projected[0], text, real)
        attended.append(jnp.concatenate([out_i, out_t[:real]], axis=0))
        attended_got.append(send(attended[g]))
        lse.append(saved)
    attended_full = whole(
        jnp.concatenate(attended, axis=1), jnp.concatenate(attended_got, axis=1)
    )
    attended_full = [attended_full[: counts[0]], attended_full[counts[0] :]]
    attended_rows = [rows_of(a) for a in attended_full]
    hidden1_rows = [rows_of(a) for a in hidden1]
    d_branch2_full = [
        whole(d_branch2[m], after(d_branch2_got[m], attended[-1])) for m in both
    ]

    branch1 = [dot("te,eb->tb", attended_full[m], proj_full[m]) for m in both]
    middle = [inputs[m] + mod[m, 2] * branch1[m] for m in both]

    def token_sums(firsts, seconds):
        own = jnp.concatenate(
            [
                jnp.stack([jnp.sum(firsts[m], axis=-1), jnp.sum(seconds[m], axis=-1)])
                for m in both
            ],
            axis=1,
        )
        sums = sum_col(own) / MODEL_WIDTH
        parts = (sums[:, : counts[0]], sums[:, counts[0] :])
        return [(p[0][:, None], p[1][:, None]) for p in parts]

    stats = token_sums(middle, [a * a for a in middle])
    rstd2 = [lax.rsqrt(sq - mean * mean + EPSILON) for mean, sq in stats]
    norm2 = [(middle[m] - stats[m][0]) * rstd2[m] for m in both]
    hidden2 = [(norm2[m] * (1.0 + mod[m, 4]) + mod[m, 3]).astype(bf16) for m in both]
    hidden2_got = [send(a) for a in hidden2]
    hidden2_got[0], *rows = lax.optimization_barrier(
        (hidden2_got[0], *attended_rows[0], *attended_rows[1], *hidden1_rows[0], *hidden1_rows[1])
    )
    attended_rows, hidden1_rows = [rows[:2], rows[2:4]], [rows[4:6], rows[6:]]
    hidden2_full = [whole(a, got) for a, got in zip(hidden2, hidden2_got)]
    hidden2_rows = [rows_of(a) for a in hidden2_full]
    preact = [dot("td,df->tf", hidden2_full[m], fc1_full[m]) for m in both]
    pairs_of = [gelu_both(a) for a in preact]
    activated = [a.astype(bf16) for a, _ in pairs_of]
    slope = [s for _, s in pairs_of]

    def fc2_part(m, act):
        def part(core):
            if parity:
                grad = lax.dynamic_slice_in_dim(d_branch2_full[m], core * w, w, 1)
                return dot("tf,te->fe", act, grad)
            whole_grad = jnp.concatenate(
                [
                    dot("tf,te->fe", act, d_branch2_full[m][:, c * w : (c + 1) * w])
                    for c in range(C)
                ],
                axis=0,
            )
            return lax.dynamic_index_in_dim(
                whole_grad.reshape(ZY, 2, blk2, w), core, 1, keepdims=False
            ).reshape(ZY * blk2, w)

        return part

    fc2_core = [core_start(fc2_part(m, activated[m])) for m in both]
    act_later = [after(activated[m], fc2_core[0][0], fc2_core[1][0]) for m in both]
    fc2_y = y_start([fc2_part(m, act_later[m]) for m in both], [s[1] for s in fc2_core])

    grads = [after(d_branch2_full[m], fc2_y[0]) for m in both]
    none = jnp.minimum(me_r, 0)
    d_activated = [
        dot(
            "tce,cfe->tf",
            grads[m].reshape(-1, C, w),
            lax.dynamic_slice(fc2_full, (m + none, 0, 0, 0), (1, C, units, w))[0],
        )
        for m in both
    ]
    d_preact = [(d_activated[m] * slope[m]).astype(bf16) for m in both]

    def hidden2_make(m, d):
        return lambda c: dot(
            "tf,df->td", d, lax.dynamic_slice(fc1_full, (m, c * w, 0), (1, w, units))[0]
        )

    hidden2_col = col_start([hidden2_make(m, d_preact[m]) for m in both])

    def branch2_make(m, act):
        return lambda c: dot(
            "tf,fe->te", act, lax.dynamic_slice(fc2_full, (m, c, 0, 0), (1, 1, units, w))[0, 0]
        )

    act_last = [after(activated[m], hidden2_col[0]) for m in both]
    branch2_col = col_start([branch2_make(m, act_last[m]) for m in both])
    d_next = [after(d_preact[m], hidden2_col[0]) for m in both]
    fc1_core = [core_start(product_part(hidden2_rows[m], d_next[m])) for m in both]
    d_next = [after(d_next[m], fc1_core[0][0], fc1_core[1][0]) for m in both]
    fc1_y = y_start(
        [product_part(hidden2_rows[m], d_next[m]) for m in both], [s[1] for s in fc1_core]
    )
    d_next = [after(d_next[m], fc1_y[0]) for m in both]
    d_hidden2 = col_end(
        [hidden2_make(m, d_next[m]) for m in both], hidden2_col, fc1_y[0], branch2_col[0]
    )
    d_hidden2 = [d.astype(bf16) for d in d_hidden2]
    fc2_z = z_start([fc2_y], None, *d_hidden2)
    d_hidden2 = [d.astype(f32) for d in d_hidden2]

    def norm_back(d_hidden, norm, rstd, scale):
        d_norm = [d_hidden[m] * (1.0 + scale[m]) for m in both]
        sums = token_sums(d_norm, [d_norm[m] * norm[m] for m in both])
        return [rstd[m] * (d_norm[m] - sums[m][0] - norm[m] * sums[m][1]) for m in both]

    back2 = norm_back(d_hidden2, norm2, rstd2, [mod[m, 4] for m in both])
    d_middle = [cotangents[m] + back2[m] for m in both]
    d_branch1 = [(mod[m, 2] * d_middle[m]).astype(bf16) for m in both]

    def attended_make(m, g, d):
        return lambda c: dot(
            "tv,yv->ty",
            d,
            lax.dynamic_slice(first_full, (m, c * w + g * wide, 3 * w), (1, wide, w))[0],
        )

    attended_col = [
        col_start([attended_make(m, g, d_branch1[m]) for m in both]) for g in range(groups)
    ]
    sent = [state[0] for state in attended_col]
    d_last = [after(d_branch1[m], *sent) for m in both]
    proj_core = [core_start(product_part(attended_rows[m], d_last[m])) for m in both]

    act_last = [after(act_last[m], *sent) for m in both]
    branch2 = col_end([branch2_make(m, act_last[m]) for m in both], branch2_col, *sent)
    results = [middle[m] + mod[m, 5] * branch2[m] for m in both]
    d_gate2 = [jnp.sum(cotangents[m] * branch2[m], axis=0) for m in both]
    proj_y = y_start(
        [product_part(attended_rows[m], d_last[m]) for m in both], [s[1] for s in proj_core]
    )

    d_projected, qkv_core, qkv_y = [], [], []
    later = [proj_y[0], fc2_z[0], *d_gate2]

    def qkv_part(g, m):
        joined = jnp.concatenate(d_projected[g][m], axis=1)
        return product_part(hidden1_rows[m], joined)

    for g in range(groups):
        makes = [attended_make(m, g, d_branch1[m]) for m in both]
        d_attended = [d.astype(bf16) for d in col_end(makes, attended_col[g], *later)]
        d_attended[1] = padded(d_attended[1])
        if kernels:
            outs = attend_back(
                projected[0], projected[1], real, g * pairs, pairs, *d_attended, lse[g]
            )
        else:
            outs = plain_attend_back(projected[0], projected[1], real, *d_attended, lse[g])
        d_projected.append([[outs[2 * j + m] for j in range(3)] for m in both])
        if g + 1 < groups:
            qkv_core.append([core_start(qkv_part(g, m)) for m in both])
            later = [qkv_core[g][m][0] for m in both]
            if g > 0:
                gots = [after(s[1], *later) for s in qkv_core[g - 1]]
                qkv_y.append(y_start([qkv_part(g - 1, m) for m in both], gots))
                later.append(qkv_y[g - 1][0])
            if g + 2 == groups:
                fc1_z = z_start([fc1_y], fc2_z, *later)
                later.append(fc1_z[0])

    d_all = [
        jnp.concatenate(
            [d_projected[g][m][j] for j in range(3) for g in range(groups)], axis=1
        )[: counts[m]]
        for m in both
    ]

    def hidden1_make(m, d):
        return lambda c: dot(
            "te,de->td", d, lax.dynamic_slice(first_full, (m, c * w, 0), (1, w, 3 * w))[0]
        )

    hidden1_col = col_start([hidden1_make(m, d_all[m]) for m in both])
    if groups == 1:
        fc1_z = z_start([fc1_y], fc2_z)
    g = groups - 1
    d_projected[g] = [
        [after(d_projected[g][m][0], hidden1_col[0]), *d_projected[g][m][1:]] for m in both
    ]
    qkv_core.append([core_start(qkv_part(g, m)) for m in both])
    for g in range(len(qkv_y), groups):
        qkv_y.append(y_start([qkv_part(g, m) for m in both], [s[1] for s in qkv_core[g]]))
    first_z = z_start([proj_y, *qkv_y[: groups // 2]], fc1_z, hidden1_col[0])

    d_gate1 = [jnp.sum(d_middle[m] * branch1[m], axis=0) for m in both]
    d_shift2 = [jnp.sum(d_hidden2[m], axis=0) for m in both]
    d_scale2 = [jnp.sum(d_hidden2[m] * norm2[m], axis=0) for m in both]

    d_hidden1 = col_end([hidden1_make(m, d_all[m]) for m in both], hidden1_col)
    d_hidden1 = [d.astype(bf16) for d in d_hidden1]
    last_z = z_start(qkv_y[groups // 2 :], first_z, *d_hidden1)
    d_hidden1 = [d.astype(f32) for d in d_hidden1]
    d_shift1 = [jnp.sum(d_hidden1[m], axis=0) for m in both]
    d_scale1 = [jnp.sum(d_hidden1[m] * norm1[m], axis=0) for m in both]
    back1 = norm_back(d_hidden1, norm1, rstd1, [mod[m, 1] for m in both])
    grad_inputs = [d_middle[m] + back1[m] for m in both]

    d_mod = jnp.concatenate(
        [
            part[m].reshape(1, w)
            for m in both
            for part in (d_shift1, d_scale1, d_gate1, d_shift2, d_scale2, d_gate2)
        ],
        axis=1,
    ).astype(bf16)
    d_mod_all = lax.all_to_all(jnp.broadcast_to(d_mod, (R, 12 * w)), "row", 0, 0, tiled=True)
    grad_ada = dot("sd,se->de", silu_rows, d_mod_all)
    d_silu = dot("se,de->sd", d_mod_all, ada_shard)
    d_silu = jnp.broadcast_to(d_silu[:, None], (R, C, fan)).reshape(R * C, fan)
    d_silu = lax.all_to_all(d_silu, ("row", "col"), 0, 0, tiled=True).reshape(C, R // C, C, fan)
    d_silu = lax.dynamic_index_in_dim(d_silu, me_c, 0, keepdims=False)
    d_silu = jnp.sum(d_silu, axis=1).reshape(1, w)
    _, pullback = jax.vjp(jax.nn.silu, conditioning)
    grad_cond = pullback(d_silu)[0]

    grad_fc2 = unmove_units(fc2_z[1].astype(f32))
    grad_fc1 = unmove_columns(fc1_z[1].astype(f32)).reshape(fan, 2, units)
    grad_proj = first_z[1][:, : 2 * w].astype(f32)
    grad_qkv = jnp.concatenate([first_z[1][:, 2 * w :], last_z[1]], axis=1).astype(f32)
    grad_qkv = jnp.concatenate(
        [
            grad_qkv[:, ((2 * g + m) * 3 + j) * wide : ((2 * g + m) * 3 + j + 1) * wide]
            for m in both
            for j in range(3)
            for g in range(groups)
        ],
        axis=1,
    )

    def stored(gradient):
        return gradient.reshape(gradient.shape[0], 1, -1)

    return (
        pack(results[0]).astype(bf16),
        pack(results[1]).astype(bf16),
        pack(grad_inputs[0]),
        pack(grad_inputs[1]),
        grad_cond,
        stored(grad_ada),
        stored(grad_qkv),
        stored(grad_proj),
        grad_fc1,
        stored(grad_fc2),
    )


def solution(mesh):
    tokens = P("row", "col", None)
    units = P("row", None, "col")
    cond = P("row", "col")
    return jax.shard_map(
        partial(per_device, mesh.shape["row"], mesh.shape["col"]),
        mesh=mesh,
        in_specs=(tokens, tokens, cond, tokens, tokens, tokens, units, tokens, tokens, tokens),
        out_specs=(tokens, tokens, tokens, tokens, cond, tokens, tokens, tokens, units, tokens),
        check_vma=False,
    )
```

time: 1500 us -> 891 us (0.59)
  waiting for transfers between devices: 470 us -> 97.9 us
  matrix products: 423 us -> 267 us
  Pallas kernels: 0 us -> 96.6 us
  other arithmetic: 199 us -> 128 us
  blocking collectives: 134 us -> 66.4 us
  local copies, waits for them, and re-layouts: 186 us -> 142 us
    all_gather x7 -> x3, waiting for transfers between devices: 173 us -> 0.02 us  [gather_rows(): return lax.all_gather(a, 'row', axis=1, tiled=True, axis_index_groups=order)]
    dot_general x49 -> x59, matrix products: 423 us -> 267 us  [dot(): return jnp.einsum(spec, a, b, preferred_element_type=f32)]
    all_gather x2 -> x0, blocking collectives: 125 us -> none  [the longest x1 70.2 us: per_device(): lax.all_gather(jax.nn.silu(conditioning).astype(bf16), ('row', 'col'), ax...]
    ppermute x22 -> x18, waiting for transfers between devices: 172 us -> 67 us  [swap(): return lax.ppermute(a, 'col', XSWAP)]
    ppermute x18 -> x20, waiting for transfers between devices: 105 us -> 0.05 us  [the longest x12 0.03 us: core_start(): return (sent, lax.ppermute(sent, 'row', CORE))]
    pallas_call x0 -> x6, Pallas kernels: none -> 96.6 us  [the longest x3 61.4 us: attend_back(): pl.pallas_call(partial(attend_back_kernel, real), grid=(pairs,), in_specs...]
    convert_element_type x17 -> x14, other arithmetic: 107 us -> 27 us  [the longest x6 17.1 us: z_start(): pieces.append((k + got[:, :, at:at + k.shape[2]].astype(f32)).astype(bf16))]
    psum x0 -> x3, blocking collectives: none -> 36.1 us  [sum_col(): return lax.psum(a, 'col')]
  transfers between devices with their start and end apart: 57 -> 48, of which waited for: 19 -> 10; matrix products, arithmetic and copies ran while one was open for 51% -> 52% of each run, Pallas kernels for 0% -> 11%
where the time goes in v2:
time: 891 us; the launch traced here: 883 us
  matrix products  267 us (30%)
  local copies, waits for them, and re-layouts  142 us (16%)
  other arithmetic  128 us (14%)
  waiting for transfers between devices  97.9 us (11%)
  Pallas kernels  96.6 us (11%)
  starting transfers between devices  69 us (8%)
  blocking collectives  66.4 us (7%)
  between operations  17.5 us (2%)
    dot_general x59, matrix products, dot(): return jnp.einsum(spec, a, b, preferred_element_type=f32)  267 us
    ppermute x18, waiting for transfers between devices, swap(): return lax.ppermute(a, 'col', XSWAP)  67 us
    pallas_call x3, Pallas kernels, attend_back(): pl.pallas_call(partial(attend_back_kernel, real), grid=(pairs,), in_specs...  61.4 us
    unnamed x400, local copies, waits for them, and re-layouts  47 us
    psum x3, blocking collectives, sum_col(): return lax.psum(a, 'col')  36.1 us
    pallas_call x3, Pallas kernels, attend(): pl.pallas_call(partial(attend_kernel, real), grid=(pairs,), in_specs=proj...  35.2 us
    ppermute x18, starting transfers between devices, swap(): return lax.ppermute(a, 'col', XSWAP)  34.5 us
    all_to_all x1, blocking collectives, per_device(): lax.all_to_all(dot('sd,de->se', silu_rows, ada_shard), 'row', 0, 0, tiled...  30.3 us
  transfers between devices with their start and end apart: 48, of which 10 were waited for; matrix products, arithmetic and copies ran while one was open for 52% of the time, Pallas kernels for 11%

profile of v2, /device:TPU:0, one launch (start us, length us, event | category | flops | bytes accessed | tf_op | source)
XLA Modules:
  0.0 883.4 jit_solution(275994496737769097)
XLA Ops:
  34.5 30.3 %all_to_all.36 = f32[16,1,9216]{2,1,0:T(1,128)S(1)} all-to-all(f32[16,1,9216]{2,1,0:T(1,128)S(1)} %copy.180), channel_id=1, replica_groups=mesh['row'=16,'col'=2] {'row'}, dimensions={0} | all-to-all | bytes 1179648 | tf_op jit(solution)/shard_map/all_to_all | solution.py:414
  87.1 13.1 %collective-permute-done.7 = bf16[2,96,4,384]{3,1,2,0:T(8,128)(2,1)S(1)} collective-permute-done((bf16[2,96,4,384]{3,1,2,0:T(8,128)(2,1)S(1)}, bf16[2,96,4,384]{3,1,2,0:T(8,128)(2,1)S(1)}, u32[]{:S(2)}, u32[]{:S(2)}) %collective-permute-start.7) | collective-permute-done | bytes 589856 | tf_op jit(solution)/shard_map/ppermute | solution.py:289
  131.4 17.3 %collective-permute-start.9 = (bf16[1024,768]{0,1:T(8,128)(2,1)S(1)}, bf16[1024,768]{0,1:T(8,128)(2,1)}, u32[]{:S(2)}, u32[]{:S(2)}) collective-permute-start(bf16[1024,768]{0,1:T(8,128)(2,1)S(1)} %fusion.90), channel_id=1, source_target_pairs={{0,1},{1,0},{2,3},{3,2},{4,5},{5,4},{6,7},{7,6},{8,9},{9,8},{10,11... | collective-permute-start | bytes 4718600 | tf_op jit(solution)/shard_map/ppermute | solution.py:289
  154.3 11.9 %fusion.25.qi.ki.vi = bf16[1024,2304]{1,0:T(8,128)(2,1)S(1)} fusion(bf16[2,1536,3072]{2,1,0:T(8,128)(2,1)} %all-gather.4.cloned.1.call-done, f32[1536]{0:T(1024)S(1)} %get-tuple-element.298, f32[1536]{0:T(1024)S(1)} %get-tuple-element.299, f32[1024]{0:T(1024)S(1)} %get-tuple-element.407, f32[1024]{0:T(1024)S(1)} %get-tuple-element.406, ...), kind=kOutput, calls=%fused_computation.43 | convolution fusion | flops 7264272384 | bytes 14962688 | tf_op jit(solution)/shard_map/td,de->te/dot_general | solution.py:23
  166.2 11.7 %shard_map.177 = (bf16[1024,256]{1,0:T(8,128)(2,1)S(1)}, bf16[256,256]{1,0:T(8,128)(2,1)S(1)}, f32[2,2,1280]{2,1,0:T(2,128)S(1)}) custom-call(bf16[1024,2304]{1,0:T(8,128)(2,1)S(1)} %fusion.25.qi.ki.vi, bf16[256,2304]{1,0:T(8,128)(2,1)S(1)} %fusion.56.qt.kt.vt, bf16[1024,2304]{1,0:T(8,128)(2,1)S(1)} %fusion.25.qi.ki.vi, ...), custom_call_target="tpu_custom_call" | custom-call | flops 6710886400 | bytes 2621440 | tf_op jit(solution)/shard_map/pallas_call | solution.py:137
  180.0 11.9 %shard_map.178 = (bf16[1024,256]{1,0:T(8,128)(2,1)S(1)}, bf16[256,256]{1,0:T(8,128)(2,1)S(1)}, f32[2,2,1280]{2,1,0:T(2,128)S(1)}) custom-call(bf16[1024,2304]{1,0:T(8,128)(2,1)S(1)} %fusion.25.qi.ki.vi, bf16[256,2304]{1,0:T(8,128)(2,1)S(1)} %fusion.56.qt.kt.vt, bf16[1024,2304]{1,0:T(8,128)(2,1)S(1)} %fusion.25.qi.ki.vi, ...), custom_call_target="tpu_custom_call" | custom-call | flops 6710886400 | bytes 2621440 | tf_op jit(solution)/shard_map/pallas_call | solution.py:137
  192.0 10.2 %collective-permute-done.3 = bf16[1178,256]{1,0:T(8,128)(2,1)S(1)} collective-permute-done((bf16[1178,256]{1,0:T(8,128)(2,1)S(1)}, bf16[1178,256]{1,0:T(8,128)(2,1)S(1)}, u32[]{:S(2)}, u32[]{:S(2)}) %collective-permute-start.3) | collective-permute-done | bytes 603168 | tf_op jit(solution)/shard_map/ppermute | solution.py:289
  202.2 11.7 %shard_map.179 = (bf16[1024,256]{1,0:T(8,128)(2,1)S(1)}, bf16[256,256]{1,0:T(8,128)(2,1)S(1)}, f32[2,2,1280]{2,1,0:T(2,128)S(1)}) custom-call(bf16[1024,2304]{1,0:T(8,128)(2,1)S(1)} %fusion.25.qi.ki.vi, bf16[256,2304]{1,0:T(8,128)(2,1)S(1)} %fusion.56.qt.kt.vt, bf16[1024,2304]{1,0:T(8,128)(2,1)S(1)} %fusion.25.qi.ki.vi, ...), custom_call_target="tpu_custom_call" | custom-call | flops 6710886400 | bytes 2621440 | tf_op jit(solution)/shard_map/pallas_call | solution.py:137
  221.2 8.1 collective-permute-done.5
  281.2 23.5 %collective-permute-done.10 = bf16[154,768]{1,0:T(8,128)(2,1)} collective-permute-done((bf16[154,768]{1,0:T(8,128)(2,1)}, bf16[154,768]{1,0:T(8,128)(2,1)}, u32[]{:S(2)}, u32[]{:S(2)}) %collective-permute-start.10) | collective-permute-done | bytes 236576 | tf_op jit(solution)/shard_map/ppermute | solution.py:289
  320.5 19.6 %multiply_convert_fusion = (bf16[1024,3072]{1,0:T(8,128)(2,1)S(1)}, f32[1024,3072]{1,0:T(8,128)}) fusion(bf16[2,1536,3072]{2,1,0:T(8,128)(2,1)} %all-gather.6.cloned.1.call-done, bf16[1024,768]{0,1:T(8,128)(2,1)S(1)} %get-tuple-element.327, bf16[1024,768]{0,1:T(8,128)(2,1)S(1)} %get-tuple-element.326), kind=kOutput, calls=%fused_computation.12 | convolution fusion | flops 9698279424 | bytes 31457280 | tf_op jit(solution)/shard_map/td,df->tf/dot_general | solution.py:23
  364.1 7.9 convert_add_fusion.3
  377.4 24.1 %fusion.9 = bf16[1024,3072]{1,0:T(8,128)(2,1)} fusion(f32[1024,3072]{1,0:T(8,128)} %get-tuple-element.415, bf16[1024,2,768]{0,2,1:T(8,128)(2,1)} %bitcast.508, bf16[2,2,3072,768]{3,2,1,0:T(8,128)(2,1)} %bitcast.498, s32[]{:T(128)S(6)} %select_n.310), kind=kOutput, calls=%fused_computation.11 | convolution fusion | flops 9720299520 | bytes 31457284 | tf_op jit(solution)/shard_map/tce,cfe->tf/dot_general | solution.py:23
  445.9 8.7 fusion.122
  492.2 10.9 %fusion.87 = (bf16[768]{0:T(1024)(128)(2,1)}, f32[1024]{0:T(1024)S(1)}, f32[1024]{0:T(1024)S(1)}, bf16[1024,768]{0,1:T(8,128)(2,1)}) fusion(f32[1024,768]{0,1:T(8,128)S(1)} %copy-done.7, f32[1024]{0:T(1024)S(1)} %copy-done.105, f32[1024]{0:T(1024)S(1)} %bitcast.539, f32[768]{0:T(1024)S(1)} %copy-done.103, bf16[1178,768]{0,1:T(8,128)(2,1)S(1)} %copy-done.61, ...), kind=kOutput, calls=%fused_computation.135 | convolution fusion | flops 4841272320 | bytes 17322500 | tf_op jit(solution)/shard_map/tf,df->td/dot_general | solution.py:23
  503.1 20.5 %psum.22 = f32[2,1178]{1,0:T(2,128)S(1)} all-reduce(f32[2,1178]{1,0:T(2,128)S(1)} %maximum_maximum_fusion.2), channel_id=1, replica_groups=mesh['row'=16,'col'=2] {'col'}, use_global_device_ids=true, to_apply=%region_14.15 | all-reduce | flops 2356 | bytes 18848 | tf_op jit(solution)/shard_map/psum | solution.py:322
  570.8 10.4 %fusion.91 = (bf16[768]{0:T(1024)(128)(2,1)S(1)}, bf16[1024,768]{0,1:T(8,128)(2,1)S(1)}) fusion(bf16[1178,768]{0,1:T(8,128)(2,1)} %copy.199, bf16[512,768]{0,1:T(8,128)(2,1)} %copy-done.26, bf16[512,768]{0,1:T(8,128)(2,1)} %copy-done.24, f32[1024,768]{0,1:T(8,128)S(1)} %copy-done.7, f32[768]{0:T(1024)S(1)} %copy-done.126, ...), kind=kOutput, calls=%fused_computation.139 | convolution fusion | flops 4840487936 | bytes 18878980 | tf_op jit(solution)/shard_map/tf,fe->te/dot_general | solution.py:23
  599.3 20.2 %shard_map.180 = (bf16[1024,256]{1,0:T(8,128)(2,1)S(1)}, bf16[256,256]{1,0:T(8,128)(2,1)S(1)}, bf16[1024,256]{1,0:T(8,128)(2,1)S(1)}, bf16[256,256]{1,0:T(8,128)...) custom-call(bf16[1024,2304]{1,0:T(8,128)(2,1)S(1)} %bitcast.458, bf16[256,2304]{1,0:T(8,128)(2,1)S(1)} %copy-done.2, ...), custom_call_target="tpu_custom_call" | custom-call | flops 16777216000 | bytes 5242880 | tf_op jit(solution)/shard_map/pallas_call | solution.py:174
  627.6 20.7 %shard_map.181 = (bf16[1024,256]{1,0:T(8,128)(2,1)S(1)}, bf16[256,256]{1,0:T(8,128)(2,1)S(1)}, bf16[1024,256]{1,0:T(8,128)(2,1)S(1)}, bf16[256,256]{1,0:T(8,128)...) custom-call(bf16[1024,2304]{1,0:T(8,128)(2,1)S(1)} %bitcast.458, bf16[256,2304]{1,0:T(8,128)(2,1)S(1)} %copy-done.2, ...), custom_call_target="tpu_custom_call" | custom-call | flops 16777216000 | bytes 5242880 | tf_op jit(solution)/shard_map/pallas_call | solution.py:174
  691.7 20.5 %shard_map.182 = (bf16[1024,256]{1,0:T(8,128)(2,1)S(1)}, bf16[256,256]{1,0:T(8,128)(2,1)S(1)}, bf16[1024,256]{1,0:T(8,128)(2,1)S(1)}, bf16[256,256]{1,0:T(8,128)...) custom-call(bf16[1024,2304]{1,0:T(8,128)(2,1)S(1)} %bitcast.460, bf16[256,2304]{1,0:T(8,128)(2,1)S(1)} %copy-done.3, ...), custom_call_target="tpu_custom_call" | custom-call | flops 16777216000 | bytes 5242880 | tf_op jit(solution)/shard_map/pallas_call | solution.py:174
  739.6 21.4 %reduce-scatter.7.cloned.1.call-done = bf16[1,96,6144]{2,1,0:T(8,128)(2,1)} async-done(((bf16[4,96,6144]{2,1,0:T(8,128)(2,1)}), bf16[1,96,6144]{2,1,0:T(8,128)(2,1)}) %reduce-scatter.7.cloned.1.call-update) | async-done | bytes 1179664 | tf_op jit(solution)/shard_map/reduce_scatter | solution.py:365
  761.1 9.1 %fusion.72 = f32[1024,768]{0,1:T(8,128)} fusion(bf16[1024,2304]{1,0:T(8,128)(2,1)} %copy-done.112, bf16[2,1536,3072]{2,1,0:T(8,128)(2,1)} %all-gather.4.cloned.1.call-done, s32[]{:T(128)S(6)} %select_n.313), kind=kOutput, calls=%fused_computation.120 | convolution fusion | flops 3623878656 | bytes 11403268 | tf_op jit(solution)/shard_map/te,de->td/dot_general | solution.py:23
  804.9 8.3 psum.23
  839.7 7.8 all-to-all-start.3
  (762 shorter events, 506.2 us)
Async XLA Ops:
  7.2 141.6 %all-gather.4.cloned.1.call-start = ((), (), s32[]{:S(2)}) async-start(), calls=%async_computation.8 | async-start | bytes 20054016 | tf_op jit(solution)/shard_map/all_gather | solution.py:388
  21.4 285.3 %all-gather.6.cloned.1.call-start = ((), (), s32[]{:S(2)}) async-start(), calls=%async_computation.9 | async-start | bytes 20054016 | tf_op jit(solution)/shard_map/all_gather | solution.py:388
  31.7 41.8 %collective-permute-start = (bf16[512,1,1536]{0,2,1:T(8,128)(2,1)}, bf16[512,1,1536]{0,2,1:T(8,128)(2,1)}, u32[]{:S(2)}, u32[]{:S(2)}) collective-permute-start(bf16[512,1,1536]{0,2,1:T(8,128)(2,1)} %copy.181), channel_id=1, source_target_pairs={{0,1},{1,0},{2,3},{3,2},{4,5},{5,4},{6,7},{7,6},{8,9},{9,8},{10,11... | collective-permute-start | bytes 4718600 | tf_op jit(solution)/shard_map/ppermute | solution.py:289
  101.8 275.6 %all-gather.8.cloned.1.call-start = ((), (), s32[]{:S(2)}) async-start(), calls=%async_computation.10 | async-start | bytes 20054016 | tf_op jit(solution)/shard_map/all_gather | solution.py:388
  108.5 566.2 %reduce-scatter.5.cloned.1.call-start = ((), (), s32[]{:S(2)}) async-start(), calls=%async_computation.11 | async-start | bytes 5898240 | tf_op jit(solution)/shard_map/reduce_scatter | solution.py:365
  131.4 84.8 %collective-permute-start.9 = (bf16[1024,768]{0,1:T(8,128)(2,1)S(1)}, bf16[1024,768]{0,1:T(8,128)(2,1)}, u32[]{:S(2)}, u32[]{:S(2)}) collective-permute-start(bf16[1024,768]{0,1:T(8,128)(2,1)S(1)} %fusion.90), channel_id=1, source_target_pairs={{0,1},{1,0},{2,3},{3,2},{4,5},{5,4},{6,7},{7,6},{8,9},{9,8},{10,11... | collective-permute-start | bytes 4718600 | tf_op jit(solution)/shard_map/ppermute | solution.py:289
  148.7 67.4 %collective-permute-start.11 = (bf16[154,768]{1,0:T(8,128)(2,1)S(1)}, bf16[154,768]{1,0:T(8,128)(2,1)}, u32[]{:S(2)}, u32[]{:S(2)}) collective-permute-start(bf16[154,768]{1,0:T(8,128)(2,1)S(1)} %copy-done.86), channel_id=1, source_target_pairs={{0,1},{1,0},{2,3},{3,2},{4,5},{5,4},{6,7},{7,6},{8,9},{9,8},{10,11... | collective-permute-start | bytes 709640 | tf_op jit(solution)/shard_map/ppermute | solution.py:289
  265.2 52.8 %collective-permute-start.6 = (bf16[1024,768]{0,1:T(8,128)(2,1)}, bf16[1024,768]{0,1:T(8,128)(2,1)}, u32[]{:S(2)}, u32[]{:S(2)}) collective-permute-start(bf16[1024,768]{0,1:T(8,128)(2,1)} %add_convert_fusion.8), channel_id=1, source_target_pairs={{0,1},{1,0},{2,3},{3,2},{4,5},{5,4},{6,7},{7,6},{8,9},{9,8},{10,11... | collective-permute-start | bytes 4718600 | tf_op jit(solution)/shard_map/ppermute | solution.py:289
  439.3 42.9 %collective-permute-start.16 = (bf16[1178,768]{1,0:T(8,128)(2,1)}, bf16[1178,768]{1,0:T(8,128)(2,1)}, u32[]{:S(2)}, u32[]{:S(2)}) collective-permute-start(bf16[1178,768]{1,0:T(8,128)(2,1)} %pad_maximum_fusion.10), channel_id=1, source_target_pairs={{0,1},{1,0},{2,3},{3,2},{4,5},{5,4},{6,7},{7,6},{8,9},{9,8},{10,11... | collective-permute-start | bytes 5428232 | tf_op jit(solution)/shard_map/ppermute | solution.py:289
  440.9 110.1 %collective-permute-start.21 = (bf16[4,384,1536]{2,1,0:T(8,128)(2,1)}, bf16[4,384,1536]{2,1,0:T(8,128)(2,1)}, u32[]{:S(2)}, u32[]{:S(2)}) collective-permute-start(bf16[4,384,1536]{2,1,0:T(8,128)(2,1)} %pad_maximum_fusion), channel_id=1, source_target_pairs={{0,4},{2,6},{4,0},{6,2},{8,12},{10,14},{12,8},{14,10},{16,20},{18,... | collective-permute-start | bytes 14155784 | tf_op jit(solution)/shard_map/ppermute | solution.py:343
  455.9 101.0 %collective-permute-start.17 = (bf16[1178,768]{1,0:T(8,128)(2,1)}, bf16[1178,768]{1,0:T(8,128)(2,1)}, u32[]{:S(2)}, u32[]{:S(2)}) collective-permute-start(bf16[1178,768]{1,0:T(8,128)(2,1)} %pad_maximum_fusion.11), channel_id=1, source_target_pairs={{0,1},{1,0},{2,3},{3,2},{4,5},{5,4},{6,7},{7,6},{8,9},{9,8},{10,11... | collective-permute-start | bytes 5428232 | tf_op jit(solution)/shard_map/ppermute | solution.py:289
  543.7 52.4 %collective-permute-start.18 = (bf16[1178,256]{1,0:T(8,128)(2,1)}, bf16[1178,256]{1,0:T(8,128)(2,1)}, u32[]{:S(2)}, u32[]{:S(2)}) collective-permute-start(bf16[1178,256]{1,0:T(8,128)(2,1)} %pad_maximum_fusion.30), channel_id=1, source_target_pairs={{0,1},{1,0},{2,3},{3,2},{4,5},{5,4},{6,7},{7,6},{8,9},{9,8},{10,11... | collective-permute-start | bytes 1809416 | tf_op jit(solution)/shard_map/ppermute | solution.py:289
  544.1 80.4 %collective-permute-start.22 = (bf16[1178,256]{1,0:T(8,128)(2,1)}, bf16[1178,256]{1,0:T(8,128)(2,1)}, u32[]{:S(2)}, u32[]{:S(2)}) collective-permute-start(bf16[1178,256]{1,0:T(8,128)(2,1)} %pad_maximum_fusion.31), channel_id=1, source_target_pairs={{0,1},{1,0},{2,3},{3,2},{4,5},{5,4},{6,7},{7,6},{8,9},{9,8},{10,11... | collective-permute-start | bytes 1809416 | tf_op jit(solution)/shard_map/ppermute | solution.py:289
  545.7 117.6 %collective-permute-start.26 = (bf16[4,96,6144]{2,1,0:T(8,128)(2,1)}, bf16[4,96,6144]{2,1,0:T(8,128)(2,1)}, u32[]{:S(2)}, u32[]{:S(2)}) collective-permute-start(bf16[4,96,6144]{2,1,0:T(8,128)(2,1)} %pad_maximum_fusion.1), channel_id=1, source_target_pairs={{0,4},{2,6},{4,0},{6,2},{8,12},{10,14},{12,8},{14,10},{16,20},{18,... | collective-permute-start | bytes 14155784 | tf_op jit(solution)/shard_map/ppermute | solution.py:343
  570.1 190.9 %reduce-scatter.7.cloned.1.call-start = ((), (), s32[]{:S(2)}) async-start(), calls=%async_computation.12 | async-start | bytes 5898240 | tf_op jit(solution)/shard_map/reduce_scatter | solution.py:365
  587.3 101.0 %collective-permute-start.23 = (bf16[1178,256]{1,0:T(8,128)(2,1)}, bf16[1178,256]{1,0:T(8,128)(2,1)}, u32[]{:S(2)}, u32[]{:S(2)}) collective-permute-start(bf16[1178,256]{1,0:T(8,128)(2,1)} %pad_maximum_fusion.32), channel_id=1, source_target_pairs={{0,1},{1,0},{2,3},{3,2},{4,5},{5,4},{6,7},{7,6},{8,9},{9,8},{10,11... | collective-permute-start | bytes 1809416 | tf_op jit(solution)/shard_map/ppermute | solution.py:289
  674.7 144.6 %reduce-scatter.9.cloned.1.call-start = ((), (), s32[]{:S(2)}) async-start(), calls=%async_computation.13 | async-start | bytes 2949120 | tf_op jit(solution)/shard_map/reduce_scatter | solution.py:365
  676.3 55.0 %collective-permute-start.34 = (bf16[4,96,1536]{2,1,0:T(8,128)(2,1)}, bf16[4,96,1536]{2,1,0:T(8,128)(2,1)S(1)}, u32[]{:S(2)}, u32[]{:S(2)}) collective-permute-start(bf16[4,96,1536]{2,1,0:T(8,128)(2,1)} %pad_maximum_fusion.21), channel_id=1, source_target_pairs={{0,4},{2,6},{4,0},{6,2},{8,12},{10,14},{12,8},{14,10},{16,20},{18,... | collective-permute-start | bytes 3538952 | tf_op jit(solution)/shard_map/ppermute | solution.py:343
  676.9 54.4 %collective-permute-start.35 = (bf16[4,96,1536]{2,1,0:T(8,128)(2,1)}, bf16[4,96,1536]{2,1,0:T(8,128)(2,1)S(1)}, u32[]{:S(2)}, u32[]{:S(2)}) collective-permute-start(bf16[4,96,1536]{2,1,0:T(8,128)(2,1)} %pad_maximum_fusion.22), channel_id=1, source_target_pairs={{0,4},{2,6},{4,0},{6,2},{8,12},{10,14},{12,8},{14,10},{16,20},{18,... | collective-permute-start | bytes 3538952 | tf_op jit(solution)/shard_map/ppermute | solution.py:343
  687.5 103.3 %collective-permute-start.30 = (bf16[4,96,1536]{2,1,0:T(8,128)(2,1)}, bf16[4,96,1536]{2,1,0:T(8,128)(2,1)}, u32[]{:S(2)}, u32[]{:S(2)}) collective-permute-start(bf16[4,96,1536]{2,1,0:T(8,128)(2,1)} %pad_maximum_fusion.23), channel_id=1, source_target_pairs={{0,4},{2,6},{4,0},{6,2},{8,12},{10,14},{12,8},{14,10},{16,20},{18,... | collective-permute-start | bytes 3538952 | tf_op jit(solution)/shard_map/ppermute | solution.py:343
  725.7 54.2 %collective-permute-start.27 = (bf16[1178,768]{1,0:T(8,128)(2,1)}, bf16[1178,768]{1,0:T(8,128)(2,1)}, u32[]{:S(2)}, u32[]{:S(2)}) collective-permute-start(bf16[1178,768]{1,0:T(8,128)(2,1)} %pad_maximum_fusion.12), channel_id=1, source_target_pairs={{0,1},{1,0},{2,3},{3,2},{4,5},{5,4},{6,7},{7,6},{8,9},{9,8},{10,11... | collective-permute-start | bytes 5428232 | tf_op jit(solution)/shard_map/ppermute | solution.py:289
  729.1 103.7 %collective-permute-start.37 = (f32[384,1536]{1,0:T(8,128)}, f32[384,1536]{1,0:T(8,128)}, u32[]{:S(2)}, u32[]{:S(2)}) collective-permute-start(f32[384,1536]{1,0:T(8,128)} %convert_element_type.587), channel_id=1, source_target_pairs={{1,2},{2,1},{5,6},{6,5},{9,10},{10,9},{13,14},{14,13},{17,18},{18,... | collective-permute-start | bytes 7077896 | tf_op jit(solution)/shard_map/ppermute | solution.py:444
  735.9 38.2 %collective-permute-start.32 = (bf16[768,768]{1,0:T(8,128)(2,1)}, bf16[768,768]{1,0:T(8,128)(2,1)}, u32[]{:S(2)}, u32[]{:S(2)}) collective-permute-start(bf16[768,768]{1,0:T(8,128)(2,1)} %convolution_convert_fusion.4), channel_id=1, source_target_pairs={{0,2},{2,0},{4,6},{6,4},{8,10},{10,8},{12,14},{14,12},{16,18},{18,... | collective-permute-start | bytes 3538952 | tf_op jit(solution)/shard_map/ppermute | solution.py:326
  804.9 67.6 %reduce-scatter.11.cloned.1.call-start = ((), (), s32[]{:S(2)}) async-start(), calls=%async_computation.14 | async-start | bytes 2949120 | tf_op jit(solution)/shard_map/reduce_scatter | solution.py:365
  (189 other events, 2595.1 us)
Sparse Core Ops, SparseCore 0:
  12.9 111.3 all-gather.3
  125.9 101.2 all-gather.5
  228.8 98.9 all-gather.7
  570.3 84.8 reduce-scatter.4
  674.8 86.1 reduce-scatter.6
  763.7 49.5 reduce-scatter.8
  819.4 48.6 reduce-scatter.10

commit v3 on v2

--- a/solution.py
+++ b/solution.py
@@ -32,15 +32,15 @@
 
 
 def attend_kernel(real, qi, qt, ki, kt, vi, vt, oi, ot, lse, q_s, k_s, v_s, s_0, s_1):
-    ni, n = qi.shape[0], q_s.shape[0]
+    ni, n, nk = qi.shape[0], q_s.shape[0], k_s.shape[0]
     scale = jnp.asarray(HEAD_DIM**-0.5, bf16)
     q_s[:ni, :] = qi[...] * scale
     q_s[ni:, :] = qt[...] * scale
     k_s[:ni, :] = ki[...]
-    k_s[ni:, :] = kt[...]
+    k_s[ni:, :] = kt[: nk - ni, :]
     v_s[:, :ni] = vi[...].T
-    v_s[:, ni:] = vt[...].T
-    key = lax.broadcasted_iota(jnp.int32, (n - ni, BLOCK), 0)
+    v_s[:, ni:] = vt[...].T[:, : nk - ni]
+    key = lax.broadcasted_iota(jnp.int32, (nk - ni, BLOCK), 0)
     held = (s_0, s_1)
 
     def scores(i, h):
@@ -77,22 +77,23 @@
 
 
 def attend_back_kernel(
-    real, qi, qt, ki, kt, vi, vt, di, dt, lse, dqi, dqt, dki, dkt, dvi, dvt,
-    q_s, k_s, kt_s, v_s, d_s, dq_s, dk_s, dv_s,
+    real, pairs, qi, qt, ki, kt, vi, vt, di, dt, lse, *rest
 ):
-    ni, n = qi.shape[0], q_s.shape[0]
+    out_i, out_t, q_s, k_s, kt_s, v_s, d_s, dq_s, dk_s, dv_s = rest[-10:]
+    ni, n, nk = qi.shape[0], q_s.shape[0], k_s.shape[0]
+    nt = nk - ni
     scale = HEAD_DIM**-0.5
     q_s[:ni, :] = qi[...] * jnp.asarray(scale, bf16)
     q_s[ni:, :] = qt[...] * jnp.asarray(scale, bf16)
     k_s[:ni, :] = ki[...]
-    k_s[ni:, :] = kt[...]
+    k_s[ni:, :] = kt[:nt, :]
     kt_s[:, :ni] = ki[...].T
-    kt_s[:, ni:] = kt[...].T
+    kt_s[:, ni:] = kt[...].T[:, :nt]
     v_s[:ni, :] = vi[...]
-    v_s[ni:, :] = vt[...]
+    v_s[ni:, :] = vt[:nt, :]
     d_s[:ni, :] = di[...]
     d_s[ni:, :] = dt[...]
-    key = lax.broadcasted_iota(jnp.int32, (n - ni, BLOCK), 0)
+    key = lax.broadcasted_iota(jnp.int32, (nt, BLOCK), 0)
     for i in range(n // BLOCK):
         rows = slice(i * BLOCK, (i + 1) * BLOCK)
         dq = []
@@ -114,30 +115,36 @@
             dq.append(mm_nn(kt_s[head, :], d_scores))
         dq_s[:, rows] = jnp.concatenate(dq, axis=0)
     d_q = (dq_s[...] * scale).T.astype(bf16)
-    dqi[...] = d_q[:ni]
-    dqt[...] = d_q[ni:]
-    dki[...] = dk_s[:ni, :].astype(bf16)
-    dkt[...] = dk_s[ni:, :].astype(bf16)
-    dvi[...] = dv_s[:ni, :].astype(bf16)
-    dvt[...] = dv_s[ni:, :].astype(bf16)
-
-
-def projection_specs(ni, nt, total, first):
+    at = pl.program_id(0)
+
+    def lanes(j):
+        return pl.ds(pl.multiple_of((j * pairs + at) * PAIR, PAIR), PAIR)
+
+    out_i[:, lanes(0)] = d_q[:ni]
+    out_t[:, lanes(0)] = d_q[ni:]
+    for j, total in ((1, dk_s), (2, dv_s)):
+        out_i[:, lanes(j)] = total[:ni, :].astype(bf16)
+        out_t[:nt, lanes(j)] = total[ni:, :].astype(bf16)
+        out_t[nt:, lanes(j)] = jnp.zeros((n - nk, PAIR), bf16)
+
+
+def projection_specs(ni, nt, group, pairs):
     specs = []
     for j in range(3):
-        at = lambda p, j=j: (0, j * total + first + p)
+        at = lambda p, j=j: (0, (3 * group + j) * pairs + p)
         specs += [pl.BlockSpec((ni, PAIR), at), pl.BlockSpec((nt, PAIR), at)]
     return specs
 
 
-def attend(image, text, real, first, pairs):
+def attend(image, text, real, group, pairs):
     ni, nt = image.shape[0], text.shape[0]
-    n, total = ni + nt, image.shape[1] // 3 // PAIR
+    n = ni + nt
+    nk = ni + (real + 15) // 16 * 16
     at = lambda p: (0, p)
     return pl.pallas_call(
         partial(attend_kernel, real),
         grid=(pairs,),
-        in_specs=projection_specs(ni, nt, total, first),
+        in_specs=projection_specs(ni, nt, group, pairs),
         out_specs=[
             pl.BlockSpec((ni, PAIR), at),
             pl.BlockSpec((nt, PAIR), at),
@@ -150,10 +157,10 @@
         ],
         scratch_shapes=[
             pltpu.VMEM((n, PAIR), bf16),
-            pltpu.VMEM((n, PAIR), bf16),
-            pltpu.VMEM((PAIR, n), bf16),
-            pltpu.VMEM((n, BLOCK), f32),
-            pltpu.VMEM((n, BLOCK), f32),
+            pltpu.VMEM((nk, PAIR), bf16),
+            pltpu.VMEM((PAIR, nk), bf16),
+            pltpu.VMEM((nk, BLOCK), f32),
+            pltpu.VMEM((nk, BLOCK), f32),
         ],
         compiler_params=pltpu.CompilerParams(vmem_limit_bytes=40 * 2**20),
         cost_estimate=pl.CostEstimate(
@@ -164,29 +171,31 @@
     )(image, text, image, text, image, text)
 
 
-def attend_back(image, text, real, first, pairs, d_image, d_text, lse):
+def attend_back(image, text, real, group, pairs, d_image, d_text, lse, filled):
     ni, nt = image.shape[0], text.shape[0]
-    n, total = ni + nt, image.shape[1] // 3 // PAIR
+    n = ni + nt
+    nk = ni + (real + 15) // 16 * 16
     at = lambda p: (0, p)
     one_i, one_t = pl.BlockSpec((ni, PAIR), at), pl.BlockSpec((nt, PAIR), at)
-    out_i = jax.ShapeDtypeStruct((ni, pairs * PAIR), bf16)
-    out_t = jax.ShapeDtypeStruct((nt, pairs * PAIR), bf16)
+    wide = 3 * pairs * PAIR
     return pl.pallas_call(
-        partial(attend_back_kernel, real),
+        partial(attend_back_kernel, real, pairs),
         grid=(pairs,),
-        in_specs=projection_specs(ni, nt, total, first)
-        + [one_i, one_t, pl.BlockSpec((1, 2, n), lambda p: (p, 0, 0))],
-        out_specs=[one_i, one_t] * 3,
-        out_shape=[out_i, out_t] * 3,
+        in_specs=projection_specs(ni, nt, group, pairs)
+        + [one_i, one_t, pl.BlockSpec((1, 2, n), lambda p: (p, 0, 0))]
+        + [pl.BlockSpec(memory_space=pl.ANY)] * len(filled),
+        out_specs=[pl.BlockSpec((n_, wide), lambda p: (0, group)) for n_ in (ni, nt)],
+        out_shape=[jax.ShapeDtypeStruct(a.shape, bf16) for a in (image, text)],
+        input_output_aliases={9: 0, 10: 1} if filled else {},
         scratch_shapes=[
             pltpu.VMEM((n, PAIR), bf16),
-            pltpu.VMEM((n, PAIR), bf16),
-            pltpu.VMEM((PAIR, n), bf16),
-            pltpu.VMEM((n, PAIR), bf16),
+            pltpu.VMEM((nk, PAIR), bf16),
+            pltpu.VMEM((PAIR, nk), bf16),
+            pltpu.VMEM((nk, PAIR), bf16),
             pltpu.VMEM((n, PAIR), bf16),
             pltpu.VMEM((PAIR, n), f32),
-            pltpu.VMEM((n, PAIR), f32),
-            pltpu.VMEM((n, PAIR), f32),
+            pltpu.VMEM((nk, PAIR), f32),
+            pltpu.VMEM((nk, PAIR), f32),
         ],
         compiler_params=pltpu.CompilerParams(vmem_limit_bytes=40 * 2**20),
         cost_estimate=pl.CostEstimate(
@@ -194,7 +203,7 @@
             bytes_accessed=pairs * n * PAIR * 2 * 8,
             transcendentals=pairs * 2 * n * n,
         ),
-    )(image, text, image, text, image, text, d_image, d_text, lse)
+    )(image, text, image, text, image, text, d_image, d_text, lse, *filled)
 
 
 def split_heads(a):
@@ -228,11 +237,8 @@
     d_scores = d_scores.astype(bf16)
     d_q = dot("hqk,khd->qhd", d_scores, k) * factor
     d_k = dot("hqk,qhd->khd", d_scores, q) * factor
-    outs = []
-    for g in (d_q, d_k, d_v):
-        g = g.reshape(-1, width).astype(bf16)
-        outs += [g[:ni], jnp.pad(g[ni:], ((0, text.shape[0] - real), (0, 0)))]
-    return outs
+    out = jnp.concatenate([g.reshape(-1, width).astype(bf16) for g in (d_q, d_k, d_v)], axis=1)
+    return out[:ni], jnp.pad(out[ni:], ((0, text.shape[0] - real), (0, 0)))
 
 
 def gelu_both(v):
@@ -283,6 +289,7 @@
     YSWAP = [(r, r ^ 2) for r in range(R)]
     YGROUPS = [[(z * Y + y) * 2 + c for y in range(Y)] for z in range(Z) for c in range(2)]
     ZGROUPS = [[(z * Y + y) * 2 + c for z in range(Z)] for y in range(Y) for c in range(2)]
+    ZYGROUPS = [[2 * k + c for k in range(ZY)] for c in range(2)]
     XSWAP = [(0, 1), (1, 0)]
 
     def swap(a):
@@ -304,10 +311,10 @@
     def gather_features(own):
         return whole(own, send(own))
 
-    def col_start(makes):
+    def col_start(makes, wait=False):
         if pair:
             sent = jnp.concatenate([make(1 - me_c).astype(bf16) for make in makes], axis=0)
-            return sent, swap(sent)
+            return sent, None if wait else swap(sent)
         sent = jnp.concatenate(
             [jnp.concatenate([make(c) for c in range(C)], axis=-1) for make in makes], axis=0
         )
@@ -322,41 +329,35 @@
         return lax.psum(a, "col")
 
     def core_start(part):
-        sent = part(1 - my_core).astype(bf16)
+        sent = part[0]().astype(bf16)
         return sent, lax.ppermute(sent, "row", CORE)
 
     def y_start(parts, gots):
-        owns = []
-        for part, got in zip(parts, gots):
-            own = part(my_core) + got.astype(f32)
-            owns.append(own.reshape(Z, Y, own.shape[0] // ZY, own.shape[1]))
+        owns = [
+            [share() + take(got).astype(f32) for share, take in part[1]]
+            for part, got in zip(parts, gots)
+        ]
         if Y == 2:
-            sent = jnp.concatenate(
-                [
-                    lax.dynamic_index_in_dim(own, 1 - my_y, 1, keepdims=False).astype(bf16)
-                    for own in owns
-                ],
-                axis=2,
-            )
-            kept = [lax.dynamic_index_in_dim(own, my_y, 1, keepdims=False) for own in owns]
-            sent, *kept = lax.optimization_barrier((sent, *kept))
-            return sent, kept, lax.ppermute(sent, "row", YSWAP)
-        own = jnp.concatenate([own.astype(bf16) for own in owns], axis=3)
+            owns = [[own.reshape(Z, own.shape[0] // Z, -1) for own in pieces] for pieces in owns]
+            sent = jnp.concatenate([pieces[0].astype(bf16) for pieces in owns], axis=2)
+            return sent, [pieces[1] for pieces in owns], lax.ppermute(sent, "row", YSWAP)
+        own = jnp.concatenate([pieces[0] for pieces in owns], axis=1)
+        own = own.reshape(Z, Y, own.shape[0] // ZY, -1).astype(bf16)
         if Y > 1:
             own = lax.psum_scatter(own, "row", scatter_dimension=1, axis_index_groups=YGROUPS)
-            return own, own, None
-        return own[:, 0], own[:, 0], None
+        else:
+            own = own[:, 0]
+        return own, [own], None
 
     def z_start(states, previous, *earlier):
         pieces = []
         for _, kept, got in states:
-            if got is None:
-                pieces.append(kept.astype(bf16))
-                continue
-            got, at = after(got, *earlier), 0
-            for k in kept:
-                pieces.append((k + got[:, :, at : at + k.shape[2]].astype(f32)).astype(bf16))
-                at += k.shape[2]
+            if got is not None:
+                got, at, own, kept = after(got, *earlier), 0, kept, []
+                for a in own:
+                    kept.append((a + got[:, :, at : at + a.shape[2]].astype(f32)).astype(bf16))
+                    at += a.shape[2]
+            pieces += kept
         kept = jnp.concatenate(pieces, axis=2)
         if Z == 1:
             return [kept, kept[0]]
@@ -365,16 +366,62 @@
         summed = lax.psum_scatter(kept, "row", scatter_dimension=0, axis_index_groups=ZGROUPS)
         return [kept, summed]
 
-    def rows_of(a):
+    def both_start(parts, gots):
+        own = [share() + got.astype(f32) for share, got in zip(parts, gots)]
+        own = jnp.concatenate([a.astype(bf16) for a in own], axis=1)
+        own = own.reshape(ZY, own.shape[0] // ZY, -1)
+        return [
+            own,
+            lax.psum_scatter(own, "row", scatter_dimension=0, axis_index_groups=ZYGROUPS),
+        ]
+
+    def rows_of(a, small=False, plain=Y != 2):
         t, width = a.shape
-        parts = a.reshape(t, ZY, 2, width // R)
-        return [
-            lax.dynamic_index_in_dim(parts, core, 2, keepdims=False).reshape(t, width // 2)
-            for core in (1 - my_core, my_core)
-        ]
+        blk = width // R
+        if plain and not small:
+            parts = a.reshape(t, ZY, 2, blk)
+            other, own = (
+                lax.dynamic_index_in_dim(parts, core, 2, keepdims=False).reshape(t, width // 2)
+                for core in (1 - my_core, my_core)
+            )
+            return other, [own]
+        if small:
+            at = jnp.arange(width)
+            core, y = at // (width // 2), at // (width // 4) % 2
+            core = jnp.where(core == 0, 1 - my_core, my_core)
+            y = jnp.where(y == 0, 1 - my_y, my_y)
+            row = (at // blk % ZY if plain else at // blk % Z * Y + y) * 2 + core
+            pick = (row * blk + at % blk)[None, :] == jnp.arange(width)[:, None]
+            picked = dot("tp,pq->tq", a, pick.astype(bf16)).astype(bf16)
+            half, quarter = width // 2, width // 4
+            if plain:
+                return picked[:, :half], [picked[:, half:]]
+            return picked[:, :half], [picked[:, half : half + quarter], picked[:, -quarter:]]
+        parts = a.reshape(t, Z, Y, 2, blk)
+
+        def pick_rows(core, y):
+            got = lax.dynamic_index_in_dim(parts, core, 3, keepdims=False)
+            return lax.dynamic_index_in_dim(got, y, 2, keepdims=False).reshape(t, Z * blk)
+
+        other = jnp.concatenate(
+            [pick_rows(1 - my_core, 1 - my_y), pick_rows(1 - my_core, my_y)], axis=1
+        )
+        return other, [pick_rows(my_core, 1 - my_y), pick_rows(my_core, my_y)]
+
+    def rows_of_both(pair_of, **how):
+        return [rows_of(pair_of[0], **how), rows_of(pair_of[1], small=True, **how)]
 
     def product_part(rows, b):
-        return lambda core: dot("tp,tn->pn", rows[0] if core is not my_core else rows[1], b)
+        other, own = rows
+        size = other.shape[1] // len(own)
+
+        def share(a):
+            return lambda: dot("tp,tn->pn", a, b)
+
+        def take(i):
+            return lambda got: got[i * size : (i + 1) * size]
+
+        return share(other), [(share(a), take(i)) for i, a in enumerate(own)]
 
     def unpack(packed):
         rows = packed.reshape(packed.shape[0], 2 * w)
@@ -387,6 +434,10 @@
     def gather_rows(a, order=None):
         return lax.all_gather(a, "row", axis=1, tiled=True, axis_index_groups=order)
 
+    total = w // PAIR
+    groups = (3 if total % 3 == 0 else 1) if kernels else 1
+    pairs = total // groups
+    wide = w // groups
     fan = MODEL_WIDTH // R
     qkv_shard = qkv_weight.reshape(fan, 6 * w)
     proj_shard = proj_weight.reshape(fan, 2 * w)
@@ -394,7 +445,11 @@
         [
             jnp.concatenate(
                 [
-                    qkv_shard[:, m * 3 * w : (m + 1) * 3 * w].astype(bf16),
+                    qkv_shard[:, (3 * m + j) * w + g * wide :][:, :wide].astype(bf16)
+                    for g in range(groups)
+                    for j in range(3)
+                ]
+                + [
                     proj_shard[:, m * w : (m + 1) * w].astype(bf16),
                 ],
                 axis=1,
@@ -415,7 +470,10 @@
     mod = jnp.sum(mod, axis=0).reshape(2, 6, w)
 
     packed = (image_tokens, text_tokens)
-    packed_got = [send(after(p, silu_got)) if pair else None for p in packed]
+    packed_got = None
+    if pair:
+        packed_got = swap(jnp.concatenate(packed, axis=0))
+        packed_got = [packed_got[: packed[0].shape[0]], packed_got[packed[0].shape[0] :]]
     first_mod = gather_features(mod[:, 0:2].reshape(4, w)).reshape(2, 2, MODEL_WIDTH)
     inputs = [unpack(p).astype(f32) for p in packed]
     cotangents = [unpack(p).astype(f32) for p in (image_cotangent, text_cotangent)]
@@ -424,8 +482,7 @@
     padding = -(counts[0] + real) % BLOCK
     d_branch2 = [(mod[m, 5] * cotangents[m]).astype(bf16) for m in both]
 
-    early = [p for p in packed_got if p is not None] + [first_mod]
-    fc1_weight, fc2_weight = lax.optimization_barrier((fc1_weight, fc2_weight, *early))[:2]
+    fc1_weight, fc2_weight = lax.optimization_barrier((fc1_weight, fc2_weight, silu_got))[:2]
     fc1_shard = jnp.stack([fc1_weight[:, m] for m in both]).astype(bf16)
     blk2 = fc2_weight.shape[0]
     fc2_shard = fc2_weight.reshape(blk2, 2 * w)
@@ -440,14 +497,17 @@
         stays = me_r % C == me_c
         ORDER = [[k * C + c for c in range(C) for k in range(R // C)]]
 
-        def move_units(a):
-            return jnp.where(stays, a, lax.ppermute(a, ("row", "col"), MOVES))
+        def move_units(a, *earlier):
+            moved = lax.ppermute(a, ("row", "col"), MOVES)
+            return jnp.where(stays, a, after(moved, *earlier) if earlier else moved)
 
         unmove_units = move_units
         group = fc1_shard.reshape(2, fan, half, 2, blk2)
         mine = lax.dynamic_index_in_dim(group, me_c, 3, keepdims=False)
         theirs = swap(lax.dynamic_index_in_dim(group, 1 - me_c, 3, keepdims=False))
-        fc1_shard = natural(mine, theirs, axis=2).reshape(fc1_shard.shape)
+
+        def moved_columns(*earlier):
+            return natural(mine, after(theirs, *earlier), axis=2).reshape(fc1_shard.shape)
 
         def unmove_columns(g):
             g = g.reshape(fan, 2, blocks, blk2)
@@ -466,8 +526,11 @@
         ]
         ORDER = None
 
-        def move_units(a):
+        def move_units(a, *earlier):
             return lax.ppermute(a, ("row", "col"), MOVES)
+
+        def moved_columns(*earlier):
+            return fc1_shard
 
         def unmove_units(a):
             return lax.ppermute(a, ("row", "col"), [(b, a) for a, b in MOVES])
@@ -475,10 +538,6 @@
         def unmove_columns(g):
             return g
 
-    fc2_shard = move_units(fc2_shard)
-    d_branch2_got = [send(after(d_branch2[m], fc1_shard, fc2_shard)) for m in both]
-    fc1_full = gather_rows(fc1_shard)
-    fc2_full = gather_rows(fc2_shard, ORDER).reshape(2, C, units, w)
 
     def padded(a):
         return jnp.pad(a, ((0, padding), (0, 0)))
@@ -501,19 +560,23 @@
         )
     hidden1[1] = padded(hidden1[1])
     norm1 = [(inputs[m] - mean1[m]) * rstd1[m] for m in both]
-    projected = [dot("td,de->te", hidden1[m], qkv_full[m]).astype(bf16) for m in both]
-
-    total = w // PAIR
-    groups = (3 if total % 3 == 0 else 1) if kernels else 1
-    pairs = total // groups
-    wide = w // groups
+    fc1_moved = moved_columns(*hidden1)
+    fc1_full = gather_rows(fc1_moved)
+    d_branch2_own = jnp.concatenate(d_branch2, axis=0)
+    d_branch2_got = send(d_branch2_own)
+    fc2_shard = after(fc2_shard, d_branch2_got)
+    hidden1_in = [after(hidden1[0], d_branch2_got), hidden1[1]]
+    projected = [dot("td,de->te", hidden1_in[m], qkv_full[m]).astype(bf16) for m in both]
+    fc2_moved = move_units(fc2_shard, *projected)
+    fc2_full = gather_rows(fc2_moved, ORDER).reshape(2, C, units, w)
+
     attended, attended_got, lse = [], [], []
     for g in range(groups):
         text = projected[1]
         if g > 1:
             text = after(text, attended_got[g - 2])
         if kernels:
-            out_i, out_t, saved = attend(projected[0], text, real, g * pairs, pairs)
+            out_i, out_t, saved = attend(projected[0], text, real, g, pairs)
         else:
             out_i, out_t, saved = plain_attend(projected[0], text, real)
         attended.append(jnp.concatenate([out_i, out_t[:real]], axis=0))
@@ -523,11 +586,7 @@
         jnp.concatenate(attended, axis=1), jnp.concatenate(attended_got, axis=1)
     )
     attended_full = [attended_full[: counts[0]], attended_full[counts[0] :]]
-    attended_rows = [rows_of(a) for a in attended_full]
-    hidden1_rows = [rows_of(a) for a in hidden1]
-    d_branch2_full = [
-        whole(d_branch2[m], after(d_branch2_got[m], attended[-1])) for m in both
-    ]
+    attended_rows, hidden1_rows = rows_of_both(attended_full), rows_of_both(hidden1)
 
     branch1 = [dot("te,eb->tb", attended_full[m], proj_full[m]) for m in both]
     middle = [inputs[m] + mod[m, 2] * branch1[m] for m in both]
@@ -548,41 +607,39 @@
     rstd2 = [lax.rsqrt(sq - mean * mean + EPSILON) for mean, sq in stats]
     norm2 = [(middle[m] - stats[m][0]) * rstd2[m] for m in both]
     hidden2 = [(norm2[m] * (1.0 + mod[m, 4]) + mod[m, 3]).astype(bf16) for m in both]
+    hidden2[0] = after(hidden2[0], hidden2[1])
     hidden2_got = [send(a) for a in hidden2]
-    hidden2_got[0], *rows = lax.optimization_barrier(
-        (hidden2_got[0], *attended_rows[0], *attended_rows[1], *hidden1_rows[0], *hidden1_rows[1])
-    )
-    attended_rows, hidden1_rows = [rows[:2], rows[2:4]], [rows[4:6], rows[6:]]
+    hidden2_got[0], attended_rows, hidden1_rows = lax.optimization_barrier(
+        (hidden2_got[0], attended_rows, hidden1_rows)
+    )
     hidden2_full = [whole(a, got) for a, got in zip(hidden2, hidden2_got)]
-    hidden2_rows = [rows_of(a) for a in hidden2_full]
+    d_branch2_full = whole(d_branch2_own, after(d_branch2_got, hidden2[0]))
+    d_branch2_full = [d_branch2_full[: counts[0]], d_branch2_full[counts[0] :]]
+    hidden2_rows = rows_of_both(hidden2_full, plain=True)
     preact = [dot("td,df->tf", hidden2_full[m], fc1_full[m]) for m in both]
     pairs_of = [gelu_both(a) for a in preact]
     activated = [a.astype(bf16) for a, _ in pairs_of]
     slope = [s for _, s in pairs_of]
 
     def fc2_part(m, act):
-        def part(core):
+        def share(a, core):
+            grad = d_branch2_full[m]
             if parity:
-                grad = lax.dynamic_slice_in_dim(d_branch2_full[m], core * w, w, 1)
-                return dot("tf,te->fe", act, grad)
-            whole_grad = jnp.concatenate(
-                [
-                    dot("tf,te->fe", act, d_branch2_full[m][:, c * w : (c + 1) * w])
-                    for c in range(C)
-                ],
-                axis=0,
-            )
-            return lax.dynamic_index_in_dim(
-                whole_grad.reshape(ZY, 2, blk2, w), core, 1, keepdims=False
-            ).reshape(ZY * blk2, w)
-
-        return part
+                grad = lax.dynamic_slice_in_dim(grad, core * w, w, 1)
+                return lambda: dot("tf,te->fe", a, grad)
+            shares = [dot("tf,te->fe", a, grad[:, c * w : (c + 1) * w]) for c in range(C)]
+            shares = jnp.concatenate(shares, axis=0).reshape(ZY, 2, blk2, w)
+            one = lax.dynamic_index_in_dim(shares, core, 1, keepdims=False)
+            return lambda: one.reshape(ZY * blk2, w)
+
+        return share(act, 1 - my_core), share(act, my_core)
 
     fc2_core = [core_start(fc2_part(m, activated[m])) for m in both]
-    act_later = [after(activated[m], fc2_core[0][0], fc2_core[1][0]) for m in both]
-    fc2_y = y_start([fc2_part(m, act_later[m]) for m in both], [s[1] for s in fc2_core])
-
-    grads = [after(d_branch2_full[m], fc2_y[0]) for m in both]
+    act_later = [after(activated[m], *[s[0] for s in fc2_core]) for m in both]
+    fc2_z = both_start(
+        [fc2_part(m, act_later[m])[1] for m in both], [s[1] for s in fc2_core]
+    )
+    grads = [after(d_branch2_full[m], fc2_z[0]) for m in both]
     none = jnp.minimum(me_r, 0)
     d_activated = [
         dot(
@@ -601,30 +658,32 @@
 
     hidden2_col = col_start([hidden2_make(m, d_preact[m]) for m in both])
 
+    d_next = [after(d_preact[m], hidden2_col[0]) for m in both]
+    fc1_core = [core_start(product_part(hidden2_rows[m], d_next[m])) for m in both]
+    fc1_sent = [s[0] for s in fc1_core]
+
     def branch2_make(m, act):
         return lambda c: dot(
             "tf,fe->te", act, lax.dynamic_slice(fc2_full, (m, c, 0, 0), (1, 1, units, w))[0, 0]
         )
 
-    act_last = [after(activated[m], hidden2_col[0]) for m in both]
-    branch2_col = col_start([branch2_make(m, act_last[m]) for m in both])
-    d_next = [after(d_preact[m], hidden2_col[0]) for m in both]
-    fc1_core = [core_start(product_part(hidden2_rows[m], d_next[m])) for m in both]
-    d_next = [after(d_next[m], fc1_core[0][0], fc1_core[1][0]) for m in both]
-    fc1_y = y_start(
-        [product_part(hidden2_rows[m], d_next[m]) for m in both], [s[1] for s in fc1_core]
-    )
-    d_next = [after(d_next[m], fc1_y[0]) for m in both]
+    act_last = [after(activated[m], *fc1_sent) for m in both]
+    branch2_col = col_start([branch2_make(m, act_last[m]) for m in both], wait=True)
+    d_next = [after(d_next[m], branch2_col[0]) for m in both]
+    fc1_z = both_start(
+        [product_part(hidden2_rows[m], d_next[m])[1][0][0] for m in both],
+        [s[1] for s in fc1_core],
+    )
     d_hidden2 = col_end(
-        [hidden2_make(m, d_next[m]) for m in both], hidden2_col, fc1_y[0], branch2_col[0]
-    )
-    d_hidden2 = [d.astype(bf16) for d in d_hidden2]
-    fc2_z = z_start([fc2_y], None, *d_hidden2)
-    d_hidden2 = [d.astype(f32) for d in d_hidden2]
-
-    def norm_back(d_hidden, norm, rstd, scale):
+        [hidden2_make(m, d_next[m]) for m in both], hidden2_col, branch2_col[0], fc1_z[0]
+    )
+    d_hidden2 = [d.astype(bf16).astype(f32) for d in d_hidden2]
+
+    def norm_back(d_hidden, norm, rstd, scale, between=None):
         d_norm = [d_hidden[m] * (1.0 + scale[m]) for m in both]
         sums = token_sums(d_norm, [d_norm[m] * norm[m] for m in both])
+        if between is not None:
+            sums = between(sums)
         return [rstd[m] * (d_norm[m] - sums[m][0] - norm[m] * sums[m][1]) for m in both]
 
     back2 = norm_back(d_hidden2, norm2, rstd2, [mod[m, 4] for m in both])
@@ -638,87 +697,88 @@
             lax.dynamic_slice(first_full, (m, c * w + g * wide, 3 * w), (1, wide, w))[0],
         )
 
-    attended_col = [
-        col_start([attended_make(m, g, d_branch1[m]) for m in both]) for g in range(groups)
-    ]
-    sent = [state[0] for state in attended_col]
-    d_last = [after(d_branch1[m], *sent) for m in both]
+    attended_col = [col_start([attended_make(m, 0, d_branch1[m]) for m in both])]
+    d_last = [after(d_branch1[m], attended_col[0][0]) for m in both]
     proj_core = [core_start(product_part(attended_rows[m], d_last[m])) for m in both]
 
-    act_last = [after(act_last[m], *sent) for m in both]
-    branch2 = col_end([branch2_make(m, act_last[m]) for m in both], branch2_col, *sent)
-    results = [middle[m] + mod[m, 5] * branch2[m] for m in both]
-    d_gate2 = [jnp.sum(cotangents[m] * branch2[m], axis=0) for m in both]
-    proj_y = y_start(
-        [product_part(attended_rows[m], d_last[m]) for m in both], [s[1] for s in proj_core]
-    )
-
     d_projected, qkv_core, qkv_y = [], [], []
-    later = [proj_y[0], fc2_z[0], *d_gate2]
+    later = [s[0] for s in proj_core]
 
     def qkv_part(g, m):
-        joined = jnp.concatenate(d_projected[g][m], axis=1)
-        return product_part(hidden1_rows[m], joined)
+        return product_part(hidden1_rows[m], d_projected[m][:, 3 * wide * g :][:, : 3 * wide])
+
+    def hidden1_make(m, d):
+        return lambda c: dot(
+            "te,de->td", d, lax.dynamic_slice(first_full, (m, c * w, 0), (1, w, 3 * w))[0]
+        )
 
     for g in range(groups):
         makes = [attended_make(m, g, d_branch1[m]) for m in both]
-        d_attended = [d.astype(bf16) for d in col_end(makes, attended_col[g], *later)]
-        d_attended[1] = padded(d_attended[1])
+        d_attended = [d.astype(bf16) for d in col_end(makes, attended_col[g], *d_projected)]
+        if g + 1 < groups:
+            d_following = [after(d_branch1[m], *d_attended) for m in both]
+            attended_col.append(
+                col_start([attended_make(m, g + 1, d_following[m]) for m in both])
+            )
+            later = [*later, attended_col[g + 1][0]]
+        if pair and g == max(groups - 2, 0):
+            branch2_col = branch2_col[0], swap(after(branch2_col[0], attended_col[-1][0]))
+        d_attended[1] = after(padded(d_attended[1]), *later)
+        if g == 1:
+            d_attended[1], fc2_z[1] = lax.optimization_barrier((d_attended[1], fc2_z[1]))
         if kernels:
+            filled = d_projected
+            if g:
+                filled = [after(a, *later) for a in d_projected]
             outs = attend_back(
-                projected[0], projected[1], real, g * pairs, pairs, *d_attended, lse[g]
+                projected[0], projected[1], real, g, pairs, *d_attended, lse[g], filled
             )
         else:
             outs = plain_attend_back(projected[0], projected[1], real, *d_attended, lse[g])
-        d_projected.append([[outs[2 * j + m] for j in range(3)] for m in both])
+        d_projected = list(outs)
+        done = list(d_projected)
+        later = []
         if g + 1 < groups:
             qkv_core.append([core_start(qkv_part(g, m)) for m in both])
-            later = [qkv_core[g][m][0] for m in both]
-            if g > 0:
-                gots = [after(s[1], *later) for s in qkv_core[g - 1]]
-                qkv_y.append(y_start([qkv_part(g - 1, m) for m in both], gots))
-                later.append(qkv_y[g - 1][0])
-            if g + 2 == groups:
-                fc1_z = z_start([fc1_y], fc2_z, *later)
-                later.append(fc1_z[0])
-
-    d_all = [
-        jnp.concatenate(
-            [d_projected[g][m][j] for j in range(3) for g in range(groups)], axis=1
-        )[: counts[m]]
-        for m in both
-    ]
-
-    def hidden1_make(m, d):
-        return lambda c: dot(
-            "te,de->td", d, lax.dynamic_slice(first_full, (m, c * w, 0), (1, w, 3 * w))[0]
-        )
-
-    hidden1_col = col_start([hidden1_make(m, d_all[m]) for m in both])
+            later += [qkv_core[g][m][0] for m in both]
+        if g == 1:
+            gots = [after(s[1], *done) for s in proj_core + qkv_core[0]]
+            parts = [product_part(attended_rows[m], d_last[m]) for m in both]
+            proj_y = y_start(parts + [qkv_part(0, m) for m in both], gots)
+            qkv_y.append(None)
+            later.append(proj_y[0])
     if groups == 1:
-        fc1_z = z_start([fc1_y], fc2_z)
+        proj_y = y_start(
+            [product_part(attended_rows[m], d_last[m]) for m in both], [s[1] for s in proj_core]
+        )
+
+    got = after(branch2_col[1], *done)
+    d_projected[1], got = lax.optimization_barrier((d_projected[1], got))
+    branch2_col = branch2_col[0], got
+    d_all = [d_projected[m][: counts[m]] for m in both]
+    hidden1_makes = [hidden1_make(m, d_all[m]) for m in both]
+    hidden1_col = col_start(hidden1_makes)
     g = groups - 1
-    d_projected[g] = [
-        [after(d_projected[g][m][0], hidden1_col[0]), *d_projected[g][m][1:]] for m in both
-    ]
+    d_projected = [after(a, hidden1_col[0]) for a in d_projected]
     qkv_core.append([core_start(qkv_part(g, m)) for m in both])
     for g in range(len(qkv_y), groups):
         qkv_y.append(y_start([qkv_part(g, m) for m in both], [s[1] for s in qkv_core[g]]))
-    first_z = z_start([proj_y, *qkv_y[: groups // 2]], fc1_z, hidden1_col[0])
+    act_last = [after(act_last[m], hidden1_col[0]) for m in both]
+    branch2 = col_end([branch2_make(m, act_last[m]) for m in both], branch2_col)
+    results = [middle[m] + mod[m, 5] * branch2[m] for m in both]
+    d_gate2 = [jnp.sum(cotangents[m] * branch2[m], axis=0) for m in both]
 
     d_gate1 = [jnp.sum(d_middle[m] * branch1[m], axis=0) for m in both]
     d_shift2 = [jnp.sum(d_hidden2[m], axis=0) for m in both]
     d_scale2 = [jnp.sum(d_hidden2[m] * norm2[m], axis=0) for m in both]
 
-    d_hidden1 = col_end([hidden1_make(m, d_all[m]) for m in both], hidden1_col)
+    d_hidden1 = col_end(hidden1_makes, hidden1_col)
     d_hidden1 = [d.astype(bf16) for d in d_hidden1]
-    last_z = z_start(qkv_y[groups // 2 :], first_z, *d_hidden1)
+    first_z = z_start([proj_y], None, d_hidden1[1])
+    d_hidden1[0], fc2_summed = lax.optimization_barrier((d_hidden1[0], fc2_z[1]))
     d_hidden1 = [d.astype(f32) for d in d_hidden1]
     d_shift1 = [jnp.sum(d_hidden1[m], axis=0) for m in both]
     d_scale1 = [jnp.sum(d_hidden1[m] * norm1[m], axis=0) for m in both]
-    back1 = norm_back(d_hidden1, norm1, rstd1, [mod[m, 1] for m in both])
-    grad_inputs = [d_middle[m] + back1[m] for m in both]
-
     d_mod = jnp.concatenate(
         [
             part[m].reshape(1, w)
@@ -727,18 +787,33 @@
         ],
         axis=1,
     ).astype(bf16)
+    d_mod, fc1_summed = lax.optimization_barrier((d_mod, fc1_z[1]))
+    last_z = z_start([state for state in qkv_y if state], None, d_mod)
     d_mod_all = lax.all_to_all(jnp.broadcast_to(d_mod, (R, 12 * w)), "row", 0, 0, tiled=True)
-    grad_ada = dot("sd,se->de", silu_rows, d_mod_all)
-    d_silu = dot("se,de->sd", d_mod_all, ada_shard)
-    d_silu = jnp.broadcast_to(d_silu[:, None], (R, C, fan)).reshape(R * C, fan)
-    d_silu = lax.all_to_all(d_silu, ("row", "col"), 0, 0, tiled=True).reshape(C, R // C, C, fan)
-    d_silu = lax.dynamic_index_in_dim(d_silu, me_c, 0, keepdims=False)
-    d_silu = jnp.sum(d_silu, axis=1).reshape(1, w)
+    late = {}
+
+    def conditioning_back(sums):
+        sums, got = lax.optimization_barrier((sums, d_mod_all))
+        late["grad_ada"] = dot("sd,se->de", silu_rows, got)
+        d_silu = dot("se,de->sd", got, ada_shard)
+        late["fc2"] = unmove_units(fc2_summed.astype(f32))
+        late["fc1"] = unmove_columns(fc1_summed.astype(f32)).reshape(fan, 2, units)
+        sums, d_silu = lax.optimization_barrier((sums, d_silu))
+        d_silu = jnp.broadcast_to(d_silu[:, None], (R, C, fan)).reshape(R * C, fan)
+        d_silu = lax.all_to_all(d_silu, ("row", "col"), 0, 0, tiled=True)
+        d_silu = d_silu.reshape(C, R // C, C, fan)
+        d_silu = lax.dynamic_index_in_dim(d_silu, me_c, 0, keepdims=False)
+        late["d_silu"] = jnp.sum(d_silu, axis=1).reshape(1, w)
+        return sums
+
+    back1 = norm_back(
+        d_hidden1, norm1, rstd1, [mod[m, 1] for m in both], conditioning_back
+    )
+    grad_inputs = [d_middle[m] + back1[m] for m in both]
+    grad_ada, grad_fc1, grad_fc2 = late["grad_ada"], late["fc1"], late["fc2"]
     _, pullback = jax.vjp(jax.nn.silu, conditioning)
-    grad_cond = pullback(d_silu)[0]
-
-    grad_fc2 = unmove_units(fc2_z[1].astype(f32))
-    grad_fc1 = unmove_columns(fc1_z[1].astype(f32)).reshape(fan, 2, units)
+    grad_cond = pullback(late["d_silu"])[0]
+
     grad_proj = first_z[1][:, : 2 * w].astype(f32)
     grad_qkv = jnp.concatenate([first_z[1][:, 2 * w :], last_z[1]], axis=1).astype(f32)
     grad_qkv = jnp.concatenate(

time: 891 us -> 837 us (0.939)
  local copies, waits for them, and re-layouts: 142 us -> 98.6 us
  waiting for transfers between devices: 97.9 us -> 138 us
  blocking collectives: 66.4 us -> 42.6 us
  starting transfers between devices: 69 us -> 48.9 us
  other arithmetic: 128 us -> 111 us
  matrix products: 267 us -> 282 us
    ppermute x18 -> x16, waiting for transfers between devices: 67 us -> 114 us  [swap(): return lax.ppermute(a, 'col', XSWAP)]
    all_to_all x1 -> x0, blocking collectives: 30.3 us -> none  [per_device(): lax.all_to_all(dot('sd,de->se', silu_rows, ada_shard), 'row', 0, 0, tiled...]
    squeeze x12 -> x0, local copies, waits for them, and re-layouts: 19.6 us -> none  [y_start(): lax.dynamic_index_in_dim(own, my_y, 1, keepdims=False)]
    dot_general x59 -> x70, matrix products: 267 us -> 282 us  [dot(): return jnp.einsum(spec, a, b, preferred_element_type=f32)]
    ppermute x18 -> x16, starting transfers between devices: 34.5 us -> 19.2 us  [swap(): return lax.ppermute(a, 'col', XSWAP)]
    reduce_scatter x4 -> x2, waiting for transfers between devices: 21.4 us -> 6.34 us  [z_start(): lax.psum_scatter(kept, 'row', scatter_dimension=0, axis_index_groups=ZGRO...]
    dynamic_slice x6 -> x1, local copies, waits for them, and re-layouts: 18.2 us -> 4.12 us  [rows_of(): lax.dynamic_index_in_dim(parts, core, 2, keepdims=False)]
    convert_element_type x7 -> x4, other arithmetic: 18.8 us -> 6.28 us  [the longest x3 4.58 us: z_start(): kept.append((a + got[:, :, at:at + a.shape[2]].astype(f32)).astype(bf16))]
  transfers between devices with their start and end apart: 48 -> 44, of which waited for: 10 -> 16; matrix products, arithmetic and copies ran while one was open for 52% -> 56% of each run, Pallas kernels for 11% -> 11%
where the time goes in v3:
time: 837 us; the launch traced here: 830 us
  matrix products  282 us (34%)
  waiting for transfers between devices  138 us (16%)
  other arithmetic  111 us (13%)
  local copies, waits for them, and re-layouts  98.6 us (12%)
  Pallas kernels  92.2 us (11%)
  starting transfers between devices  48.9 us (6%)
  blocking collectives  42.6 us (5%)
  between operations  17.3 us (2%)
    dot_general x70, matrix products, dot(): return jnp.einsum(spec, a, b, preferred_element_type=f32)  282 us
    ppermute x16, waiting for transfers between devices, swap(): return lax.ppermute(a, 'col', XSWAP)  114 us
    pallas_call x3, Pallas kernels, attend_back(): pl.pallas_call(partial(attend_back_kernel, real, pairs), grid=(pairs,), i...  58.5 us
    psum x3, blocking collectives, sum_col(): return lax.psum(a, 'col')  42.6 us
    unnamed x371, local copies, waits for them, and re-layouts  39.3 us
    pallas_call x3, Pallas kernels, attend(): pl.pallas_call(partial(attend_kernel, real), grid=(pairs,), in_specs=proj...  33.7 us
    ppermute x16, starting transfers between devices, swap(): return lax.ppermute(a, 'col', XSWAP)  19.2 us
  transfers between devices with their start and end apart: 44, of which 16 were waited for; matrix products, arithmetic and copies ran while one was open for 56% of the time, Pallas kernels for 11%

profile of v3, /device:TPU:0, one launch (start us, length us, event | category | flops | bytes accessed | tf_op | source)
XLA Modules:
  0.0 830.4 jit_solution(11312918154047942355)
XLA Ops:
  49.1 9.4 %all-to-all-done.1 = f32[16,1,9216]{2,1,0:T(1,128)} async-done(((f32[16,1,9216]{2,1,0:T(1,128)}), f32[16,1,9216]{2,1,0:T(1,128)}, u32[]{:S(2)}, u32[]{:S(2)}) %all-to-all-start.1) | async-done | bytes 589856 | tf_op jit(solution)/shard_map/all_to_all | solution.py:469
  65.7 13.9 %collective-permute-done.1 = f32[4,768]{1,0:T(4,128)S(1)} collective-permute-done((f32[4,768]{1,0:T(4,128)S(1)}, f32[4,768]{1,0:T(4,128)S(1)}, u32[]{:S(2)}, u32[]{:S(2)}) %collective-permute-start.1) | collective-permute-done | bytes 12320 | tf_op jit(solution)/shard_map/ppermute | solution.py:296
  103.0 36.7 %collective-permute-done.2 = bf16[1178,768]{1,0:T(8,128)(2,1)} collective-permute-done((bf16[1178,768]{1,0:T(8,128)(2,1)S(1)}, bf16[1178,768]{1,0:T(8,128)(2,1)}, u32[]{:S(2)}, u32[]{:S(2)}) %collective-permute-start.2) | collective-permute-done | bytes 1809440 | tf_op jit(solution)/shard_map/ppermute | solution.py:296
  141.4 12.9 %fusion.28.qi.ki.vi = bf16[1024,2304]{1,0:T(8,128)(2,1)} fusion(bf16[1024,1536]{1,0:T(8,128)(2,1)} %fusion.26, bf16[2,1536,3072]{2,1,0:T(8,128)(2,1)} %all-gather.4.cloned.1.call-done), kind=kOutput, calls=%fused_computation.50 | convolution fusion | flops 7250116608 | bytes 14942208 | tf_op jit(solution)/shard_map/td,de->te/dot_general | solution.py:23
  177.0 11.1 %shard_map.177 = (bf16[1024,256]{1,0:T(8,128)(2,1)S(1)}, bf16[256,256]{1,0:T(8,128)(2,1)S(1)}, f32[2,2,1280]{2,1,0:T(2,128)S(1)}) custom-call(bf16[1024,2304]{1,0:T(8,128)(2,1)S(1)} %bitcast.385, bf16[256,2304]{1,0:T(8,128)(2,1)S(1)} %fusion.62.qt.kt.vt, bf16[1024,2304]{1,0:T(8,128)(2,1)S(1)} %bitcast.385, bf16[256,2304]{1,0:T(8,128)(2,1)S(1)} %fusion.62.qt.kt.vt, ...), custom_call_target="tpu_custom_call" | custom-call | flops 6710886400 | bytes 2621440 | tf_op jit(solution)/shard_map/pallas_call | solution.py:144
  190.3 11.1 %shard_map.178 = (bf16[1024,256]{1,0:T(8,128)(2,1)S(1)}, bf16[256,256]{1,0:T(8,128)(2,1)S(1)}, f32[2,2,1280]{2,1,0:T(2,128)S(1)}) custom-call(bf16[1024,2304]{1,0:T(8,128)(2,1)S(1)} %bitcast.385, bf16[256,2304]{1,0:T(8,128)(2,1)S(1)} %fusion.62.qt.kt.vt, bf16[1024,2304]{1,0:T(8,128)(2,1)S(1)} %bitcast.385, bf16[256,2304]{1,0:T(8,128)(2,1)S(1)} %fusion.62.qt.kt.vt, ...), custom_call_target="tpu_custom_call" | custom-call | flops 6710886400 | bytes 2621440 | tf_op jit(solution)/shard_map/pallas_call | solution.py:144
  204.0 11.5 %shard_map.179 = (bf16[1024,256]{1,0:T(8,128)(2,1)S(1)}, bf16[256,256]{1,0:T(8,128)(2,1)S(1)}, f32[2,2,1280]{2,1,0:T(2,128)S(1)}) custom-call(bf16[1024,2304]{1,0:T(8,128)(2,1)S(1)} %bitcast.385, bf16[256,2304]{1,0:T(8,128)(2,1)S(1)} %fusion.62.qt.kt.vt, bf16[1024,2304]{1,0:T(8,128)(2,1)S(1)} %bitcast.385, bf16[256,2304]{1,0:T(8,128)(2,1)S(1)} %fusion.62.qt.kt.vt, ...), custom_call_target="tpu_custom_call" | custom-call | flops 6710886400 | bytes 2621440 | tf_op jit(solution)/shard_map/pallas_call | solution.py:144
  219.6 12.8 %collective-permute-done.5 = bf16[1178,256]{1,0:T(8,128)(2,1)S(1)} collective-permute-done((bf16[1178,256]{1,0:T(8,128)(2,1)S(1)}, bf16[1178,256]{1,0:T(8,128)(2,1)S(1)}, u32[]{:S(2)}, u32[]{:S(2)}) %collective-permute-start.5) | collective-permute-done | bytes 603168 | tf_op jit(solution)/shard_map/ppermute | solution.py:296
  296.1 10.0 %collective-permute-done.6 = bf16[1024,768]{1,0:T(8,128)(2,1)} collective-permute-done((bf16[1024,768]{1,0:T(8,128)(2,1)}, bf16[1024,768]{1,0:T(8,128)(2,1)}, u32[]{:S(2)}, u32[]{:S(2)}) %collective-permute-start.6) | collective-permute-done | bytes 1572896 | tf_op jit(solution)/shard_map/ppermute | solution.py:296
  308.4 17.5 %multiply_convert_fusion = (bf16[1024,3072]{1,0:T(8,128)(2,1)S(1)}, f32[1024,3072]{1,0:T(8,128)}) fusion(bf16[2,1536,3072]{2,1,0:T(8,128)(2,1)} %all-gather.6.cloned.1.call-done, bf16[1024,768]{1,0:T(8,128)(2,1)S(1)} %get-tuple-element.308, bf16[1024,768]{1,0:T(8,128)(2,1)S(1)} %get-tuple-element.307), kind=kOutput, calls=%fused_computation.12 | convolution fusion | flops 9698279424 | bytes 31457280 | tf_op jit(solution)/shard_map/td,df->tf/dot_general | solution.py:23
  361.2 7.7 fusion.69
  373.8 20.4 %fusion.9 = bf16[1024,3072]{1,0:T(8,128)(2,1)} fusion(f32[1024,3072]{1,0:T(8,128)} %get-tuple-element.406, bf16[2,2,3072,768]{3,2,1,0:T(8,128)(2,1)} %bitcast.399, s32[]{:T(128)S(6)} %select_n.403, bf16[128,2,8,768]{3,2,1,0:T(8,128)(2,1)S(1)} %bitcast.422), kind=kOutput, calls=%fused_computation.11 | convolution fusion | flops 9720299520 | bytes 31457284 | tf_op jit(solution)/shard_map/tce,cfe->tf/dot_general | solution.py:23
  394.2 8.9 %fusion.124 = bf16[1024,768]{1,0:T(8,128)(2,1)S(1)} fusion(bf16[1024,3072]{1,0:T(8,128)(2,1)} %fusion.9, bf16[2,1536,3072]{2,1,0:T(8,128)(2,1)} %all-gather.6.cloned.1.call-done, s32[]{:T(128)S(6)} %select_n.404), kind=kOutput, calls=%fused_computation.184 | convolution fusion | flops 4832624640 | bytes 12582916 | tf_op jit(solution)/shard_map/tf,df->td/dot_general | solution.py:23
  421.6 8.9 %fusion.127 = bf16[1024,768]{1,0:T(8,128)(2,1)S(1)} fusion(bf16[1024,3072]{1,0:T(8,128)(2,1)} %copy-done.151, bf16[2,2,3072,768]{3,2,1,0:T(8,128)(2,1)} %bitcast.401, s32[]{:T(128)S(6)} %select_n.392), kind=kOutput, calls=%fused_computation.185 | convolution fusion | flops 4832624640 | bytes 12582916 | tf_op jit(solution)/shard_map/tf,fe->te/dot_general | solution.py:23
  449.2 25.3 %collective-permute-done.12 = bf16[1178,768]{1,0:T(8,128)(2,1)S(1)} collective-permute-done((bf16[1178,768]{1,0:T(8,128)(2,1)S(1)}, bf16[1178,768]{1,0:T(8,128)(2,1)S(1)}, u32[]{:S(2)}, u32[]{:S(2)}) %collective-permute-start.12) | collective-permute-done | bytes 1809440 | tf_op jit(solution)/shard_map/ppermute | solution.py:296
  481.4 11.0 %fusion.94 = (bf16[768]{0:T(1024)(128)(2,1)S(1)}, f32[1024]{0:T(1024)S(1)}, f32[1024]{0:T(1024)S(1)}, bf16[1024,768]{1,0:T(8,128)(2,1)}) fusion(f32[1024,768]{1,0:T(8,128)S(1)} %copy-done.26, f32[1024]{0:T(1024)S(1)} %copy-done.123, f32[1024]{0:T(1024)S(1)} %bitcast.463, f32[768]{0:T(1024)S(1)} %copy-done.121, bf16[1178,768]{1,0:T(8,128)(2,1)S(1)} %copy-done.149, ...), kind=kOutput, calls=%fused_computation.127 | convolution fusion | flops 4841272320 | bytes 17322500 | tf_op jit(solution)/shard_map/tf,df->td/dot_general | solution.py:23
  492.4 8.4 %psum.22 = f32[2,1178]{1,0:T(2,128)S(1)} all-reduce(f32[2,1178]{1,0:T(2,128)S(1)} %maximum_maximum_fusion.2), channel_id=1, replica_groups=mesh['row'=16,'col'=2] {'col'}, use_global_device_ids=true, to_apply=%region_14.15 | all-reduce | flops 2356 | bytes 18848 | tf_op jit(solution)/shard_map/psum | solution.py:329
  534.9 19.4 %shard_map.180 = (bf16[1024,2304]{1,0:T(8,128)(2,1)S(1)}, bf16[256,2304]{1,0:T(8,128)(2,1)S(1)}) custom-call(bf16[1024,2304]{1,0:T(8,128)(2,1)S(1)} %copy-done.5, bf16[256,2304]{1,0:T(8,128)(2,1)S(1)} %copy-done.8, bf16[1024,2304]{1,0:T(8,128)(2,1)S(1)} %copy-done.5, bf16[256,2304]{1,0:T(8,128)(2,1)S(1)} %copy-done.8, bf16[1024,2304]{1,0:T(8,128)(2,1)S(1)} %copy-done.5, ...), custom_call_target="tpu_custom_call" | custom-call | flops 16777216000 | bytes 5242880 | tf_op jit(solution)/shard_map/pallas_call | solution.py:181
  572.2 19.4 %shard_map.181 = (bf16[1024,2304]{1,0:T(8,128)(2,1)S(1)}, bf16[256,2304]{1,0:T(8,128)(2,1)S(1)}) custom-call(bf16[1024,2304]{1,0:T(8,128)(2,1)S(1)} %copy-done.6, bf16[256,2304]{1,0:T(8,128)(2,1)S(1)} %copy-done.8, bf16[1024,2304]{1,0:T(8,128)(2,1)S(1)} %copy-done.6, bf16[256,2304]{1,0:T(8,128)(2,1)S(1)} %copy-done.8, ...), custom_call_target="tpu_custom_call", output_to_operand_aliasing={{0}: (9, {}), {1}: (10, {})} | custom-call | flops 16777216000 | bytes 5242880 | tf_op jit(solution)/shard_map/pallas_call | solution.py:181
  619.9 19.7 %shard_map.182 = (bf16[1024,2304]{1,0:T(8,128)(2,1)S(1)}, bf16[256,2304]{1,0:T(8,128)(2,1)S(1)}) custom-call(bf16[1024,2304]{1,0:T(8,128)(2,1)S(1)} %bitcast.387, bf16[256,2304]{1,0:T(8,128)(2,1)S(1)} %copy-done.8, bf16[1024,2304]{1,0:T(8,128)(2,1)S(1)} %bitcast.387, bf16[256,2304]{1,0:T(8,128)(2,1)S(1)} %copy-done.8, ...), custom_call_target="tpu_custom_call", output_to_operand_aliasing={{0}: (9, {}), {1}: (10, {})} | custom-call | flops 16777216000 | bytes 5242880 | tf_op jit(solution)/shard_map/pallas_call | solution.py:181
  639.6 7.6 fusion.121
  660.8 10.2 %fusion.98 = (bf16[768]{0:T(1024)(128)(2,1)S(1)}, bf16[1024,768]{1,0:T(8,128)(2,1)S(1)}) fusion(bf16[1178,768]{1,0:T(8,128)(2,1)} %collective-permute-done.22, bf16[512,768]{1,0:T(8,128)(2,1)S(1)} %copy-done.40, bf16[512,768]{1,0:T(8,128)(2,1)S(1)} %copy-done.37, f32[1024,768]{1,0:T(8,128)S(1)} %copy-done.27, f32[768]{0:T(1024)S(1)} %copy-done.135, ...), kind=kOutput, calls=%fused_computation.131 | convolution fusion | flops 4840487936 | bytes 18878980 | tf_op jit(solution)/shard_map/tf,fe->te/dot_general | solution.py:23
  701.5 7.9 add_convert_fusion.5
  716.4 27.1 %psum.23 = f32[2,1178]{1,0:T(2,128)S(1)} all-reduce(f32[2,1178]{1,0:T(2,128)S(1)} %maximum_maximum_fusion.3), channel_id=1, replica_groups=mesh['row'=16,'col'=2] {'col'}, use_global_device_ids=true, to_apply=%region_20.21 | all-reduce | flops 2356 | bytes 18848 | tf_op jit(solution)/shard_map/psum | solution.py:329
  (693 shorter events, 464.5 us)
Async XLA Ops:
  7.2 134.2 %all-gather.4.cloned.1.call-start = ((), (), s32[]{:S(2)}) async-start(), calls=%async_computation.8 | async-start | bytes 20054016 | tf_op jit(solution)/shard_map/all_gather | solution.py:435
  33.4 251.7 %all-gather.6.cloned.1.call-start = ((), (), s32[]{:S(2)}) async-start(), calls=%async_computation.9 | async-start | bytes 20054016 | tf_op jit(solution)/shard_map/all_gather | solution.py:435
  36.7 43.1 %collective-permute-start = (bf16[589,1,1536]{2,0,1:T(8,128)(2,1)}, bf16[589,1,1536]{2,0,1:T(8,128)(2,1)}, u32[]{:S(2)}, u32[]{:S(2)}) collective-permute-start(bf16[589,1,1536]{2,0,1:T(8,128)(2,1)} %pad_maximum_fusion.8), channel_id=1, source_target_pairs={{0,1},{1,0},{2,3},{3,2},{4,5},{5,4},{6,7},{7,6},{8,9},{9,8},{10,11... | collective-permute-start | bytes 5428232 | tf_op jit(solution)/shard_map/ppermute | solution.py:296
  93.2 268.1 %all-gather.8.cloned.1.call-start = ((), (), s32[]{:S(2)}) async-start(), calls=%async_computation.10 | async-start | bytes 20054016 | tf_op jit(solution)/shard_map/all_gather | solution.py:435
  98.5 41.2 %collective-permute-start.2 = (bf16[1178,768]{1,0:T(8,128)(2,1)S(1)}, bf16[1178,768]{1,0:T(8,128)(2,1)}, u32[]{:S(2)}, u32[]{:S(2)}) collective-permute-start(bf16[1178,768]{1,0:T(8,128)(2,1)S(1)} %pad_maximum_fusion.9), channel_id=1, source_target_pairs={{0,1},{1,0},{2,3},{3,2},{4,5},{5,4},{6,7},{7,6},{8,9},{9,8},{10,11... | collective-permute-start | bytes 5428232 | tf_op jit(solution)/shard_map/ppermute | solution.py:296
  162.4 405.0 %reduce-scatter.5.cloned.1.call-start = ((), (), s32[]{:S(2)}) async-start(), calls=%async_computation.11 | async-start | bytes 10616832 | tf_op jit(solution)/shard_map/reduce_scatter | solution.py:375
  296.1 49.2 %collective-permute-start.10 = (bf16[3072,768]{1,0:T(8,128)(2,1)}, bf16[3072,768]{1,0:T(8,128)(2,1)}, u32[]{:S(2)}, u32[]{:S(2)}) collective-permute-start(bf16[3072,768]{1,0:T(8,128)(2,1)} %convolution_convert_fusion.3), channel_id=1, source_target_pairs={{0,2},{2,0},{4,6},{6,4},{8,10},{10,8},{12,14},{14,12},{16,18},{18,... | collective-permute-start | bytes 14155784 | tf_op jit(solution)/shard_map/ppermute | solution.py:333
  361.1 382.5 %reduce-scatter.7.cloned.1.call-start = ((), (), s32[]{:S(2)}) async-start(), calls=%async_computation.12 | async-start | bytes 10616832 | tf_op jit(solution)/shard_map/reduce_scatter | solution.py:375
  432.6 41.9 %collective-permute-start.12 = (bf16[1178,768]{1,0:T(8,128)(2,1)S(1)}, bf16[1178,768]{1,0:T(8,128)(2,1)S(1)}, u32[]{:S(2)}, u32[]{:S(2)}) collective-permute-start(bf16[1178,768]{1,0:T(8,128)(2,1)S(1)} %copy-done.69), channel_id=1, source_target_pairs={{0,1},{1,0},{2,3},{3,2},{4,5},{5,4},{6,7},{7,6},{8,9},{9,8},{10,11... | collective-permute-start | bytes 5428232 | tf_op jit(solution)/shard_map/ppermute | solution.py:296
  517.2 74.4 %collective-permute-start.18 = (bf16[768,768]{1,0:T(8,128)(2,1)}, bf16[768,768]{1,0:T(8,128)(2,1)}, u32[]{:S(2)}, u32[]{:S(2)}) collective-permute-start(bf16[768,768]{1,0:T(8,128)(2,1)} %convolution_convert_fusion.9), channel_id=1, source_target_pairs={{0,2},{2,0},{4,6},{6,4},{8,10},{10,8},{12,14},{14,12},{16,18},{18,... | collective-permute-start | bytes 3538952 | tf_op jit(solution)/shard_map/ppermute | solution.py:333
  518.7 72.9 %collective-permute-start.19 = (bf16[768,768]{1,0:T(8,128)(2,1)}, bf16[768,768]{1,0:T(8,128)(2,1)}, u32[]{:S(2)}, u32[]{:S(2)}) collective-permute-start(bf16[768,768]{1,0:T(8,128)(2,1)} %convolution_convert_fusion.8), channel_id=1, source_target_pairs={{0,2},{2,0},{4,6},{6,4},{8,10},{10,8},{12,14},{14,12},{16,18},{18,... | collective-permute-start | bytes 3538952 | tf_op jit(solution)/shard_map/ppermute | solution.py:333
  519.2 250.0 %reduce-scatter.9.cloned.1.call-start = ((), (), s32[]{:S(2)}) async-start(), calls=%async_computation.13 | async-start | bytes 2949120 | tf_op jit(solution)/shard_map/reduce_scatter | solution.py:366
  556.8 48.0 %collective-permute-start.20 = (bf16[768,768]{1,0:T(8,128)(2,1)}, bf16[768,768]{1,0:T(8,128)(2,1)}, u32[]{:S(2)}, u32[]{:S(2)}) collective-permute-start(bf16[768,768]{1,0:T(8,128)(2,1)} %fusion.139), channel_id=1, source_target_pairs={{0,2},{2,0},{4,6},{6,4},{8,10},{10,8},{12,14},{14,12},{16,18},{18,... | collective-permute-start | bytes 3538952 | tf_op jit(solution)/shard_map/ppermute | solution.py:333
  558.4 46.4 %collective-permute-start.21 = (bf16[768,768]{1,0:T(8,128)(2,1)}, bf16[768,768]{1,0:T(8,128)(2,1)}, u32[]{:S(2)}, u32[]{:S(2)}) collective-permute-start(bf16[768,768]{1,0:T(8,128)(2,1)} %convolution_convert_fusion.7), channel_id=1, source_target_pairs={{0,2},{2,0},{4,6},{6,4},{8,10},{10,8},{12,14},{14,12},{16,18},{18,... | collective-permute-start | bytes 3538952 | tf_op jit(solution)/shard_map/ppermute | solution.py:333
  565.6 48.8 %collective-permute-start.17 = (bf16[1178,256]{1,0:T(8,128)(2,1)}, bf16[1178,256]{1,0:T(8,128)(2,1)}, u32[]{:S(2)}, u32[]{:S(2)}) collective-permute-start(bf16[1178,256]{1,0:T(8,128)(2,1)} %pad_maximum_fusion.30), channel_id=1, source_target_pairs={{0,1},{1,0},{2,3},{3,2},{4,5},{5,4},{6,7},{7,6},{8,9},{9,8},{10,11... | collective-permute-start | bytes 1809416 | tf_op jit(solution)/shard_map/ppermute | solution.py:296
  591.6 55.6 %collective-permute-start.22 = (bf16[1178,768]{1,0:T(8,128)(2,1)S(1)}, bf16[1178,768]{1,0:T(8,128)(2,1)}, u32[]{:S(2)}, u32[]{:S(2)}) collective-permute-start(bf16[1178,768]{1,0:T(8,128)(2,1)S(1)} %copy-done.68), channel_id=1, source_target_pairs={{0,1},{1,0},{2,3},{3,2},{4,5},{5,4},{6,7},{7,6},{8,9},{9,8},{10,11... | collective-permute-start | bytes 5428232 | tf_op jit(solution)/shard_map/ppermute | solution.py:296
  593.7 58.3 %collective-permute-start.26 = (bf16[768,768]{1,0:T(8,128)(2,1)}, bf16[768,768]{1,0:T(8,128)(2,1)}, u32[]{:S(2)}, u32[]{:S(2)}) collective-permute-start(bf16[768,768]{1,0:T(8,128)(2,1)} %convolution_convert_fusion.6), channel_id=1, source_target_pairs={{0,2},{2,0},{4,6},{6,4},{8,10},{10,8},{12,14},{14,12},{16,18},{18,... | collective-permute-start | bytes 3538952 | tf_op jit(solution)/shard_map/ppermute | solution.py:333
  604.7 48.7 %collective-permute-start.25 = (bf16[768,768]{1,0:T(8,128)(2,1)}, bf16[768,768]{1,0:T(8,128)(2,1)}, u32[]{:S(2)}, u32[]{:S(2)}) collective-permute-start(bf16[768,768]{1,0:T(8,128)(2,1)} %fusion.142), channel_id=1, source_target_pairs={{0,2},{2,0},{4,6},{6,4},{8,10},{10,8},{12,14},{14,12},{16,18},{18,... | collective-permute-start | bytes 3538952 | tf_op jit(solution)/shard_map/ppermute | solution.py:333
  608.3 88.2 %collective-permute-start.24 = (bf16[4,96,3072]{2,1,0:T(8,128)(2,1)S(1)}, bf16[4,96,3072]{2,1,0:T(8,128)(2,1)S(1)}, u32[]{:S(2)}, u32[]{:S(2)}) collective-permute-start(bf16[4,96,3072]{2,1,0:T(8,128)(2,1)S(1)} %pad_maximum_fusion.4), channel_id=1, source_target_pairs={{0,4},{2,6},{4,0},{6,2},{8,12},{10,14},{12,8},{14,10},{16,20},{18,... | collective-permute-start | bytes 7077896 | tf_op jit(solution)/shard_map/ppermute | solution.py:343
  650.7 42.1 %collective-permute-start.23 = (bf16[1178,768]{1,0:T(8,128)(2,1)S(1)}, bf16[1178,768]{1,0:T(8,128)(2,1)}, u32[]{:S(2)}, u32[]{:S(2)}) collective-permute-start(bf16[1178,768]{1,0:T(8,128)(2,1)S(1)} %pad_maximum_fusion.12), channel_id=1, source_target_pairs={{0,1},{1,0},{2,3},{3,2},{4,5},{5,4},{6,7},{7,6},{8,9},{9,8},{10,11... | collective-permute-start | bytes 5428232 | tf_op jit(solution)/shard_map/ppermute | solution.py:296
  656.5 87.2 %collective-permute-start.27 = (bf16[4,96,1536]{2,1,0:T(8,128)(2,1)}, bf16[4,96,1536]{2,1,0:T(8,128)(2,1)}, u32[]{:S(2)}, u32[]{:S(2)}) collective-permute-start(bf16[4,96,1536]{2,1,0:T(8,128)(2,1)} %pad_maximum_fusion.23), channel_id=1, source_target_pairs={{0,4},{2,6},{4,0},{6,2},{8,12},{10,14},{12,8},{14,10},{16,20},{18,... | collective-permute-start | bytes 3538952 | tf_op jit(solution)/shard_map/ppermute | solution.py:343
  688.1 59.9 %collective-permute-start.30 = (bf16[4,96,1536]{2,1,0:T(8,128)(2,1)}, bf16[4,96,1536]{2,1,0:T(8,128)(2,1)}, u32[]{:S(2)}, u32[]{:S(2)}) collective-permute-start(bf16[4,96,1536]{2,1,0:T(8,128)(2,1)} %pad_maximum_fusion.24), channel_id=1, source_target_pairs={{0,4},{2,6},{4,0},{6,2},{8,12},{10,14},{12,8},{14,10},{16,20},{18,... | collective-permute-start | bytes 3538952 | tf_op jit(solution)/shard_map/ppermute | solution.py:343
  698.9 120.5 %reduce-scatter.11.cloned.1.call-start = ((), (), s32[]{:S(2)}) async-start(), calls=%async_computation.14 | async-start | bytes 2949120 | tf_op jit(solution)/shard_map/reduce_scatter | solution.py:366
  711.1 43.0 %collective-permute-start.32 = (f32[384,1536]{1,0:T(8,128)}, f32[384,1536]{1,0:T(8,128)}, u32[]{:S(2)}, u32[]{:S(2)}) collective-permute-start(f32[384,1536]{1,0:T(8,128)} %convert_element_type.605), channel_id=1, source_target_pairs={{1,2},{2,1},{5,6},{6,5},{9,10},{10,9},{13,14},{14,13},{17,18},{18,... | collective-permute-start | bytes 7077896 | tf_op jit(solution)/shard_map/ppermute | solution.py:501
  (181 other events, 3012.5 us)
Sparse Core Ops, SparseCore 0:
  10.9 111.3 all-gather.3
  124.4 101.2 all-gather.5
  227.3 98.9 all-gather.7
  361.3 164.6 reduce-scatter.4
  529.4 190.8 reduce-scatter.6
  723.0 46.2 reduce-scatter.8
  771.6 47.7 reduce-scatter.10

commit v4 on v3

--- a/solution.py
+++ b/solution.py
@@ -667,15 +667,13 @@
             "tf,fe->te", act, lax.dynamic_slice(fc2_full, (m, c, 0, 0), (1, 1, units, w))[0, 0]
         )
 
-    act_last = [after(activated[m], *fc1_sent) for m in both]
-    branch2_col = col_start([branch2_make(m, act_last[m]) for m in both], wait=True)
-    d_next = [after(d_next[m], branch2_col[0]) for m in both]
+    d_next = [after(d_next[m], *fc1_sent) for m in both]
     fc1_z = both_start(
         [product_part(hidden2_rows[m], d_next[m])[1][0][0] for m in both],
         [s[1] for s in fc1_core],
     )
     d_hidden2 = col_end(
-        [hidden2_make(m, d_next[m]) for m in both], hidden2_col, branch2_col[0], fc1_z[0]
+        [hidden2_make(m, d_next[m]) for m in both], hidden2_col, fc1_z[0]
     )
     d_hidden2 = [d.astype(bf16).astype(f32) for d in d_hidden2]
 
@@ -698,11 +696,13 @@
         )
 
     attended_col = [col_start([attended_make(m, 0, d_branch1[m]) for m in both])]
+    act_last = [after(activated[m], attended_col[0][0]) for m in both]
+    branch2_col = col_start([branch2_make(m, act_last[m]) for m in both], wait=True)
     d_last = [after(d_branch1[m], attended_col[0][0]) for m in both]
     proj_core = [core_start(product_part(attended_rows[m], d_last[m])) for m in both]
 
     d_projected, qkv_core, qkv_y = [], [], []
-    later = [s[0] for s in proj_core]
+    later = [s[0] for s in proj_core] + [branch2_col[0]]
 
     def qkv_part(g, m):
         return product_part(hidden1_rows[m], d_projected[m][:, 3 * wide * g :][:, : 3 * wide])

time: 837 us -> 844 us (level)
    reduce_scatter x2, waiting for transfers between devices: 6.34 us -> 18 us  [z_start(): lax.psum_scatter(kept, 'row', scatter_dimension=0, axis_index_groups=ZGRO...]
    unnamed x371 -> x363, local copies, waits for them, and re-layouts: 39.3 us -> 34.6 us
  transfers between devices with their start and end apart: 44 -> 44, of which waited for: 16 -> 15; matrix products, arithmetic and copies ran while one was open for 56% -> 55% of each run, Pallas kernels for 11% -> 11%
where the time goes in v4:
time: 844 us; the launch traced here: 837 us
  matrix products  283 us (34%)
  waiting for transfers between devices  144 us (17%)
  other arithmetic  113 us (13%)
  local copies, waits for them, and re-layouts  93.8 us (11%)
  Pallas kernels  92.6 us (11%)
  starting transfers between devices  51.3 us (6%)
  blocking collectives  42 us (5%)
  between operations  17.3 us (2%)
    dot_general x70, matrix products, dot(): return jnp.einsum(spec, a, b, preferred_element_type=f32)  283 us
    ppermute x16, waiting for transfers between devices, swap(): return lax.ppermute(a, 'col', XSWAP)  106 us
    pallas_call x3, Pallas kernels, attend_back(): pl.pallas_call(partial(attend_back_kernel, real, pairs), grid=(pairs,), i...  58.9 us
    psum x3, blocking collectives, sum_col(): return lax.psum(a, 'col')  42 us
    unnamed x363, local copies, waits for them, and re-layouts  34.6 us
    pallas_call x3, Pallas kernels, attend(): pl.pallas_call(partial(attend_kernel, real), grid=(pairs,), in_specs=proj...  33.7 us
    ppermute x16, starting transfers between devices, swap(): return lax.ppermute(a, 'col', XSWAP)  18.3 us
    reduce_scatter x2, waiting for transfers between devices, z_start(): lax.psum_scatter(kept, 'row', scatter_dimension=0, axis_index_groups=ZGRO...  18 us
  transfers between devices with their start and end apart: 44, of which 15 were waited for; matrix products, arithmetic and copies ran while one was open for 55% of the time, Pallas kernels for 11%

profile of v4, /device:TPU:0, one launch (start us, length us, event | category | flops | bytes accessed | tf_op | source)
XLA Modules:
  0.0 836.7 jit_solution(15346271641211838901)
XLA Ops:
  49.1 9.4 %all-to-all-done.1 = f32[16,1,9216]{2,1,0:T(1,128)} async-done(((f32[16,1,9216]{2,1,0:T(1,128)}), f32[16,1,9216]{2,1,0:T(1,128)}, u32[]{:S(2)}, u32[]{:S(2)}) %all-to-all-start.1) | async-done | bytes 589856 | tf_op jit(solution)/shard_map/all_to_all | solution.py:469
  65.7 13.9 %collective-permute-done.1 = f32[4,768]{1,0:T(4,128)S(1)} collective-permute-done((f32[4,768]{1,0:T(4,128)S(1)}, f32[4,768]{1,0:T(4,128)S(1)}, u32[]{:S(2)}, u32[]{:S(2)}) %collective-permute-start.1) | collective-permute-done | bytes 12320 | tf_op jit(solution)/shard_map/ppermute | solution.py:296
  102.9 36.7 %collective-permute-done.2 = bf16[1178,768]{1,0:T(8,128)(2,1)} collective-permute-done((bf16[1178,768]{1,0:T(8,128)(2,1)S(1)}, bf16[1178,768]{1,0:T(8,128)(2,1)}, u32[]{:S(2)}, u32[]{:S(2)}) %collective-permute-start.2) | collective-permute-done | bytes 1809440 | tf_op jit(solution)/shard_map/ppermute | solution.py:296
  141.3 12.9 %fusion.28.qi.ki.vi = bf16[1024,2304]{1,0:T(8,128)(2,1)} fusion(bf16[1024,1536]{1,0:T(8,128)(2,1)} %fusion.26, bf16[2,1536,3072]{2,1,0:T(8,128)(2,1)} %all-gather.4.cloned.1.call-done), kind=kOutput, calls=%fused_computation.50 | convolution fusion | flops 7250116608 | bytes 14942208 | tf_op jit(solution)/shard_map/td,de->te/dot_general | solution.py:23
  177.1 11.1 %shard_map.177 = (bf16[1024,256]{1,0:T(8,128)(2,1)S(1)}, bf16[256,256]{1,0:T(8,128)(2,1)S(1)}, f32[2,2,1280]{2,1,0:T(2,128)S(1)}) custom-call(bf16[1024,2304]{1,0:T(8,128)(2,1)S(1)} %bitcast.385, bf16[256,2304]{1,0:T(8,128)(2,1)S(1)} %fusion.62.qt.kt.vt, bf16[1024,2304]{1,0:T(8,128)(2,1)S(1)} %bitcast.385, bf16[256,2304]{1,0:T(8,128)(2,1)S(1)} %fusion.62.qt.kt.vt, ...), custom_call_target="tpu_custom_call" | custom-call | flops 6710886400 | bytes 2621440 | tf_op jit(solution)/shard_map/pallas_call | solution.py:144
  190.1 11.1 %shard_map.178 = (bf16[1024,256]{1,0:T(8,128)(2,1)S(1)}, bf16[256,256]{1,0:T(8,128)(2,1)S(1)}, f32[2,2,1280]{2,1,0:T(2,128)S(1)}) custom-call(bf16[1024,2304]{1,0:T(8,128)(2,1)S(1)} %bitcast.385, bf16[256,2304]{1,0:T(8,128)(2,1)S(1)} %fusion.62.qt.kt.vt, bf16[1024,2304]{1,0:T(8,128)(2,1)S(1)} %bitcast.385, bf16[256,2304]{1,0:T(8,128)(2,1)S(1)} %fusion.62.qt.kt.vt, ...), custom_call_target="tpu_custom_call" | custom-call | flops 6710886400 | bytes 2621440 | tf_op jit(solution)/shard_map/pallas_call | solution.py:144
  204.1 11.5 %shard_map.179 = (bf16[1024,256]{1,0:T(8,128)(2,1)S(1)}, bf16[256,256]{1,0:T(8,128)(2,1)S(1)}, f32[2,2,1280]{2,1,0:T(2,128)S(1)}) custom-call(bf16[1024,2304]{1,0:T(8,128)(2,1)S(1)} %bitcast.385, bf16[256,2304]{1,0:T(8,128)(2,1)S(1)} %fusion.62.qt.kt.vt, bf16[1024,2304]{1,0:T(8,128)(2,1)S(1)} %bitcast.385, bf16[256,2304]{1,0:T(8,128)(2,1)S(1)} %fusion.62.qt.kt.vt, ...), custom_call_target="tpu_custom_call" | custom-call | flops 6710886400 | bytes 2621440 | tf_op jit(solution)/shard_map/pallas_call | solution.py:144
  219.5 12.8 %collective-permute-done.5 = bf16[1178,256]{1,0:T(8,128)(2,1)S(1)} collective-permute-done((bf16[1178,256]{1,0:T(8,128)(2,1)S(1)}, bf16[1178,256]{1,0:T(8,128)(2,1)S(1)}, u32[]{:S(2)}, u32[]{:S(2)}) %collective-permute-start.5) | collective-permute-done | bytes 603168 | tf_op jit(solution)/shard_map/ppermute | solution.py:296
  296.3 10.2 %collective-permute-done.6 = bf16[1024,768]{1,0:T(8,128)(2,1)} collective-permute-done((bf16[1024,768]{1,0:T(8,128)(2,1)}, bf16[1024,768]{1,0:T(8,128)(2,1)}, u32[]{:S(2)}, u32[]{:S(2)}) %collective-permute-start.6) | collective-permute-done | bytes 1572896 | tf_op jit(solution)/shard_map/ppermute | solution.py:296
  308.7 17.3 %multiply_convert_fusion = (bf16[1024,3072]{1,0:T(8,128)(2,1)S(1)}, f32[1024,3072]{1,0:T(8,128)}) fusion(bf16[2,1536,3072]{2,1,0:T(8,128)(2,1)} %all-gather.6.cloned.1.call-done, bf16[1024,768]{1,0:T(8,128)(2,1)S(1)} %get-tuple-element.308, bf16[1024,768]{1,0:T(8,128)(2,1)S(1)} %get-tuple-element.307), kind=kOutput, calls=%fused_computation.12 | convolution fusion | flops 9698279424 | bytes 31457280 | tf_op jit(solution)/shard_map/td,df->tf/dot_general | solution.py:23
  361.3 22.5 %fusion.9 = bf16[1024,3072]{1,0:T(8,128)(2,1)} fusion(f32[1024,3072]{1,0:T(8,128)} %get-tuple-element.406, bf16[2,2,3072,768]{3,2,1,0:T(8,128)(2,1)} %bitcast.400, s32[]{:T(128)S(6)} %select_n.403, bf16[128,2,8,768]{3,2,1,0:T(8,128)(2,1)} %bitcast.424), kind=kOutput, calls=%fused_computation.11 | convolution fusion | flops 9720299520 | bytes 31457284 | tf_op jit(solution)/shard_map/tce,cfe->tf/dot_general | solution.py:23
  420.3 8.4 add_convert_fusion.1
  436.5 24.0 %collective-permute-done.12 = bf16[1178,768]{1,0:T(8,128)(2,1)} collective-permute-done((bf16[1178,768]{1,0:T(8,128)(2,1)}, bf16[1178,768]{1,0:T(8,128)(2,1)}, u32[]{:S(2)}, u32[]{:S(2)}) %collective-permute-start.12) | collective-permute-done | bytes 1809440 | tf_op jit(solution)/shard_map/ppermute | solution.py:296
  466.3 11.0 %fusion.94 = (bf16[768]{0:T(1024)(128)(2,1)}, f32[1024]{0:T(1024)S(1)}, f32[1024]{0:T(1024)S(1)}, bf16[1024,768]{1,0:T(8,128)(2,1)}) fusion(f32[1024,768]{1,0:T(8,128)S(1)} %copy-done.25, f32[1024]{0:T(1024)S(1)} %copy-done.117, f32[1024]{0:T(1024)S(1)} %bitcast.465, f32[768]{0:T(1024)S(1)} %copy-done.115, bf16[1178,768]{1,0:T(8,128)(2,1)} %collective-permute-done.12, ...), kind=kOutput, calls=%fused_computation.127 | convolution fusion | flops 4841272320 | bytes 17322500 | tf_op jit(solution)/shard_map/tf,df->td/dot_general | solution.py:23
  477.3 8.0 psum.22
  503.3 8.6 %fusion.127 = bf16[1024,768]{1,0:T(8,128)(2,1)S(1)} fusion(bf16[1024,3072]{1,0:T(8,128)(2,1)} %copy-done.147, bf16[2,2,3072,768]{3,2,1,0:T(8,128)(2,1)} %bitcast.402, s32[]{:T(128)S(6)} %select_n.392), kind=kOutput, calls=%fused_computation.185 | convolution fusion | flops 4832624640 | bytes 12582916 | tf_op jit(solution)/shard_map/tf,fe->te/dot_general | solution.py:23
  526.6 19.8 %shard_map.180 = (bf16[1024,2304]{1,0:T(8,128)(2,1)S(1)}, bf16[256,2304]{1,0:T(8,128)(2,1)S(1)}) custom-call(bf16[1024,2304]{1,0:T(8,128)(2,1)S(1)} %bitcast.387, bf16[256,2304]{1,0:T(8,128)(2,1)S(1)} %copy-done.7, bf16[1024,2304]{1,0:T(8,128)(2,1)S(1)} %bitcast.387, bf16[256,2304]{1,0:T(8,128)(2,1)S(1)} %copy-done.7, bf16[1024,2304]{1,0:T(8,128)(2,1)S(1)} %bitcast.387, ...), custom_call_target="tpu_custom_call" | custom-call | flops 16777216000 | bytes 5242880 | tf_op jit(solution)/shard_map/pallas_call | solution.py:181
  563.2 19.4 %shard_map.181 = (bf16[1024,2304]{1,0:T(8,128)(2,1)S(1)}, bf16[256,2304]{1,0:T(8,128)(2,1)S(1)}) custom-call(bf16[1024,2304]{1,0:T(8,128)(2,1)S(1)} %copy-done.5, bf16[256,2304]{1,0:T(8,128)(2,1)S(1)} %copy-done.7, bf16[1024,2304]{1,0:T(8,128)(2,1)S(1)} %copy-done.5, bf16[256,2304]{1,0:T(8,128)(2,1)S(1)} %copy-done.7, ...), custom_call_target="tpu_custom_call", output_to_operand_aliasing={{0}: (9, {}), {1}: (10, {})} | custom-call | flops 16777216000 | bytes 5242880 | tf_op jit(solution)/shard_map/pallas_call | solution.py:181
  611.5 19.7 %shard_map.182 = (bf16[1024,2304]{1,0:T(8,128)(2,1)S(1)}, bf16[256,2304]{1,0:T(8,128)(2,1)S(1)}) custom-call(bf16[1024,2304]{1,0:T(8,128)(2,1)S(1)} %bitcast.389, bf16[256,2304]{1,0:T(8,128)(2,1)S(1)} %copy-done.7, bf16[1024,2304]{1,0:T(8,128)(2,1)S(1)} %bitcast.389, bf16[256,2304]{1,0:T(8,128)(2,1)S(1)} %copy-done.7, ...), custom_call_target="tpu_custom_call", output_to_operand_aliasing={{0}: (9, {}), {1}: (10, {})} | custom-call | flops 16777216000 | bytes 5242880 | tf_op jit(solution)/shard_map/pallas_call | solution.py:181
  631.3 7.6 fusion.121
  652.1 10.1 %fusion.98 = (bf16[768]{0:T(1024)(128)(2,1)S(1)}, bf16[1024,768]{1,0:T(8,128)(2,1)S(1)}) fusion(bf16[1178,768]{1,0:T(8,128)(2,1)} %collective-permute-done.22, bf16[512,768]{1,0:T(8,128)(2,1)S(1)} %copy-done.39, bf16[512,768]{1,0:T(8,128)(2,1)S(1)} %copy-done.37, f32[1024,768]{1,0:T(8,128)S(1)} %copy-done.27, f32[768]{0:T(1024)S(1)} %copy-done.129, ...), kind=kOutput, calls=%fused_computation.131 | convolution fusion | flops 4840487936 | bytes 18878980 | tf_op jit(solution)/shard_map/tf,fe->te/dot_general | solution.py:23
  692.7 7.8 add_convert_fusion.5
  707.6 26.9 %psum.23 = f32[2,1178]{1,0:T(2,128)S(1)} all-reduce(f32[2,1178]{1,0:T(2,128)S(1)} %maximum_maximum_fusion.3), channel_id=1, replica_groups=mesh['row'=16,'col'=2] {'col'}, use_global_device_ids=true, to_apply=%region_20.21 | all-reduce | flops 2356 | bytes 18848 | tf_op jit(solution)/shard_map/psum | solution.py:329
  762.6 12.2 %reduce-scatter.9.cloned.1.call-done = bf16[1,96,3072]{2,1,0:T(8,128)(2,1)} async-done(((bf16[4,96,3072]{2,1,0:T(8,128)(2,1)}), bf16[1,96,3072]{2,1,0:T(8,128)(2,1)}) %reduce-scatter.9.cloned.1.call-update) | async-done | bytes 589840 | tf_op jit(solution)/shard_map/reduce_scatter | solution.py:366
  (685 shorter events, 466.4 us)
Async XLA Ops:
  7.2 134.1 %all-gather.4.cloned.1.call-start = ((), (), s32[]{:S(2)}) async-start(), calls=%async_computation.8 | async-start | bytes 20054016 | tf_op jit(solution)/shard_map/all_gather | solution.py:435
  33.4 251.9 %all-gather.6.cloned.1.call-start = ((), (), s32[]{:S(2)}) async-start(), calls=%async_computation.9 | async-start | bytes 20054016 | tf_op jit(solution)/shard_map/all_gather | solution.py:435
  36.6 43.1 %collective-permute-start = (bf16[589,1,1536]{2,0,1:T(8,128)(2,1)}, bf16[589,1,1536]{2,0,1:T(8,128)(2,1)}, u32[]{:S(2)}, u32[]{:S(2)}) collective-permute-start(bf16[589,1,1536]{2,0,1:T(8,128)(2,1)} %pad_maximum_fusion.8), channel_id=1, source_target_pairs={{0,1},{1,0},{2,3},{3,2},{4,5},{5,4},{6,7},{7,6},{8,9},{9,8},{10,11... | collective-permute-start | bytes 5428232 | tf_op jit(solution)/shard_map/ppermute | solution.py:296
  93.1 268.2 %all-gather.8.cloned.1.call-start = ((), (), s32[]{:S(2)}) async-start(), calls=%async_computation.10 | async-start | bytes 20054016 | tf_op jit(solution)/shard_map/all_gather | solution.py:435
  98.4 41.2 %collective-permute-start.2 = (bf16[1178,768]{1,0:T(8,128)(2,1)S(1)}, bf16[1178,768]{1,0:T(8,128)(2,1)}, u32[]{:S(2)}, u32[]{:S(2)}) collective-permute-start(bf16[1178,768]{1,0:T(8,128)(2,1)S(1)} %pad_maximum_fusion.9), channel_id=1, source_target_pairs={{0,1},{1,0},{2,3},{3,2},{4,5},{5,4},{6,7},{7,6},{8,9},{9,8},{10,11... | collective-permute-start | bytes 5428232 | tf_op jit(solution)/shard_map/ppermute | solution.py:296
  162.3 396.0 %reduce-scatter.5.cloned.1.call-start = ((), (), s32[]{:S(2)}) async-start(), calls=%async_computation.11 | async-start | bytes 10616832 | tf_op jit(solution)/shard_map/reduce_scatter | solution.py:375
  296.3 49.1 %collective-permute-start.10 = (bf16[3072,768]{1,0:T(8,128)(2,1)}, bf16[3072,768]{1,0:T(8,128)(2,1)}, u32[]{:S(2)}, u32[]{:S(2)}) collective-permute-start(bf16[3072,768]{1,0:T(8,128)(2,1)} %convolution_convert_fusion.3), channel_id=1, source_target_pairs={{0,2},{2,0},{4,6},{6,4},{8,10},{10,8},{12,14},{14,12},{16,18},{18,... | collective-permute-start | bytes 14155784 | tf_op jit(solution)/shard_map/ppermute | solution.py:333
  361.2 373.4 %reduce-scatter.7.cloned.1.call-start = ((), (), s32[]{:S(2)}) async-start(), calls=%async_computation.12 | async-start | bytes 10616832 | tf_op jit(solution)/shard_map/reduce_scatter | solution.py:375
  418.1 42.4 %collective-permute-start.12 = (bf16[1178,768]{1,0:T(8,128)(2,1)}, bf16[1178,768]{1,0:T(8,128)(2,1)}, u32[]{:S(2)}, u32[]{:S(2)}) collective-permute-start(bf16[1178,768]{1,0:T(8,128)(2,1)} %pad_maximum_fusion.10), channel_id=1, source_target_pairs={{0,1},{1,0},{2,3},{3,2},{4,5},{5,4},{6,7},{7,6},{8,9},{9,8},{10,11... | collective-permute-start | bytes 5428232 | tf_op jit(solution)/shard_map/ppermute | solution.py:296
  503.3 79.4 %collective-permute-start.18 = (bf16[768,768]{1,0:T(8,128)(2,1)}, bf16[768,768]{1,0:T(8,128)(2,1)}, u32[]{:S(2)}, u32[]{:S(2)}) collective-permute-start(bf16[768,768]{1,0:T(8,128)(2,1)} %convolution_convert_fusion.9), channel_id=1, source_target_pairs={{0,2},{2,0},{4,6},{6,4},{8,10},{10,8},{12,14},{14,12},{16,18},{18,... | collective-permute-start | bytes 3538952 | tf_op jit(solution)/shard_map/ppermute | solution.py:333
  513.4 69.3 %collective-permute-start.19 = (bf16[768,768]{1,0:T(8,128)(2,1)}, bf16[768,768]{1,0:T(8,128)(2,1)}, u32[]{:S(2)}, u32[]{:S(2)}) collective-permute-start(bf16[768,768]{1,0:T(8,128)(2,1)} %convolution_convert_fusion.8), channel_id=1, source_target_pairs={{0,2},{2,0},{4,6},{6,4},{8,10},{10,8},{12,14},{14,12},{16,18},{18,... | collective-permute-start | bytes 3538952 | tf_op jit(solution)/shard_map/ppermute | solution.py:333
  514.0 260.9 %reduce-scatter.9.cloned.1.call-start = ((), (), s32[]{:S(2)}) async-start(), calls=%async_computation.13 | async-start | bytes 2949120 | tf_op jit(solution)/shard_map/reduce_scatter | solution.py:366
  549.0 47.1 %collective-permute-start.20 = (bf16[768,768]{1,0:T(8,128)(2,1)}, bf16[768,768]{1,0:T(8,128)(2,1)}, u32[]{:S(2)}, u32[]{:S(2)}) collective-permute-start(bf16[768,768]{1,0:T(8,128)(2,1)} %fusion.139), channel_id=1, source_target_pairs={{0,2},{2,0},{4,6},{6,4},{8,10},{10,8},{12,14},{14,12},{16,18},{18,... | collective-permute-start | bytes 3538952 | tf_op jit(solution)/shard_map/ppermute | solution.py:333
  550.5 46.1 %collective-permute-start.21 = (bf16[768,768]{1,0:T(8,128)(2,1)}, bf16[768,768]{1,0:T(8,128)(2,1)}, u32[]{:S(2)}, u32[]{:S(2)}) collective-permute-start(bf16[768,768]{1,0:T(8,128)(2,1)} %convolution_convert_fusion.7), channel_id=1, source_target_pairs={{0,2},{2,0},{4,6},{6,4},{8,10},{10,8},{12,14},{14,12},{16,18},{18,... | collective-permute-start | bytes 3538952 | tf_op jit(solution)/shard_map/ppermute | solution.py:333
  557.7 48.1 %collective-permute-start.17 = (bf16[1178,256]{1,0:T(8,128)(2,1)}, bf16[1178,256]{1,0:T(8,128)(2,1)}, u32[]{:S(2)}, u32[]{:S(2)}) collective-permute-start(bf16[1178,256]{1,0:T(8,128)(2,1)} %pad_maximum_fusion.30), channel_id=1, source_target_pairs={{0,1},{1,0},{2,3},{3,2},{4,5},{5,4},{6,7},{7,6},{8,9},{9,8},{10,11... | collective-permute-start | bytes 1809416 | tf_op jit(solution)/shard_map/ppermute | solution.py:296
  582.7 56.2 %collective-permute-start.22 = (bf16[1178,768]{1,0:T(8,128)(2,1)S(1)}, bf16[1178,768]{1,0:T(8,128)(2,1)}, u32[]{:S(2)}, u32[]{:S(2)}) collective-permute-start(bf16[1178,768]{1,0:T(8,128)(2,1)S(1)} %copy-done.65), channel_id=1, source_target_pairs={{0,1},{1,0},{2,3},{3,2},{4,5},{5,4},{6,7},{7,6},{8,9},{9,8},{10,11... | collective-permute-start | bytes 5428232 | tf_op jit(solution)/shard_map/ppermute | solution.py:296
  585.8 57.5 %collective-permute-start.26 = (bf16[768,768]{1,0:T(8,128)(2,1)}, bf16[768,768]{1,0:T(8,128)(2,1)}, u32[]{:S(2)}, u32[]{:S(2)}) collective-permute-start(bf16[768,768]{1,0:T(8,128)(2,1)} %convolution_convert_fusion.6), channel_id=1, source_target_pairs={{0,2},{2,0},{4,6},{6,4},{8,10},{10,8},{12,14},{14,12},{16,18},{18,... | collective-permute-start | bytes 3538952 | tf_op jit(solution)/shard_map/ppermute | solution.py:333
  596.1 48.6 %collective-permute-start.25 = (bf16[768,768]{1,0:T(8,128)(2,1)}, bf16[768,768]{1,0:T(8,128)(2,1)}, u32[]{:S(2)}, u32[]{:S(2)}) collective-permute-start(bf16[768,768]{1,0:T(8,128)(2,1)} %fusion.142), channel_id=1, source_target_pairs={{0,2},{2,0},{4,6},{6,4},{8,10},{10,8},{12,14},{14,12},{16,18},{18,... | collective-permute-start | bytes 3538952 | tf_op jit(solution)/shard_map/ppermute | solution.py:333
  600.2 87.5 %collective-permute-start.24 = (bf16[4,96,3072]{2,1,0:T(8,128)(2,1)S(1)}, bf16[4,96,3072]{2,1,0:T(8,128)(2,1)S(1)}, u32[]{:S(2)}, u32[]{:S(2)}) collective-permute-start(bf16[4,96,3072]{2,1,0:T(8,128)(2,1)S(1)} %pad_maximum_fusion.4), channel_id=1, source_target_pairs={{0,4},{2,6},{4,0},{6,2},{8,12},{10,14},{12,8},{14,10},{16,20},{18,... | collective-permute-start | bytes 7077896 | tf_op jit(solution)/shard_map/ppermute | solution.py:343
  642.5 41.5 %collective-permute-start.23 = (bf16[1178,768]{1,0:T(8,128)(2,1)S(1)}, bf16[1178,768]{1,0:T(8,128)(2,1)}, u32[]{:S(2)}, u32[]{:S(2)}) collective-permute-start(bf16[1178,768]{1,0:T(8,128)(2,1)S(1)} %pad_maximum_fusion.12), channel_id=1, source_target_pairs={{0,1},{1,0},{2,3},{3,2},{4,5},{5,4},{6,7},{7,6},{8,9},{9,8},{10,11... | collective-permute-start | bytes 5428232 | tf_op jit(solution)/shard_map/ppermute | solution.py:296
  647.7 86.9 %collective-permute-start.27 = (bf16[4,96,1536]{2,1,0:T(8,128)(2,1)}, bf16[4,96,1536]{2,1,0:T(8,128)(2,1)}, u32[]{:S(2)}, u32[]{:S(2)}) collective-permute-start(bf16[4,96,1536]{2,1,0:T(8,128)(2,1)} %pad_maximum_fusion.23), channel_id=1, source_target_pairs={{0,4},{2,6},{4,0},{6,2},{8,12},{10,14},{12,8},{14,10},{16,20},{18,... | collective-permute-start | bytes 3538952 | tf_op jit(solution)/shard_map/ppermute | solution.py:343
  679.0 63.0 %collective-permute-start.30 = (bf16[4,96,1536]{2,1,0:T(8,128)(2,1)}, bf16[4,96,1536]{2,1,0:T(8,128)(2,1)}, u32[]{:S(2)}, u32[]{:S(2)}) collective-permute-start(bf16[4,96,1536]{2,1,0:T(8,128)(2,1)} %pad_maximum_fusion.24), channel_id=1, source_target_pairs={{0,4},{2,6},{4,0},{6,2},{8,12},{10,14},{12,8},{14,10},{16,20},{18,... | collective-permute-start | bytes 3538952 | tf_op jit(solution)/shard_map/ppermute | solution.py:343
  690.1 135.6 %reduce-scatter.11.cloned.1.call-start = ((), (), s32[]{:S(2)}) async-start(), calls=%async_computation.14 | async-start | bytes 2949120 | tf_op jit(solution)/shard_map/reduce_scatter | solution.py:366
  702.2 45.9 %collective-permute-start.32 = (f32[384,1536]{1,0:T(8,128)}, f32[384,1536]{1,0:T(8,128)}, u32[]{:S(2)}, u32[]{:S(2)}) collective-permute-start(f32[384,1536]{1,0:T(8,128)} %convert_element_type.605), channel_id=1, source_target_pairs={{1,2},{2,1},{5,6},{6,5},{9,10},{10,9},{13,14},{14,13},{17,18},{18,... | collective-permute-start | bytes 7077896 | tf_op jit(solution)/shard_map/ppermute | solution.py:501
  (177 other events, 3137.3 us)
Sparse Core Ops, SparseCore 0:
  10.8 111.3 all-gather.3
  123.8 101.2 all-gather.5
  226.7 98.9 all-gather.7
  361.3 164.1 reduce-scatter.4
  529.0 193.8 reduce-scatter.6
  725.6 49.1 reduce-scatter.8
  777.1 48.4 reduce-scatter.10
